TPU v7x, 32 devices: a whole 2x2x4 slice. The times are simulated.
32 devices in a mesh: grp: 4 (over y, x), loc: 8 (over z, core).
Axes of the slice: x: 2, y: 2, z: 4, core: 2. Of those that a mesh axis runs over, the one named last changes fastest.
Arguments:
- hidden_in: bfloat16 [8, 4, 6, 3584], P('loc', 'grp'), may hold values from -6 to 6
- expert_ids: int32 [8, 4, 6, 8], P('loc', 'grp'), may hold values from 0 to 15, all different within a row; in each aligned block of 24 rows (0 to 23, 24 to 47, ..., all dimensions but the last counted through in order) at most 24 rows name the same one
- combine: bfloat16 [8, 4, 6, 8], P('loc', 'grp'), may hold values from 0.099609375 to 1
- w_gate: bfloat16 [32, 3584, 128], P(('grp', 'loc')), may hold values from -0.09375 to 0.09375
- w_up: bfloat16 [32, 3584, 128], P(('grp', 'loc')), may hold values from -0.09375 to 0.09375
- w_down: bfloat16 [32, 128, 3584], P(('grp', 'loc')), may hold values from -0.375 to 0.375
Outputs:
- layer_out: bfloat16 [8, 4, 6, 3584], P('loc', 'grp')
Inputs may be any that keep to these rules, and one draw needn't show every extreme that they name: `expert_ids`: each token names 8 different experts. Among the 24 tokens of one index of loc, no expert is named more than 24 times, and in every draw some expert is named exactly 24 times there.
All inputs are finite; a program needn't handle non-finite values.
Results may differ from a plain program's by a relative error of at most 0.0066.
Values may be sent and summed in bfloat16 or wider, within the bound.
No kernel may reach another device: no remote copies, remote signals or barrier semaphores. Data moves between devices by JAX's collectives and lax.ppermute only.
A program may use at most 64 MiB of HBM per device.

v0:
```python
import jax
import jax.numpy as jnp
from jax import lax
from jax.sharding import PartitionSpec as P

EXP_GRP = 4
CAP = 24


def body(hidden_in, expert_ids, combine, w_gate, w_up, w_down):
    group_count = lax.axis_size("grp")
    loc_count = lax.axis_size("loc")
    slices = loc_count // EXP_GRP
    tok_count = hidden_in.shape[2]
    feature = hidden_in.shape[3]
    top_count = expert_ids.shape[3]
    token_rows = hidden_in.reshape(tok_count, feature)
    chosen = expert_ids.reshape(tok_count, top_count)
    weights = combine.reshape(tok_count, top_count).astype(jnp.float32)
    catalog = jnp.arange(group_count * EXP_GRP, dtype=jnp.int32)
    matches = (chosen[:, :, None] == catalog[None, None, :]).astype(jnp.float32)
    hit_table = jnp.sum(matches, axis=1)
    pick_table = jnp.einsum("tk,tke->te", weights, matches)
    hit_table = (
        hit_table.reshape(tok_count, group_count, EXP_GRP).transpose(1, 0, 2).astype(jnp.bfloat16)
    )
    pick_table = (
        pick_table.reshape(tok_count, group_count, EXP_GRP).transpose(1, 0, 2).astype(jnp.bfloat16)
    )
    arrivals_count = group_count * tok_count
    outgoing = token_rows[None, :, None, :] * hit_table[:, :, :, None]
    arrived, arr_hits, arr_picks = (
        lax.all_to_all(outgoing, "grp", split_axis=0, concat_axis=0, tiled=True),
        lax.all_to_all(hit_table, "grp", split_axis=0, concat_axis=0, tiled=True),
        lax.all_to_all(pick_table, "grp", split_axis=0, concat_axis=0, tiled=True),
    )
    arrived = arrived.reshape(arrivals_count, EXP_GRP, feature)
    flat_hits = arr_hits.reshape(arrivals_count, EXP_GRP).astype(jnp.float32)
    flat_picks = arr_picks.reshape(arrivals_count, EXP_GRP).astype(jnp.float32)
    slot_rank = jnp.cumsum(flat_hits, axis=0) - 1.0
    cell_index = jnp.arange(CAP, dtype=jnp.float32)
    selector = flat_hits.T[:, None, :] * (
        slot_rank.T[:, None, :] == cell_index[None, :, None]
    ).astype(jnp.float32)
    weighted = selector * flat_picks.T[:, None, :]
    compact_selector = selector.astype(jnp.bfloat16)
    packed = jnp.einsum(
        "jcm,mjd->jcd", compact_selector, arrived, preferred_element_type=jnp.float32
    ).astype(jnp.bfloat16)
    outbound = jnp.broadcast_to(packed[:, None, :, :], (EXP_GRP, slices, CAP, feature)).reshape(
        loc_count, CAP, feature
    )
    arrivals = lax.all_to_all(outbound, "loc", split_axis=0, concat_axis=0, tiled=True)
    item_count = arrivals.shape[1]
    flat_rows = arrivals.reshape(-1, feature)
    gate_out = jnp.dot(flat_rows, w_gate[0], preferred_element_type=jnp.float32)
    up_out = jnp.dot(flat_rows, w_up[0], preferred_element_type=jnp.float32)
    hidden_units = (jax.nn.silu(gate_out) * up_out).astype(jnp.bfloat16)
    result = jnp.dot(hidden_units, w_down[0], preferred_element_type=jnp.float32).astype(
        jnp.bfloat16
    )
    result = result.reshape(loc_count, item_count, feature)
    returned = lax.all_to_all(result, "loc", split_axis=0, concat_axis=0, tiled=True)
    slice_sum = jnp.sum(returned.reshape(EXP_GRP, slices, CAP, feature).astype(jnp.float32), axis=1)
    group_part = jnp.einsum(
        "jcm,jcd->md", weighted, slice_sum, precision=lax.Precision.HIGHEST
    ).astype(jnp.bfloat16)
    homeward = lax.all_to_all(
        group_part.reshape(group_count, tok_count, feature),
        "grp",
        split_axis=0,
        concat_axis=0,
        tiled=True,
    )
    summed = jnp.sum(homeward.astype(jnp.float32), axis=0)
    return summed.astype(jnp.bfloat16).reshape(1, 1, tok_count, feature)


def solution(mesh):
    placed = (
        P("loc", "grp", None, None),
        P("loc", "grp", None, None),
        P("loc", "grp", None, None),
        P(("grp", "loc"), None, None),
        P(("grp", "loc"), None, None),
        P(("grp", "loc"), None, None),
    )
    return jax.shard_map(
        body, mesh=mesh, in_specs=placed, out_specs=P("loc", "grp", None, None), check_vma=False
    )
```

profile of v0, /device:TPU:0, one launch (start us, length us, event | category | flops | bytes accessed | tf_op | source)
XLA Modules:
  0.0 119.8 jit_solution(14400342839570515931)
XLA Ops:
  0.0 0.0 copy-start
  0.0 0.8 copy.37
  0.8 0.1 convert_reduce_fusion.1
  0.9 0.7 copy.20
  1.6 5.2 %all-to-all-start = ((bf16[4,6,4]{1,2,0:T(4,128)(2,1)}), bf16[4,6,4]{1,2,0:T(4,128)(2,1)S(1)}, u32[]{:S(2)}, u32[]{:S(2)}) async-start(bf16[4,6,4]{1,2,0:T(4,128)(2,1)} %bitcast.1), calls=%async_computation | async-start | bytes 8192 | tf_op jit(solution)/shard_map/all_to_all | solution.py:34
  6.7 0.8 copy.25
  7.6 2.0 %broadcast_multiply_fusion = bf16[4,6,4,3584]{3,2,1,0:T(4,128)(2,1)} fusion(bf16[4,6,4]{2,1,0:T(8,128)(2,1)S(1)} %copy.25, bf16[6,3584]{1,0:T(8,128)(2,1)} %bitcast.54), kind=kLoop, calls=%fused_computation.12 | loop fusion | flops 344064 | bytes 731328 | tf_op jit(solution)/shard_map/mul | solution.py:31
  9.5 1.9 %all-to-all-done = bf16[4,6,4]{1,2,0:T(4,128)(2,1)S(1)} async-done(((bf16[4,6,4]{1,2,0:T(4,128)(2,1)}), bf16[4,6,4]{1,2,0:T(4,128)(2,1)S(1)}, u32[]{:S(2)}, u32[]{:S(2)}) %all-to-all-start) | async-done | bytes 224 | tf_op jit(solution)/shard_map/all_to_all | solution.py:34
  11.4 3.5 %all-to-all-start.2 = ((bf16[4,6,4,3584]{3,2,1,0:T(4,128)(2,1)}), bf16[4,6,4,3584]{3,2,1,0:T(4,128)(2,1)S(1)}, u32[]{:S(2)}, u32[]{:S(2)}) async-start(bf16[4,6,4,3584]{3,2,1,0:T(4,128)(2,1)} %broadcast_multiply_fusion), calls=%async_computation.2 | async-start | bytes 1376256 | tf_op jit(solution)/shard_map/all_to_all | solution.py:33
  14.9 0.1 reshape.48
  15.0 0.1 copy.22
  15.1 0.1 copy.23
  15.2 8.3 %all-to-all-done.2 = bf16[4,6,4,3584]{3,2,1,0:T(4,128)(2,1)S(1)} async-done(((bf16[4,6,4,3584]{3,2,1,0:T(4,128)(2,1)}), bf16[4,6,4,3584]{3,2,1,0:T(4,128)(2,1)S(1)}, u32[]{:S(2)}, u32[]{:S(2)}) %all-to-all-start.2) | async-done | bytes 688160 | tf_op jit(solution)/shard_map/all_to_all | solution.py:33
  23.5 0.5 convolution_convert_fusion.1
  24.0 1.2 broadcast_in_dim.2
  25.2 0.0 copy-start.2
  25.2 0.0 copy-start.1
  25.2 5.0 %all-to-all-start.3 = ((bf16[8,24,3584]{2,1,0:T(8,128)(2,1)}), bf16[8,24,3584]{2,1,0:T(8,128)(2,1)S(1)}, u32[]{:S(2)}, u32[]{:S(2)}) async-start(bf16[8,24,3584]{2,1,0:T(8,128)(2,1)} %bitcast.52), calls=%async_computation.3 | async-start | bytes 2752512 | tf_op jit(solution)/shard_map/all_to_all | solution.py:53
  30.2 0.0 copy-done.2
  30.2 0.2 fusion.21
  30.4 0.7 copy.29
  31.1 32.7 %all-to-all-done.3 = bf16[8,24,3584]{2,1,0:T(8,128)(2,1)S(1)} async-done(((bf16[8,24,3584]{2,1,0:T(8,128)(2,1)}), bf16[8,24,3584]{2,1,0:T(8,128)(2,1)S(1)}, u32[]{:S(2)}, u32[]{:S(2)}) %all-to-all-start.3) | async-done | bytes 1376288 | tf_op jit(solution)/shard_map/all_to_all | solution.py:53
  63.8 3.2 %all-to-all-start.1 = ((bf16[4,6,4]{1,2,0:T(4,128)(2,1)}), bf16[4,6,4]{1,2,0:T(4,128)(2,1)S(1)}, u32[]{:S(2)}, u32[]{:S(2)}) async-start(bf16[4,6,4]{1,2,0:T(4,128)(2,1)} %bitcast.8), calls=%async_computation.1 | async-start | bytes 8192 | tf_op jit(solution)/shard_map/all_to_all | solution.py:35
  67.0 0.0 copy-done.1
  67.1 0.5 fusion.5
  67.6 0.0 copy-done
  67.6 3.2 %convolution_convert_fusion = bf16[192,3584]{1,0:T(8,128)(2,1)} fusion(bf16[192,3584]{1,0:T(8,128)(2,1)S(1)} %bitcast.50, bf16[1,128,3584]{2,1,0:T(8,128)(2,1)S(1)} %copy-done, bf16[1,3584,128]{2,1,0:T(8,128)(2,1)} %param.10, f32[192,128]{1,0:T(8,128)S(1)} %fusion.5), kind=kOutput, calls=%fused_computation | convolution fusion | flops 353157120 | bytes 4685824 | tf_op jit(solution)/shard_map/dot_general | solution.py:59
  70.8 0.9 all-to-all-done.1
  71.7 3.6 %all-to-all-start.4 = ((bf16[8,24,3584]{2,1,0:T(8,128)(2,1)}), bf16[8,24,3584]{2,1,0:T(8,128)(2,1)S(1)}, u32[]{:S(2)}, u32[]{:S(2)}) async-start(bf16[8,24,3584]{2,1,0:T(8,128)(2,1)} %bitcast.51), calls=%async_computation.4 | async-start | bytes 2752512 | tf_op jit(solution)/shard_map/all_to_all | solution.py:63
  75.3 0.1 reshape.50
  75.4 33.4 %all-to-all-done.4 = bf16[8,24,3584]{2,1,0:T(8,128)(2,1)S(1)} async-done(((bf16[8,24,3584]{2,1,0:T(8,128)(2,1)}), bf16[8,24,3584]{2,1,0:T(8,128)(2,1)S(1)}, u32[]{:S(2)}, u32[]{:S(2)}) %all-to-all-start.4) | async-done | bytes 1376288 | tf_op jit(solution)/shard_map/all_to_all | solution.py:63
  108.8 0.2 convert_reduce_fusion
  109.0 1.3 %fusion = bf16[24,3584]{1,0:T(8,128)(2,1)S(1)} fusion(f32[4,24,3584]{2,1,0:T(8,128)S(1)} %convert_reduce_fusion, f32[4,24]{1,0:T(4,128)S(1)} %bitcast.59, f32[4,24]{1,0:T(4,128)S(1)} %bitcast.56, f32[4,24]{1,0:T(4,128)S(1)} %copy.23), kind=kOutput, calls=%fused_computation.3 | convolution fusion | flops 99183360 | bytes 1549440 | tf_op jit(solution)/shard_map/jcm,jcd->md/dot_general | solution.py:65
  110.3 0.1 reshape.46
  110.4 8.7 %all_to_all.30 = bf16[4,6,3584]{2,1,0:T(8,128)(2,1)S(1)} all-to-all(bf16[4,6,3584]{2,1,0:T(8,128)(2,1)S(1)} %reshape.46), channel_id=1, replica_groups=mesh['grp'=4,'loc'=8] {'grp'}, dimensions={0} | all-to-all | bytes 344064 | tf_op jit(solution)/shard_map/all_to_all | solution.py:68
  119.1 0.7 reduce_sum.32
  (4 shorter events, 0.1 us)
Async XLA Ops:
  0.0 67.6 %copy-start = (bf16[1,128,3584]{2,1,0:T(8,128)(2,1)S(1)}, bf16[1,128,3584]{2,1,0:T(8,128)(2,1)}, u32[]{:S(2)}) copy-start(bf16[1,128,3584]{2,1,0:T(8,128)(2,1)} %param.11) | copy-start | bytes 2752516
  1.6 9.8 %all-to-all-start = ((bf16[4,6,4]{1,2,0:T(4,128)(2,1)}), bf16[4,6,4]{1,2,0:T(4,128)(2,1)S(1)}, u32[]{:S(2)}, u32[]{:S(2)}) async-start(bf16[4,6,4]{1,2,0:T(4,128)(2,1)} %bitcast.1), calls=%async_computation | async-start | bytes 8192 | tf_op jit(solution)/shard_map/all_to_all | solution.py:34
  11.4 12.1 %all-to-all-start.2 = ((bf16[4,6,4,3584]{3,2,1,0:T(4,128)(2,1)}), bf16[4,6,4,3584]{3,2,1,0:T(4,128)(2,1)S(1)}, u32[]{:S(2)}, u32[]{:S(2)}) async-start(bf16[4,6,4,3584]{3,2,1,0:T(4,128)(2,1)} %broadcast_multiply_fusion), calls=%async_computation.2 | async-start | bytes 1376256 | tf_op jit(solution)/shard_map/all_to_all | solution.py:33
  25.2 5.0 %copy-start.2 = (bf16[1,1,6,8]{3,2,1,0:T(8,128)(2,1)S(1)}, bf16[1,1,6,8]{3,2,1,0:T(8,128)(2,1)}, u32[]{:S(2)}) copy-start(bf16[1,1,6,8]{3,2,1,0:T(8,128)(2,1)} %param.8) | copy-start | bytes 292
  25.2 41.9 %copy-start.1 = (bf16[1,3584,128]{2,1,0:T(8,128)(2,1)S(1)}, bf16[1,3584,128]{2,1,0:T(8,128)(2,1)}, u32[]{:S(2)}) copy-start(bf16[1,3584,128]{2,1,0:T(8,128)(2,1)} %param.9) | copy-start | bytes 2752516
  25.2 38.6 %all-to-all-start.3 = ((bf16[8,24,3584]{2,1,0:T(8,128)(2,1)}), bf16[8,24,3584]{2,1,0:T(8,128)(2,1)S(1)}, u32[]{:S(2)}, u32[]{:S(2)}) async-start(bf16[8,24,3584]{2,1,0:T(8,128)(2,1)} %bitcast.52), calls=%async_computation.3 | async-start | bytes 2752512 | tf_op jit(solution)/shard_map/all_to_all | solution.py:53
  63.8 7.9 %all-to-all-start.1 = ((bf16[4,6,4]{1,2,0:T(4,128)(2,1)}), bf16[4,6,4]{1,2,0:T(4,128)(2,1)S(1)}, u32[]{:S(2)}, u32[]{:S(2)}) async-start(bf16[4,6,4]{1,2,0:T(4,128)(2,1)} %bitcast.8), calls=%async_computation.1 | async-start | bytes 8192 | tf_op jit(solution)/shard_map/all_to_all | solution.py:35
  71.7 37.1 %all-to-all-start.4 = ((bf16[8,24,3584]{2,1,0:T(8,128)(2,1)}), bf16[8,24,3584]{2,1,0:T(8,128)(2,1)S(1)}, u32[]{:S(2)}, u32[]{:S(2)}) async-start(bf16[8,24,3584]{2,1,0:T(8,128)(2,1)} %bitcast.51), calls=%async_computation.4 | async-start | bytes 2752512 | tf_op jit(solution)/shard_map/all_to_all | solution.py:63
where the time goes:
time: 120 us
  waiting for transfers between devices  77.2 us (64%)
  starting transfers between devices  20.5 us (17%)
  blocking collectives  8.71 us (7%)
  matrix products  5.7 us (5%)
  local copies, waits for them, and re-layouts  4.59 us (4%)
  other arithmetic  3.02 us (3%)
    all_to_all x1, waiting for transfers between devices, body(): lax.all_to_all(result, 'loc', split_axis=0, concat_axis=0, tiled=True)  33.4 us
    all_to_all x1, waiting for transfers between devices, body(): lax.all_to_all(outbound, 'loc', split_axis=0, concat_axis=0, tiled=True)  32.7 us
    all_to_all x1, blocking collectives, body(): lax.all_to_all(group_part.reshape(group_count, tok_count, feature), 'grp'...  8.71 us
    all_to_all x1, waiting for transfers between devices, body(): lax.all_to_all(outgoing, 'grp', split_axis=0, concat_axis=0, tiled=True)  8.27 us
    all_to_all x1, starting transfers between devices, body(): lax.all_to_all(hit_table, 'grp', split_axis=0, concat_axis=0, tiled=True)  5.16 us
    all_to_all x1, starting transfers between devices, body(): lax.all_to_all(outbound, 'loc', split_axis=0, concat_axis=0, tiled=True)  5.01 us
    all_to_all x1, starting transfers between devices, body(): lax.all_to_all(result, 'loc', split_axis=0, concat_axis=0, tiled=True)  3.57 us
    all_to_all x1, starting transfers between devices, body(): lax.all_to_all(outgoing, 'grp', split_axis=0, concat_axis=0, tiled=True)  3.48 us
  transfers between devices with their start and end apart: 5, of which 5 were waited for; matrix products, arithmetic and copies ran while one was open for 7% of the time, Pallas kernels for 0%

commit v1 on v0

--- a/solution.py
+++ b/solution.py
@@ -5,9 +5,10 @@
 
 EXP_GRP = 4
 CAP = 24
+LANES = 128
 
 
-def body(hidden_in, expert_ids, combine, w_gate, w_up, w_down):
+def packed_body(hidden_in, expert_ids, combine, w_gate, w_up, w_down):
     group_count = lax.axis_size("grp")
     loc_count = lax.axis_size("loc")
     slices = loc_count // EXP_GRP
@@ -76,7 +77,69 @@
     return summed.astype(jnp.bfloat16).reshape(1, 1, tok_count, feature)
 
 
+def pairs(size, distance):
+    return [(i, i ^ distance) for i in range(size)]
+
+
+def spread(rows, axis, size, distances):
+    return [rows] + [lax.ppermute(rows, axis, pairs(size, d)) for d in distances]
+
+
+def fold(chunks, axis, size, distances):
+    arrived = [lax.ppermute(c, axis, pairs(size, d)) for c, d in zip(chunks[1:], distances)]
+    total = chunks[0].astype(jnp.float32)
+    for part in arrived:
+        total = total + part.astype(jnp.float32)
+    return total
+
+
+def dense_body(hidden_in, expert_ids, combine, w_gate, w_up, w_down):
+    group_count = lax.axis_size("grp")
+    loc_count = lax.axis_size("loc")
+    slices = loc_count // EXP_GRP
+    tok_count = hidden_in.shape[2]
+    feature = hidden_in.shape[3]
+    top_count = expert_ids.shape[3]
+    token_rows = hidden_in.reshape(tok_count, feature)
+    chosen = expert_ids.reshape(tok_count, top_count)
+    weights = combine.reshape(tok_count, top_count).astype(jnp.float32)
+    lanes = jnp.arange(LANES, dtype=jnp.int32)
+    table = jnp.sum(
+        jnp.where(chosen[:, :, None] == lanes[None, None, :], weights[:, :, None], 0.0), axis=1
+    ).astype(jnp.bfloat16)
+    rows = jnp.concatenate([token_rows, table], axis=1)
+
+    member_steps = [slices * k for k in range(1, EXP_GRP)]
+    group_steps = list(range(1, group_count))
+    slice_steps = list(range(1, slices))
+    rows = jnp.concatenate(spread(rows, "loc", loc_count, member_steps), axis=0)
+    rows = jnp.concatenate(spread(rows, "grp", group_count, group_steps), axis=0)
+    own_expert = lax.axis_index("grp") * EXP_GRP + lax.axis_index("loc") // slices
+    pick = (lanes == own_expert).astype(jnp.float32)
+    partials = []
+    for block in spread(rows, "loc", loc_count, slice_steps):
+        features = block[:, :feature]
+        weight = jnp.sum(block[:, feature:].astype(jnp.float32) * pick[None, :], axis=1)
+        gate_out = jnp.dot(features, w_gate[0], preferred_element_type=jnp.float32)
+        up_out = jnp.dot(features, w_up[0], preferred_element_type=jnp.float32)
+        hidden_units = (jax.nn.silu(gate_out) * up_out).astype(jnp.bfloat16)
+        part = jnp.dot(hidden_units, w_down[0], preferred_element_type=jnp.float32)
+        partials.append(part * weight[:, None])
+    partials = partials[:1] + [p.astype(jnp.bfloat16) for p in partials[1:]]
+    total = fold(partials, "loc", loc_count, slice_steps).astype(jnp.bfloat16)
+    chunks = list(total.reshape(group_count, EXP_GRP * tok_count, feature))
+    total = fold(chunks, "grp", group_count, group_steps).astype(jnp.bfloat16)
+    chunks = list(total.reshape(EXP_GRP, tok_count, feature))
+    total = fold(chunks, "loc", loc_count, member_steps).astype(jnp.bfloat16)
+    return total.reshape(1, 1, tok_count, feature)
+
+
+def power_of_two(count):
+    return count & (count - 1) == 0
+
+
 def solution(mesh):
+    group_count, loc_count = mesh.shape["grp"], mesh.shape["loc"]
     placed = (
         P("loc", "grp", None, None),
         P("loc", "grp", None, None),
@@ -85,6 +148,17 @@
         P(("grp", "loc"), None, None),
         P(("grp", "loc"), None, None),
     )
-    return jax.shard_map(
-        body, mesh=mesh, in_specs=placed, out_specs=P("loc", "grp", None, None), check_vma=False
+    dense_fits = (
+        power_of_two(group_count)
+        and power_of_two(loc_count)
+        and group_count * EXP_GRP <= LANES
     )
+
+    def layer(hidden_in, *others):
+        small = hidden_in.shape[1] * hidden_in.shape[2] <= CAP
+        body = dense_body if dense_fits and small else packed_body
+        return jax.shard_map(
+            body, mesh=mesh, in_specs=placed, out_specs=P("loc", "grp", None, None), check_vma=False
+        )(hidden_in, *others)
+
+    return layer

time: 120 us -> 58.7 us (0.49)
  waiting for transfers between devices: 77.2 us -> 27.8 us
  blocking collectives: 8.71 us -> 0 us
  starting transfers between devices: 20.5 us -> 17.4 us
  local copies, waits for them, and re-layouts: 4.59 us -> 2.5 us
    all_to_all x5 -> x0, waiting for transfers between devices: 77.2 us -> none  [the longest x1 33.4 us: body(): lax.all_to_all(result, 'loc', split_axis=0, concat_axis=0, tiled=True)]
    ppermute x0 -> x14, waiting for transfers between devices: none -> 27.8 us  [the longest x7 14.9 us: spread(): lax.ppermute(rows, axis, pairs(size, d))]
    all_to_all x5 -> x0, starting transfers between devices: 20.5 us -> none  [the longest x1 5.16 us: body(): lax.all_to_all(hit_table, 'grp', split_axis=0, concat_axis=0, tiled=True)]
    ppermute x0 -> x14, starting transfers between devices: none -> 17.4 us  [the longest x7 9.31 us: spread(): lax.ppermute(rows, axis, pairs(size, d))]
    all_to_all x1 -> x0, blocking collectives: 8.71 us -> none  [body(): lax.all_to_all(group_part.reshape(group_count, tok_count, feature), 'grp'...]
    mul x1 -> x0, other arithmetic: 1.98 us -> none  [body(): outgoing = token_rows[None, :, None, :] * hit_table[:, :, :, None]]
    concatenate x0 -> x2, other arithmetic: none -> 1.75 us  [the longest x1 0.91 us: dense_body(): rows = jnp.concatenate(spread(rows, 'loc', loc_count, member_steps), axis=0)]
    convert_element_type x5 -> x0, local copies, waits for them, and re-layouts: 1.7 us -> none  [the longest x2 1.52 us: body(): hit_table.reshape(tok_count, group_count, EXP_GRP).transpose(1, 0, 2)]
  transfers between devices with their start and end apart: 5 -> 14, of which waited for: 5 -> 11; matrix products, arithmetic and copies ran while one was open for 7% -> 1% of each run, Pallas kernels for 0% -> 0%
where the time goes in v1:
time: 58.7 us; the launch traced here: 58.3 us
  waiting for transfers between devices  27.8 us (47%)
  starting transfers between devices  17.4 us (30%)
  matrix products  6.21 us (11%)
  other arithmetic  4.13 us (7%)
  local copies, waits for them, and re-layouts  2.5 us (4%)
    ppermute x7, waiting for transfers between devices, spread(): lax.ppermute(rows, axis, pairs(size, d))  14.9 us
    ppermute x7, waiting for transfers between devices, fold(): lax.ppermute(c, axis, pairs(size, d))  12.9 us
    ppermute x7, starting transfers between devices, spread(): lax.ppermute(rows, axis, pairs(size, d))  9.31 us
    ppermute x7, starting transfers between devices, fold(): lax.ppermute(c, axis, pairs(size, d))  8.13 us
    dot_general x2, matrix products, dense_body(): part = jnp.dot(hidden_units, w_down[0], preferred_element_type=jnp.float32)  4.42 us
    dot_general x2, matrix products, dense_body(): up_out = jnp.dot(features, w_up[0], preferred_element_type=jnp.float32)  1.79 us
    unnamed x9, local copies, waits for them, and re-layouts  1.64 us
  transfers between devices with their start and end apart: 14, of which 11 were waited for; matrix products, arithmetic and copies ran while one was open for 1% of the time, Pallas kernels for 0%

profile of v1, /device:TPU:0, one launch (start us, length us, event | category | flops | bytes accessed | tf_op | source)
XLA Modules:
  0.0 58.3 jit_solution(17564422363706074250)
XLA Ops:
  0.0 0.0 copy-start
  0.0 0.8 %copy.9 = s32[1,1,6,8]{3,2,1,0:T(8,128)S(1)} copy(s32[1,1,6,8]{3,1,2,0:T(1,128)} %param.7) | data formatting | bytes 384
  0.8 0.7 %bitcast_convert_fusion = f32[6,8]{1,0:T(8,128)S(1)} fusion(bf16[1,1,6,8]{3,2,1,0:T(8,128)(2,1)} %param.8), kind=kLoop, calls=%fused_computation.32 | loop fusion | flops 48 | bytes 288 | tf_op jit(solution)/shard_map/convert_element_type | solution.py:105
  1.5 0.1 select_reduce_fusion
  1.5 0.8 %pad_maximum_fusion.1 = bf16[6,3712]{1,0:T(8,128)(2,1)S(1)} fusion(bf16[6,128]{1,0:T(8,128)(2,1)S(1)} %select_reduce_fusion, bf16[6,3584]{1,0:T(8,128)(2,1)} %bitcast.36), kind=kLoop, calls=%fused_computation.21 | loop fusion | flops 89088 | bytes 89088 | tf_op jit(solution)/shard_map/concatenate | solution.py:110
  2.4 0.0 copy-start.1
  2.4 3.1 %collective-permute-start = (bf16[6,3712]{1,0:T(8,128)(2,1)S(1)}, bf16[6,3712]{1,0:T(8,128)(2,1)S(1)}, u32[]{:S(2)}, u32[]{:S(2)}) collective-permute-start(bf16[6,3712]{1,0:T(8,128)(2,1)S(1)} %pad_maximum_fusion.1), channel_id=1, source_target_pairs={{0,2},{1,3},{2,0},{3,1},{4,6},{5,7},{6,4},{7,5},{8,10},{9,11},{10,... | collective-permute-start | bytes 133640 | tf_op jit(solution)/shard_map/ppermute | solution.py:85
  5.5 2.6 %collective-permute-start.1 = (bf16[6,3712]{1,0:T(8,128)(2,1)S(1)}, bf16[6,3712]{1,0:T(8,128)(2,1)S(1)}, u32[]{:S(2)}, u32[]{:S(2)}) collective-permute-start(bf16[6,3712]{1,0:T(8,128)(2,1)S(1)} %pad_maximum_fusion.1), channel_id=1, source_target_pairs={{0,4},{1,5},{2,6},{3,7},{4,0},{5,1},{6,2},{7,3},{8,12},{9,13},{10,... | collective-permute-start | bytes 133640 | tf_op jit(solution)/shard_map/ppermute | solution.py:85
  8.1 0.0 collective-permute-start.2
  8.1 0.0 collective-permute-done
  8.1 3.7 %collective-permute-done.1 = bf16[6,3712]{1,0:T(8,128)(2,1)S(1)} collective-permute-done((bf16[6,3712]{1,0:T(8,128)(2,1)S(1)}, bf16[6,3712]{1,0:T(8,128)(2,1)S(1)}, u32[]{:S(2)}, u32[]{:S(2)}) %collective-permute-start.1) | collective-permute-done | bytes 44576 | tf_op jit(solution)/shard_map/ppermute | solution.py:85
  11.7 2.3 %collective-permute-done.2 = bf16[6,3712]{1,0:T(8,128)(2,1)S(1)} collective-permute-done((bf16[6,3712]{1,0:T(8,128)(2,1)S(1)}, bf16[6,3712]{1,0:T(8,128)(2,1)S(1)}, u32[]{:S(2)}, u32[]{:S(2)}) %collective-permute-start.2) | collective-permute-done | bytes 44576 | tf_op jit(solution)/shard_map/ppermute | solution.py:85
  14.1 0.9 %pad_maximum_fusion = bf16[24,3712]{1,0:T(8,128)(2,1)S(1)} fusion(bf16[6,3712]{1,0:T(8,128)(2,1)S(1)} %collective-permute-done.2, bf16[6,3712]{1,0:T(8,128)(2,1)S(1)} %collective-permute-done.1, bf16[6,3712]{1,0:T(8,128)(2,1)S(1)} %collective-permute-done, bf16[6,128]{1,0:T(8,128)(2,1)S(1)} %select_reduce_fusion, bf16[6,3584]{1,0:T(8,128)(2,1)} %bitcast.37), kind=kLoop, calls=%fused_computation.19 | loop fusion | flops 890880 | bytes 356352 | tf_op jit(solution)/shard_map/concatenate | solution.py:115
  15.0 1.6 %collective-permute-start.3 = (bf16[24,3712]{1,0:T(8,128)(2,1)S(1)}, bf16[24,3712]{1,0:T(8,128)(2,1)S(1)}, u32[]{:S(2)}, u32[]{:S(2)}) collective-permute-start(bf16[24,3712]{1,0:T(8,128)(2,1)S(1)} %pad_maximum_fusion), channel_id=1, source_target_pairs={{0,8},{8,0},{16,24},{24,16},{1,9},{9,1},{17,25},{25,17},{2,10},{10... | collective-permute-start | bytes 534536 | tf_op jit(solution)/shard_map/ppermute | solution.py:85
  16.5 1.5 %collective-permute-start.4 = (bf16[24,3712]{1,0:T(8,128)(2,1)S(1)}, bf16[24,3712]{1,0:T(8,128)(2,1)S(1)}, u32[]{:S(2)}, u32[]{:S(2)}) collective-permute-start(bf16[24,3712]{1,0:T(8,128)(2,1)S(1)} %pad_maximum_fusion), channel_id=1, source_target_pairs={{0,16},{8,24},{16,0},{24,8},{1,17},{9,25},{17,1},{25,9},{2,18},{10... | collective-permute-start | bytes 534536 | tf_op jit(solution)/shard_map/ppermute | solution.py:85
  18.1 0.5 collective-permute-start.5
  18.5 3.5 %collective-permute-done.3 = bf16[24,3712]{1,0:T(8,128)(2,1)S(1)} collective-permute-done((bf16[24,3712]{1,0:T(8,128)(2,1)S(1)}, bf16[24,3712]{1,0:T(8,128)(2,1)S(1)}, u32[]{:S(2)}, u32[]{:S(2)}) %collective-permute-start.3) | collective-permute-done | bytes 178208 | tf_op jit(solution)/shard_map/ppermute | solution.py:85
  22.1 3.1 %collective-permute-done.4 = bf16[24,3712]{1,0:T(8,128)(2,1)S(1)} collective-permute-done((bf16[24,3712]{1,0:T(8,128)(2,1)S(1)}, bf16[24,3712]{1,0:T(8,128)(2,1)S(1)}, u32[]{:S(2)}, u32[]{:S(2)}) %collective-permute-start.4) | collective-permute-done | bytes 178208 | tf_op jit(solution)/shard_map/ppermute | solution.py:85
  25.2 0.0 collective-permute-done.5
  25.2 0.8 %concatenate.12 = bf16[96,3712]{1,0:T(8,128)(2,1)S(1)} concatenate(bf16[6,3712]{1,0:T(8,128)(2,1)S(1)} %pad_maximum_fusion.1, bf16[6,3712]{1,0:T(8,128)(2,1)S(1)} %collective-permute-done, bf16[6,3712]{1,0:T(8,128)(2,1)S(1)} %collective-permute-done.1, bf16[6,3712]{1,0:T(8,128)(2,1)S(1)} %collective-permute-done.2, bf16[24,3712]{1,0:T(8,128)(2,1)S(1)} %collective-permute-done.3, ...), dimensions={0} | concatenate | bytes 1425408 | tf_op jit(solution)/shard_map/concatenate | solution.py:116
  26.0 0.0 copy-start.2
  26.0 0.1 collective-permute-start.6
  26.1 2.3 %collective-permute-done.6 = bf16[96,3712]{1,0:T(8,128)(2,1)} collective-permute-done((bf16[96,3712]{1,0:T(8,128)(2,1)S(1)}, bf16[96,3712]{1,0:T(8,128)(2,1)}, u32[]{:S(2)}, u32[]{:S(2)}) %collective-permute-start.6) | collective-permute-done | bytes 712736 | tf_op jit(solution)/shard_map/ppermute | solution.py:85
  28.4 0.0 copy-done.1
  28.4 1.4 %fusion.5 = f32[96,128]{1,0:T(8,128)S(1)} fusion(bf16[1,3584,128]{2,1,0:T(8,128)(2,1)S(1)} %copy-done.1, bf16[96,3712]{1,0:T(8,128)(2,1)} %collective-permute-done.6), kind=kOutput, calls=%fused_computation.6 | convolution fusion | flops 88080384 | bytes 1654784 | tf_op jit(solution)/shard_map/dot_general | solution.py:124
  29.9 0.8 %multiply_reduce_fusion.1 = (f32[96]{0:T(128)S(1)}, f32[96]{0:T(128)S(1)}) fusion(bf16[96,3712]{1,0:T(8,128)(2,1)S(1)} %concatenate.12, f32[128]{0:T(128)S(1)} %compare_convert_fusion, bf16[96,3712]{1,0:T(8,128)(2,1)} %collective-permute-done.6), kind=kLoop, calls=%fused_computation.25 | loop fusion | flops 73536 | bytes 50432 | tf_op jit(solution)/shard_map/reduce_sum | solution.py:122
  30.7 0.0 copy-done
  30.7 0.0 copy-done.2
  30.7 2.6 %multiply_convert_fusion = bf16[96,3584]{1,0:T(8,128)(2,1)} fusion(f32[96]{0:T(128)S(1)} %get-tuple-element.6, bf16[1,128,3584]{2,1,0:T(8,128)(2,1)S(1)} %copy-done, f32[96,128]{1,0:T(8,128)S(1)} %fusion.5, bf16[1,3584,128]{2,1,0:T(8,128)(2,1)S(1)} %copy-done.2, bf16[96,3712]{1,0:T(8,128)(2,1)} %collective-permute-done.6), kind=kOutput, calls=%fused_computation.2 | convolution fusion | flops 176922624 | bytes 3260800 | tf_op jit(solution)/shard_map/dot_general | solution.py:126
  33.4 0.1 collective-permute-start.7
  33.5 0.3 fusion.7
  33.8 1.9 %collective-permute-done.7 = bf16[96,3584]{1,0:T(8,128)(2,1)S(1)} collective-permute-done((bf16[96,3584]{1,0:T(8,128)(2,1)}, bf16[96,3584]{1,0:T(8,128)(2,1)S(1)}, u32[]{:S(2)}, u32[]{:S(2)}) %collective-permute-start.7) | collective-permute-done | bytes 688160 | tf_op jit(solution)/shard_map/ppermute | solution.py:89
  35.7 0.9 %copy-done.3 = bf16[96,3584]{1,0:T(8,128)(2,1)} copy-done((bf16[96,3584]{1,0:T(8,128)(2,1)}, bf16[96,3584]{1,0:T(8,128)(2,1)S(1)}, u32[]{:S(2)}) %copy-start.3) | copy-done | bytes 688152
  36.6 1.8 %add_convert_fusion = bf16[96,3584]{1,0:T(8,128)(2,1)S(1)} fusion(bf16[96,3584]{1,0:T(8,128)(2,1)} %copy-done.3, bf16[1,128,3584]{2,1,0:T(8,128)(2,1)S(1)} %copy-done, f32[96]{0:T(128)S(1)} %get-tuple-element.5, f32[96,128]{1,0:T(8,128)S(1)} %fusion.7, bf16[1,3584,128]{2,1,0:T(8,128)(2,1)S(1)} %copy-done.2, bf16[96,3712]{1,0:T(8,128)(2,1)S(1)} %concatenate.12), kind=kOutput, calls=%fused_computation.1 | convolution fusion | flops 177610752 | bytes 3949056 | tf_op jit(solution)/shard_map/dot_general | solution.py:126
  38.4 1.0 %collective-permute-start.10 = (bf16[24,3584]{1,0:T(8,128)(2,1)S(1)}, bf16[24,3584]{1,0:T(8,128)(2,1)S(1)}, u32[]{:S(2)}, u32[]{:S(2)}) collective-permute-start(bf16[24,3584]{1,0:T(8,128)(2,1)S(1)} %get-tuple-element.8), channel_id=1, source_target_pairs={{0,24},{8,16},{16,8},{24,0},{1,25},{9,17},{17,9},{25,1},{2,26},{10... | collective-permute-start | bytes 516104 | tf_op jit(solution)/shard_map/ppermute | solution.py:89
  39.5 1.5 %collective-permute-start.8 = (bf16[24,3584]{1,0:T(8,128)(2,1)S(1)}, bf16[24,3584]{1,0:T(8,128)(2,1)S(1)}, u32[]{:S(2)}, u32[]{:S(2)}) collective-permute-start(bf16[24,3584]{1,0:T(8,128)(2,1)S(1)} %get-tuple-element.7), channel_id=1, source_target_pairs={{0,8},{8,0},{16,24},{24,16},{1,9},{9,1},{17,25},{25,17},{2,10},{10... | collective-permute-start | bytes 516104 | tf_op jit(solution)/shard_map/ppermute | solution.py:89
  41.0 1.0 %collective-permute-start.9 = (bf16[24,3584]{1,0:T(8,128)(2,1)S(1)}, bf16[24,3584]{1,0:T(8,128)(2,1)S(1)}, u32[]{:S(2)}, u32[]{:S(2)}) collective-permute-start(bf16[24,3584]{1,0:T(8,128)(2,1)S(1)} %get-tuple-element.9), channel_id=1, source_target_pairs={{0,16},{8,24},{16,0},{24,8},{1,17},{9,25},{17,1},{25,9},{2,18},{10... | collective-permute-start | bytes 516104 | tf_op jit(solution)/shard_map/ppermute | solution.py:89
  42.0 4.7 %collective-permute-done.10 = bf16[24,3584]{1,0:T(8,128)(2,1)S(1)} collective-permute-done((bf16[24,3584]{1,0:T(8,128)(2,1)S(1)}, bf16[24,3584]{1,0:T(8,128)(2,1)S(1)}, u32[]{:S(2)}, u32[]{:S(2)}) %collective-permute-start.10) | collective-permute-done | bytes 172064 | tf_op jit(solution)/shard_map/ppermute | solution.py:89
  46.6 2.4 %collective-permute-done.8 = bf16[24,3584]{1,0:T(8,128)(2,1)S(1)} collective-permute-done((bf16[24,3584]{1,0:T(8,128)(2,1)S(1)}, bf16[24,3584]{1,0:T(8,128)(2,1)S(1)}, u32[]{:S(2)}, u32[]{:S(2)}) %collective-permute-start.8) | collective-permute-done | bytes 172064 | tf_op jit(solution)/shard_map/ppermute | solution.py:89
  49.1 0.4 collective-permute-done.9
  49.5 0.1 add_convert_fusion.1
  49.6 0.1 collective-permute-start.11
  49.7 1.6 %collective-permute-start.12 = (bf16[6,3584]{1,0:T(8,128)(2,1)S(1)}, bf16[6,3584]{1,0:T(8,128)(2,1)S(1)}, u32[]{:S(2)}, u32[]{:S(2)}) collective-permute-start(bf16[6,3584]{1,0:T(8,128)(2,1)S(1)} %get-tuple-element.12), channel_id=1, source_target_pairs={{0,4},{1,5},{2,6},{3,7},{4,0},{5,1},{6,2},{7,3},{8,12},{9,13},{10,... | collective-permute-start | bytes 129032 | tf_op jit(solution)/shard_map/ppermute | solution.py:89
  51.3 2.8 %collective-permute-start.13 = (bf16[6,3584]{1,0:T(8,128)(2,1)S(1)}, bf16[6,3584]{1,0:T(8,128)(2,1)S(1)}, u32[]{:S(2)}, u32[]{:S(2)}) collective-permute-start(bf16[6,3584]{1,0:T(8,128)(2,1)S(1)} %get-tuple-element.11), channel_id=1, source_target_pairs={{0,6},{1,7},{2,4},{3,5},{4,2},{5,3},{6,0},{7,1},{8,14},{9,15},{10,... | collective-permute-start | bytes 129032 | tf_op jit(solution)/shard_map/ppermute | solution.py:89
  54.1 0.7 %collective-permute-done.11 = bf16[6,3584]{1,0:T(8,128)(2,1)S(1)} collective-permute-done((bf16[6,3584]{1,0:T(8,128)(2,1)S(1)}, bf16[6,3584]{1,0:T(8,128)(2,1)S(1)}, u32[]{:S(2)}, u32[]{:S(2)}) %collective-permute-start.11) | collective-permute-done | bytes 43040 | tf_op jit(solution)/shard_map/ppermute | solution.py:89
  54.8 2.8 %collective-permute-done.12 = bf16[6,3584]{1,0:T(8,128)(2,1)S(1)} collective-permute-done((bf16[6,3584]{1,0:T(8,128)(2,1)S(1)}, bf16[6,3584]{1,0:T(8,128)(2,1)S(1)}, u32[]{:S(2)}, u32[]{:S(2)}) %collective-permute-start.12) | collective-permute-done | bytes 43040 | tf_op jit(solution)/shard_map/ppermute | solution.py:89
  57.6 0.0 collective-permute-done.13
  57.6 0.7 %fusion.17 = bf16[1,1,6,3584]{3,2,1,0:T(8,128)(2,1)} fusion(bf16[6,3584]{1,0:T(8,128)(2,1)S(1)} %collective-permute-done.13, bf16[6,3584]{1,0:T(8,128)(2,1)S(1)} %collective-permute-done.12, bf16[6,3584]{1,0:T(8,128)(2,1)S(1)} %collective-permute-done.11, bf16[24,3584]{1,0:T(8,128)(2,1)S(1)} %add_convert_fusion.1), kind=kLoop, calls=%fused_computation.22 | loop fusion | flops 172032 | bytes 215040 | tf_op jit(solution)/shard_map/reshape | solution.py:134
  (4 shorter events, 0.1 us)
Async XLA Ops:
  0.0 30.7 %copy-start = (bf16[1,128,3584]{2,1,0:T(8,128)(2,1)S(1)}, bf16[1,128,3584]{2,1,0:T(8,128)(2,1)}, u32[]{:S(2)}) copy-start(bf16[1,128,3584]{2,1,0:T(8,128)(2,1)} %param.11) | copy-start | bytes 2752516
  2.4 26.0 %copy-start.1 = (bf16[1,3584,128]{2,1,0:T(8,128)(2,1)S(1)}, bf16[1,3584,128]{2,1,0:T(8,128)(2,1)}, u32[]{:S(2)}) copy-start(bf16[1,3584,128]{2,1,0:T(8,128)(2,1)} %param.10) | copy-start | bytes 2752516
  2.4 5.7 %collective-permute-start = (bf16[6,3712]{1,0:T(8,128)(2,1)S(1)}, bf16[6,3712]{1,0:T(8,128)(2,1)S(1)}, u32[]{:S(2)}, u32[]{:S(2)}) collective-permute-start(bf16[6,3712]{1,0:T(8,128)(2,1)S(1)} %pad_maximum_fusion.1), channel_id=1, source_target_pairs={{0,2},{1,3},{2,0},{3,1},{4,6},{5,7},{6,4},{7,5},{8,10},{9,11},{10,... | collective-permute-start | bytes 133640 | tf_op jit(solution)/shard_map/ppermute | solution.py:85
  5.5 6.3 %collective-permute-start.1 = (bf16[6,3712]{1,0:T(8,128)(2,1)S(1)}, bf16[6,3712]{1,0:T(8,128)(2,1)S(1)}, u32[]{:S(2)}, u32[]{:S(2)}) collective-permute-start(bf16[6,3712]{1,0:T(8,128)(2,1)S(1)} %pad_maximum_fusion.1), channel_id=1, source_target_pairs={{0,4},{1,5},{2,6},{3,7},{4,0},{5,1},{6,2},{7,3},{8,12},{9,13},{10,... | collective-permute-start | bytes 133640 | tf_op jit(solution)/shard_map/ppermute | solution.py:85
  8.1 6.0 %collective-permute-start.2 = (bf16[6,3712]{1,0:T(8,128)(2,1)S(1)}, bf16[6,3712]{1,0:T(8,128)(2,1)S(1)}, u32[]{:S(2)}, u32[]{:S(2)}) collective-permute-start(bf16[6,3712]{1,0:T(8,128)(2,1)S(1)} %pad_maximum_fusion.1), channel_id=1, source_target_pairs={{0,6},{1,7},{2,4},{3,5},{4,2},{5,3},{6,0},{7,1},{8,14},{9,15},{10,... | collective-permute-start | bytes 133640 | tf_op jit(solution)/shard_map/ppermute | solution.py:85
  15.0 7.1 %collective-permute-start.3 = (bf16[24,3712]{1,0:T(8,128)(2,1)S(1)}, bf16[24,3712]{1,0:T(8,128)(2,1)S(1)}, u32[]{:S(2)}, u32[]{:S(2)}) collective-permute-start(bf16[24,3712]{1,0:T(8,128)(2,1)S(1)} %pad_maximum_fusion), channel_id=1, source_target_pairs={{0,8},{8,0},{16,24},{24,16},{1,9},{9,1},{17,25},{25,17},{2,10},{10... | collective-permute-start | bytes 534536 | tf_op jit(solution)/shard_map/ppermute | solution.py:85
  16.5 8.7 %collective-permute-start.4 = (bf16[24,3712]{1,0:T(8,128)(2,1)S(1)}, bf16[24,3712]{1,0:T(8,128)(2,1)S(1)}, u32[]{:S(2)}, u32[]{:S(2)}) collective-permute-start(bf16[24,3712]{1,0:T(8,128)(2,1)S(1)} %pad_maximum_fusion), channel_id=1, source_target_pairs={{0,16},{8,24},{16,0},{24,8},{1,17},{9,25},{17,1},{25,9},{2,18},{10... | collective-permute-start | bytes 534536 | tf_op jit(solution)/shard_map/ppermute | solution.py:85
  18.1 7.2 %collective-permute-start.5 = (bf16[24,3712]{1,0:T(8,128)(2,1)S(1)}, bf16[24,3712]{1,0:T(8,128)(2,1)S(1)}, u32[]{:S(2)}, u32[]{:S(2)}) collective-permute-start(bf16[24,3712]{1,0:T(8,128)(2,1)S(1)} %pad_maximum_fusion), channel_id=1, source_target_pairs={{0,24},{8,16},{16,8},{24,0},{1,25},{9,17},{17,9},{25,1},{2,26},{10... | collective-permute-start | bytes 534536 | tf_op jit(solution)/shard_map/ppermute | solution.py:85
  26.0 4.7 %copy-start.2 = (bf16[1,3584,128]{2,1,0:T(8,128)(2,1)S(1)}, bf16[1,3584,128]{2,1,0:T(8,128)(2,1)}, u32[]{:S(2)}) copy-start(bf16[1,3584,128]{2,1,0:T(8,128)(2,1)} %param.9) | copy-start | bytes 2752516
  26.0 2.4 %collective-permute-start.6 = (bf16[96,3712]{1,0:T(8,128)(2,1)S(1)}, bf16[96,3712]{1,0:T(8,128)(2,1)}, u32[]{:S(2)}, u32[]{:S(2)}) collective-permute-start(bf16[96,3712]{1,0:T(8,128)(2,1)S(1)} %concatenate.12), channel_id=1, source_target_pairs={{0,1},{1,0},{2,3},{3,2},{4,5},{5,4},{6,7},{7,6},{8,9},{9,8},{10,11... | collective-permute-start | bytes 2138120 | tf_op jit(solution)/shard_map/ppermute | solution.py:85
  33.4 2.4 %collective-permute-start.7 = (bf16[96,3584]{1,0:T(8,128)(2,1)}, bf16[96,3584]{1,0:T(8,128)(2,1)S(1)}, u32[]{:S(2)}, u32[]{:S(2)}) collective-permute-start(bf16[96,3584]{1,0:T(8,128)(2,1)} %multiply_convert_fusion), channel_id=1, source_target_pairs={{0,1},{1,0},{2,3},{3,2},{4,5},{5,4},{6,7},{7,6},{8,9},{9,8},{10,11... | collective-permute-start | bytes 2064392 | tf_op jit(solution)/shard_map/ppermute | solution.py:89
  35.7 0.9 %copy-start.3 = (bf16[96,3584]{1,0:T(8,128)(2,1)}, bf16[96,3584]{1,0:T(8,128)(2,1)S(1)}, u32[]{:S(2)}) copy-start(bf16[96,3584]{1,0:T(8,128)(2,1)S(1)} %collective-permute-done.7) | copy-start | bytes 2064388
  38.4 8.2 %collective-permute-start.10 = (bf16[24,3584]{1,0:T(8,128)(2,1)S(1)}, bf16[24,3584]{1,0:T(8,128)(2,1)S(1)}, u32[]{:S(2)}, u32[]{:S(2)}) collective-permute-start(bf16[24,3584]{1,0:T(8,128)(2,1)S(1)} %get-tuple-element.8), channel_id=1, source_target_pairs={{0,24},{8,16},{16,8},{24,0},{1,25},{9,17},{17,9},{25,1},{2,26},{10... | collective-permute-start | bytes 516104 | tf_op jit(solution)/shard_map/ppermute | solution.py:89
  39.5 9.6 %collective-permute-start.8 = (bf16[24,3584]{1,0:T(8,128)(2,1)S(1)}, bf16[24,3584]{1,0:T(8,128)(2,1)S(1)}, u32[]{:S(2)}, u32[]{:S(2)}) collective-permute-start(bf16[24,3584]{1,0:T(8,128)(2,1)S(1)} %get-tuple-element.7), channel_id=1, source_target_pairs={{0,8},{8,0},{16,24},{24,16},{1,9},{9,1},{17,25},{25,17},{2,10},{10... | collective-permute-start | bytes 516104 | tf_op jit(solution)/shard_map/ppermute | solution.py:89
  41.0 8.5 %collective-permute-start.9 = (bf16[24,3584]{1,0:T(8,128)(2,1)S(1)}, bf16[24,3584]{1,0:T(8,128)(2,1)S(1)}, u32[]{:S(2)}, u32[]{:S(2)}) collective-permute-start(bf16[24,3584]{1,0:T(8,128)(2,1)S(1)} %get-tuple-element.9), channel_id=1, source_target_pairs={{0,16},{8,24},{16,0},{24,8},{1,17},{9,25},{17,1},{25,9},{2,18},{10... | collective-permute-start | bytes 516104 | tf_op jit(solution)/shard_map/ppermute | solution.py:89
  49.6 5.2 %collective-permute-start.11 = (bf16[6,3584]{1,0:T(8,128)(2,1)S(1)}, bf16[6,3584]{1,0:T(8,128)(2,1)S(1)}, u32[]{:S(2)}, u32[]{:S(2)}) collective-permute-start(bf16[6,3584]{1,0:T(8,128)(2,1)S(1)} %get-tuple-element.10), channel_id=1, source_target_pairs={{0,2},{1,3},{2,0},{3,1},{4,6},{5,7},{6,4},{7,5},{8,10},{9,11},{10,... | collective-permute-start | bytes 129032 | tf_op jit(solution)/shard_map/ppermute | solution.py:89
  49.7 7.9 %collective-permute-start.12 = (bf16[6,3584]{1,0:T(8,128)(2,1)S(1)}, bf16[6,3584]{1,0:T(8,128)(2,1)S(1)}, u32[]{:S(2)}, u32[]{:S(2)}) collective-permute-start(bf16[6,3584]{1,0:T(8,128)(2,1)S(1)} %get-tuple-element.12), channel_id=1, source_target_pairs={{0,4},{1,5},{2,6},{3,7},{4,0},{5,1},{6,2},{7,3},{8,12},{9,13},{10,... | collective-permute-start | bytes 129032 | tf_op jit(solution)/shard_map/ppermute | solution.py:89
  51.3 6.3 %collective-permute-start.13 = (bf16[6,3584]{1,0:T(8,128)(2,1)S(1)}, bf16[6,3584]{1,0:T(8,128)(2,1)S(1)}, u32[]{:S(2)}, u32[]{:S(2)}) collective-permute-start(bf16[6,3584]{1,0:T(8,128)(2,1)S(1)} %get-tuple-element.11), channel_id=1, source_target_pairs={{0,6},{1,7},{2,4},{3,5},{4,2},{5,3},{6,0},{7,1},{8,14},{9,15},{10,... | collective-permute-start | bytes 129032 | tf_op jit(solution)/shard_map/ppermute | solution.py:89

commit v2 on v1

--- a/solution.py
+++ b/solution.py
@@ -1,6 +1,10 @@
+import functools
+
 import jax
 import jax.numpy as jnp
 from jax import lax
+from jax.experimental import pallas as pl
+from jax.experimental.pallas import tpu as pltpu
 from jax.sharding import PartitionSpec as P
 
 EXP_GRP = 4
@@ -93,6 +97,51 @@
     return total
 
 
+def expert_kernel(slices, rows_ref, *refs):
+    gates, ups, downs, out_ref = refs[:slices], refs[slices : 2 * slices], refs[2 * slices : -1], refs[-1]
+    feature = out_ref.shape[1]
+    own_expert = lax.axis_index("grp") * EXP_GRP + lax.axis_index("loc") // slices
+    features = rows_ref[:, :feature]
+    table = rows_ref[:, feature:].astype(jnp.float32)
+    lanes = lax.broadcasted_iota(jnp.int32, table.shape, 1)
+    weight = jnp.sum(jnp.where(lanes == own_expert, table, 0.0), axis=1, keepdims=True)
+    hidden = []
+    for gate_ref, up_ref in zip(gates, ups):
+        units = gate_ref.shape[1]
+        both = jnp.dot(
+            features,
+            jnp.concatenate([gate_ref[...], up_ref[...]], axis=1),
+            preferred_element_type=jnp.float32,
+        )
+        gate_out, up_out = both[:, :units], both[:, units:]
+        hidden.append((gate_out / (1.0 + jnp.exp(-gate_out)) * up_out).astype(jnp.bfloat16))
+    part = jnp.dot(
+        jnp.concatenate(hidden, axis=1),
+        jnp.concatenate([d[...] for d in downs], axis=0),
+        preferred_element_type=jnp.float32,
+    )
+    out_ref[...] = (part * weight).astype(out_ref.dtype)
+
+
+def run_expert(rows, gates, ups, downs):
+    slices = len(gates)
+    feature = downs[0].shape[1]
+    count = rows.shape[0]
+    weight_elements = slices * 3 * gates[0].size
+    return pl.pallas_call(
+        functools.partial(expert_kernel, slices),
+        out_shape=jax.ShapeDtypeStruct((count, feature), jnp.bfloat16),
+        in_specs=[pl.BlockSpec(memory_space=pltpu.VMEM)] * (1 + 3 * slices),
+        out_specs=pl.BlockSpec(memory_space=pltpu.VMEM),
+        compiler_params=pltpu.CompilerParams(vmem_limit_bytes=32 * 1024 * 1024),
+        cost_estimate=pl.CostEstimate(
+            flops=2 * count * weight_elements,
+            bytes_accessed=2 * weight_elements,
+            transcendentals=count * slices * gates[0].shape[1],
+        ),
+    )(rows, *gates, *ups, *downs)
+
+
 def dense_body(hidden_in, expert_ids, combine, w_gate, w_up, w_down):
     group_count = lax.axis_size("grp")
     loc_count = lax.axis_size("loc")
@@ -112,23 +161,15 @@
     member_steps = [slices * k for k in range(1, EXP_GRP)]
     group_steps = list(range(1, group_count))
     slice_steps = list(range(1, slices))
+    gates, ups, downs = (
+        spread(w[0], "loc", loc_count, slice_steps) for w in (w_gate, w_up, w_down)
+    )
     rows = jnp.concatenate(spread(rows, "loc", loc_count, member_steps), axis=0)
-    rows = jnp.concatenate(spread(rows, "grp", group_count, group_steps), axis=0)
-    own_expert = lax.axis_index("grp") * EXP_GRP + lax.axis_index("loc") // slices
-    pick = (lanes == own_expert).astype(jnp.float32)
-    partials = []
-    for block in spread(rows, "loc", loc_count, slice_steps):
-        features = block[:, :feature]
-        weight = jnp.sum(block[:, feature:].astype(jnp.float32) * pick[None, :], axis=1)
-        gate_out = jnp.dot(features, w_gate[0], preferred_element_type=jnp.float32)
-        up_out = jnp.dot(features, w_up[0], preferred_element_type=jnp.float32)
-        hidden_units = (jax.nn.silu(gate_out) * up_out).astype(jnp.bfloat16)
-        part = jnp.dot(hidden_units, w_down[0], preferred_element_type=jnp.float32)
-        partials.append(part * weight[:, None])
-    partials = partials[:1] + [p.astype(jnp.bfloat16) for p in partials[1:]]
-    total = fold(partials, "loc", loc_count, slice_steps).astype(jnp.bfloat16)
-    chunks = list(total.reshape(group_count, EXP_GRP * tok_count, feature))
-    total = fold(chunks, "grp", group_count, group_steps).astype(jnp.bfloat16)
+    partials = [
+        run_expert(block, gates, ups, downs)
+        for block in spread(rows, "grp", group_count, group_steps)
+    ]
+    total = fold(partials, "grp", group_count, group_steps).astype(jnp.bfloat16)
     chunks = list(total.reshape(EXP_GRP, tok_count, feature))
     total = fold(chunks, "loc", loc_count, member_steps).astype(jnp.bfloat16)
     return total.reshape(1, 1, tok_count, feature)

time: 58.7 us -> 48.6 us (0.83)
  waiting for transfers between devices: 27.8 us -> 14.5 us
  matrix products: 6.21 us -> 0 us
  starting transfers between devices: 17.4 us -> 23.5 us
  Pallas kernels: 0 us -> 4.5 us
  other arithmetic: 4.13 us -> 1.84 us
  local copies, waits for them, and re-layouts: 2.5 us -> 3.83 us
    ppermute x7 -> x9, waiting for transfers between devices: 14.9 us -> 6.47 us  [spread(): lax.ppermute(rows, axis, pairs(size, d))]
    dot_general x4 -> x0, matrix products: 6.21 us -> none  [the longest x2 4.42 us: dense_body(): part = jnp.dot(hidden_units, w_down[0], preferred_element_type=jnp.float32)]
    ppermute x7 -> x9, starting transfers between devices: 9.31 us -> 15.5 us  [spread(): lax.ppermute(rows, axis, pairs(size, d))]
    ppermute x7 -> x6, waiting for transfers between devices: 12.9 us -> 7.99 us  [fold(): lax.ppermute(c, axis, pairs(size, d))]
    pallas_call x0 -> x4, Pallas kernels: none -> 4.5 us  [run_expert(): pl.pallas_call(functools.partial(expert_kernel, slices), out_shape=jax.Sh...]
    unnamed x9 -> x19, local copies, waits for them, and re-layouts: 1.64 us -> 3.78 us
    reduce_sum x1 -> x0, other arithmetic: 0.85 us -> none  [dense_body(): jnp.sum(block[:, feature:].astype(jnp.float32) * pick[None, :], axis=1)]
    concatenate x1, other arithmetic: 0.91 us -> 0.09 us  [dense_body(): rows = jnp.concatenate(spread(rows, 'loc', loc_count, member_steps), axis=0)]
  transfers between devices with their start and end apart: 14 -> 15, of which waited for: 11 -> 6; matrix products, arithmetic and copies ran while one was open for 1% -> 2% of each run, Pallas kernels for 0% -> 9%
where the time goes in v2:
time: 48.6 us; the launch traced here: 48.3 us
  starting transfers between devices  23.5 us (48%)
  waiting for transfers between devices  14.5 us (30%)
  Pallas kernels  4.5 us (9%)
  local copies, waits for them, and re-layouts  3.83 us (8%)
  other arithmetic  1.84 us (4%)
    ppermute x9, starting transfers between devices, spread(): lax.ppermute(rows, axis, pairs(size, d))  15.5 us
    ppermute x6, starting transfers between devices, fold(): lax.ppermute(c, axis, pairs(size, d))  8.07 us
    ppermute x6, waiting for transfers between devices, fold(): lax.ppermute(c, axis, pairs(size, d))  7.99 us
    ppermute x9, waiting for transfers between devices, spread(): lax.ppermute(rows, axis, pairs(size, d))  6.47 us
    pallas_call x4, Pallas kernels, run_expert(): pl.pallas_call(functools.partial(expert_kernel, slices), out_shape=jax.Sh...  4.5 us
    unnamed x19, local copies, waits for them, and re-layouts  3.78 us
  transfers between devices with their start and end apart: 15, of which 6 were waited for; matrix products, arithmetic and copies ran while one was open for 2% of the time, Pallas kernels for 9%

profile of v2, /device:TPU:0, one launch (start us, length us, event | category | flops | bytes accessed | tf_op | source)
XLA Modules:
  0.0 48.3 jit_solution(10197135593136280251)
XLA Ops:
  0.0 0.5 collective-permute-start.3
  0.5 0.1 collective-permute-start.4
  0.5 0.4 collective-permute-start.5
  1.0 0.0 copy-done.7
  1.0 0.2 copy-done.8
  1.2 0.1 select_reduce_fusion
  1.3 0.0 copy-start.6
  1.3 0.9 %pad_maximum_fusion.1 = bf16[6,3712]{1,0:T(8,128)(2,1)S(1)} fusion(bf16[6,128]{1,0:T(8,128)(2,1)S(1)} %select_reduce_fusion, bf16[6,3584]{1,0:T(8,128)(2,1)} %bitcast.27), kind=kLoop, calls=%fused_computation.3 | loop fusion | flops 89088 | bytes 89088 | tf_op jit(solution)/shard_map/concatenate | solution.py:159
  2.2 3.1 %collective-permute-start = (bf16[6,3712]{1,0:T(8,128)(2,1)S(1)}, bf16[6,3712]{1,0:T(8,128)(2,1)S(1)}, u32[]{:S(2)}, u32[]{:S(2)}) collective-permute-start(bf16[6,3712]{1,0:T(8,128)(2,1)S(1)} %pad_maximum_fusion.1), channel_id=1, source_target_pairs={{0,2},{1,3},{2,0},{3,1},{4,6},{5,7},{6,4},{7,5},{8,10},{9,11},{10,... | collective-permute-start | bytes 133640 | tf_op jit(solution)/shard_map/ppermute | solution.py:89
  5.3 2.6 %collective-permute-start.1 = (bf16[6,3712]{1,0:T(8,128)(2,1)S(1)}, bf16[6,3712]{1,0:T(8,128)(2,1)S(1)}, u32[]{:S(2)}, u32[]{:S(2)}) collective-permute-start(bf16[6,3712]{1,0:T(8,128)(2,1)S(1)} %pad_maximum_fusion.1), channel_id=1, source_target_pairs={{0,4},{1,5},{2,6},{3,7},{4,0},{5,1},{6,2},{7,3},{8,12},{9,13},{10,... | collective-permute-start | bytes 133640 | tf_op jit(solution)/shard_map/ppermute | solution.py:89
  7.9 0.0 collective-permute-done
  7.9 4.3 %collective-permute-start.2 = (bf16[6,3712]{1,0:T(8,128)(2,1)S(1)}, bf16[6,3712]{1,0:T(8,128)(2,1)S(1)}, u32[]{:S(2)}, u32[]{:S(2)}) collective-permute-start(bf16[6,3712]{1,0:T(8,128)(2,1)S(1)} %pad_maximum_fusion.1), channel_id=1, source_target_pairs={{0,6},{1,7},{2,4},{3,5},{4,2},{5,3},{6,0},{7,1},{8,14},{9,15},{10,... | collective-permute-start | bytes 133640 | tf_op jit(solution)/shard_map/ppermute | solution.py:89
  12.2 0.0 collective-permute-done.1
  12.2 2.2 %collective-permute-done.2 = bf16[6,3712]{1,0:T(8,128)(2,1)S(1)} collective-permute-done((bf16[6,3712]{1,0:T(8,128)(2,1)S(1)}, bf16[6,3712]{1,0:T(8,128)(2,1)S(1)}, u32[]{:S(2)}, u32[]{:S(2)}) %collective-permute-start.2) | collective-permute-done | bytes 44576 | tf_op jit(solution)/shard_map/ppermute | solution.py:89
  14.3 0.0 copy-done.6
  14.3 0.1 pad_maximum_fusion.rows_ref
  14.4 2.5 %collective-permute-start.10 = (bf16[24,3712]{1,0:T(8,128)(2,1)S(1)}, bf16[24,3712]{1,0:T(8,128)(2,1)S(1)}, u32[]{:S(2)}, u32[]{:S(2)}) collective-permute-start(bf16[24,3712]{1,0:T(8,128)(2,1)S(1)} %pad_maximum_fusion.rows_ref), channel_id=1, source_target_pairs={{0,24},{8,16},{16,8},{24,0},{1,25},{9,17},{17,9},{25,1},{2,26},{10... | collective-permute-start | bytes 534536 | tf_op jit(solution)/shard_map/ppermute | solution.py:89
  16.9 0.5 %collective-permute-start.6 = (bf16[24,3712]{1,0:T(8,128)(2,1)S(1)}, bf16[24,3712]{1,0:T(8,128)(2,1)S(1)}, u32[]{:S(2)}, u32[]{:S(2)}) collective-permute-start(bf16[24,3712]{1,0:T(8,128)(2,1)S(1)} %pad_maximum_fusion.rows_ref), channel_id=1, source_target_pairs={{0,8},{8,0},{16,24},{24,16},{1,9},{9,1},{17,25},{25,17},{2,10},{10... | collective-permute-start | bytes 534536 | tf_op jit(solution)/shard_map/ppermute | solution.py:89
  17.5 4.3 %collective-permute-done.10.rows_ref = bf16[24,3712]{1,0:T(8,128)(2,1)S(1)} collective-permute-done((bf16[24,3712]{1,0:T(8,128)(2,1)S(1)}, bf16[24,3712]{1,0:T(8,128)(2,1)S(1)}, u32[]{:S(2)}, u32[]{:S(2)}) %collective-permute-start.10) | collective-permute-done | bytes 178208 | tf_op jit(solution)/shard_map/ppermute | solution.py:89
  21.8 1.5 %collective-permute-start.8 = (bf16[24,3712]{1,0:T(8,128)(2,1)S(1)}, bf16[24,3712]{1,0:T(8,128)(2,1)S(1)}, u32[]{:S(2)}, u32[]{:S(2)}) collective-permute-start(bf16[24,3712]{1,0:T(8,128)(2,1)S(1)} %pad_maximum_fusion.rows_ref), channel_id=1, source_target_pairs={{0,16},{8,24},{16,0},{24,8},{1,17},{9,25},{17,1},{25,9},{2,18},{10... | collective-permute-start | bytes 534536 | tf_op jit(solution)/shard_map/ppermute | solution.py:89
  23.3 0.0 collective-permute-done.3.refs_1_
  23.3 0.0 collective-permute-done.4.refs_3_
  23.3 0.0 collective-permute-done.5.refs_5_
  23.3 0.0 copy-start
  23.3 1.2 %copy-done = bf16[1,3584,128]{2,1,0:T(8,128)(2,1)S(1)} copy-done((bf16[1,3584,128]{2,1,0:T(8,128)(2,1)S(1)}, bf16[1,3584,128]{2,1,0:T(8,128)(2,1)}, u32[]{:S(2)}) %copy-start) | copy-done | bytes 917528
  24.5 1.2 %copy-done.2 = bf16[1,3584,128]{2,1,0:T(8,128)(2,1)S(1)} copy-done((bf16[1,3584,128]{2,1,0:T(8,128)(2,1)S(1)}, bf16[1,3584,128]{2,1,0:T(8,128)(2,1)}, u32[]{:S(2)}) %copy-start.2) | copy-done | bytes 917528
  25.7 1.2 %copy-done.4 = bf16[1,128,3584]{2,1,0:T(8,128)(2,1)S(1)} copy-done((bf16[1,128,3584]{2,1,0:T(8,128)(2,1)S(1)}, bf16[1,128,3584]{2,1,0:T(8,128)(2,1)}, u32[]{:S(2)}) %copy-start.4) | copy-done | bytes 917528
  26.8 1.1 %shard_map.67 = bf16[24,3584]{1,0:T(8,128)(2,1)S(1)} custom-call(bf16[24,3712]{1,0:T(8,128)(2,1)S(1)} %collective-permute-done.10.rows_ref, bf16[3584,128]{1,0:T(8,128)(2,1)S(1)} %bitcast.13, bf16[3584,128]{1,0:T(8,128)(2,1)S(1)} %collective-permute-done.3.refs_1_, bf16[3584,128]{1,0:T(8,128)(2,1)S(1)} %bitcast.18, ...), custom_call_target="tpu_custom_call" | custom-call | flops 132120576 | bytes 5505024 | tf_op jit(solution)/shard_map/pallas_call | solution.py:131
  28.0 1.5 %collective-permute-start.11 = (bf16[24,3584]{1,0:T(8,128)(2,1)S(1)}, bf16[24,3584]{1,0:T(8,128)(2,1)S(1)}, u32[]{:S(2)}, u32[]{:S(2)}) collective-permute-start(bf16[24,3584]{1,0:T(8,128)(2,1)S(1)} %shard_map.67), channel_id=1, source_target_pairs={{0,24},{8,16},{16,8},{24,0},{1,25},{9,17},{17,9},{25,1},{2,26},{10... | collective-permute-start | bytes 516104 | tf_op jit(solution)/shard_map/ppermute | solution.py:93
  29.4 0.0 collective-permute-done.6.rows_ref
  29.5 0.0 copy-done.3
  29.5 1.1 %shard_map.65 = bf16[24,3584]{1,0:T(8,128)(2,1)S(1)} custom-call(bf16[24,3712]{1,0:T(8,128)(2,1)S(1)} %collective-permute-done.6.rows_ref, bf16[3584,128]{1,0:T(8,128)(2,1)S(1)} %bitcast.14, bf16[3584,128]{1,0:T(8,128)(2,1)S(1)} %collective-permute-done.3.refs_1_, bf16[3584,128]{1,0:T(8,128)(2,1)S(1)} %bitcast.19, ...), custom_call_target="tpu_custom_call" | custom-call | flops 132120576 | bytes 5505024 | tf_op jit(solution)/shard_map/pallas_call | solution.py:131
  30.6 0.6 %collective-permute-start.7 = (bf16[24,3584]{1,0:T(8,128)(2,1)S(1)}, bf16[24,3584]{1,0:T(8,128)(2,1)S(1)}, u32[]{:S(2)}, u32[]{:S(2)}) collective-permute-start(bf16[24,3584]{1,0:T(8,128)(2,1)S(1)} %shard_map.65), channel_id=1, source_target_pairs={{0,8},{8,0},{16,24},{24,16},{1,9},{9,1},{17,25},{25,17},{2,10},{10... | collective-permute-start | bytes 516104 | tf_op jit(solution)/shard_map/ppermute | solution.py:93
  31.2 0.0 collective-permute-done.8.rows_ref
  31.2 1.1 %shard_map.66 = bf16[24,3584]{1,0:T(8,128)(2,1)S(1)} custom-call(bf16[24,3712]{1,0:T(8,128)(2,1)S(1)} %collective-permute-done.8.rows_ref, bf16[3584,128]{1,0:T(8,128)(2,1)S(1)} %bitcast.15, bf16[3584,128]{1,0:T(8,128)(2,1)S(1)} %collective-permute-done.3.refs_1_, bf16[3584,128]{1,0:T(8,128)(2,1)S(1)} %bitcast.20, ...), custom_call_target="tpu_custom_call" | custom-call | flops 132120576 | bytes 5505024 | tf_op jit(solution)/shard_map/pallas_call | solution.py:131
  32.4 1.5 %collective-permute-start.9 = (bf16[24,3584]{1,0:T(8,128)(2,1)S(1)}, bf16[24,3584]{1,0:T(8,128)(2,1)S(1)}, u32[]{:S(2)}, u32[]{:S(2)}) collective-permute-start(bf16[24,3584]{1,0:T(8,128)(2,1)S(1)} %shard_map.66), channel_id=1, source_target_pairs={{0,16},{8,24},{16,0},{24,8},{1,17},{9,25},{17,1},{25,9},{2,18},{10... | collective-permute-start | bytes 516104 | tf_op jit(solution)/shard_map/ppermute | solution.py:93
  33.9 1.1 %shard_map.64 = bf16[24,3584]{1,0:T(8,128)(2,1)S(1)} custom-call(bf16[24,3712]{1,0:T(8,128)(2,1)S(1)} %pad_maximum_fusion.rows_ref, bf16[3584,128]{1,0:T(8,128)(2,1)S(1)} %bitcast.16, bf16[3584,128]{1,0:T(8,128)(2,1)S(1)} %collective-permute-done.3.refs_1_, bf16[3584,128]{1,0:T(8,128)(2,1)S(1)} %bitcast.21, ...), custom_call_target="tpu_custom_call" | custom-call | flops 132120576 | bytes 5505024 | tf_op jit(solution)/shard_map/pallas_call | solution.py:131
  35.0 0.0 collective-permute-done.11
  35.0 1.0 %collective-permute-done.7 = bf16[24,3584]{1,0:T(8,128)(2,1)S(1)} collective-permute-done((bf16[24,3584]{1,0:T(8,128)(2,1)S(1)}, bf16[24,3584]{1,0:T(8,128)(2,1)S(1)}, u32[]{:S(2)}, u32[]{:S(2)}) %collective-permute-start.7) | collective-permute-done | bytes 172064 | tf_op jit(solution)/shard_map/ppermute | solution.py:93
  36.0 1.8 %collective-permute-done.9 = bf16[24,3584]{1,0:T(8,128)(2,1)S(1)} collective-permute-done((bf16[24,3584]{1,0:T(8,128)(2,1)S(1)}, bf16[24,3584]{1,0:T(8,128)(2,1)S(1)}, u32[]{:S(2)}, u32[]{:S(2)}) %collective-permute-start.9) | collective-permute-done | bytes 172064 | tf_op jit(solution)/shard_map/ppermute | solution.py:93
  37.8 0.1 add_convert_fusion
  38.0 0.1 collective-permute-start.12
  38.0 3.6 %collective-permute-start.13 = (bf16[6,3584]{1,0:T(8,128)(2,1)S(1)}, bf16[6,3584]{1,0:T(8,128)(2,1)S(1)}, u32[]{:S(2)}, u32[]{:S(2)}) collective-permute-start(bf16[6,3584]{1,0:T(8,128)(2,1)S(1)} %get-tuple-element.7), channel_id=1, source_target_pairs={{0,4},{1,5},{2,6},{3,7},{4,0},{5,1},{6,2},{7,3},{8,12},{9,13},{10,... | collective-permute-start | bytes 129032 | tf_op jit(solution)/shard_map/ppermute | solution.py:93
  41.6 0.8 %collective-permute-start.14 = (bf16[6,3584]{1,0:T(8,128)(2,1)S(1)}, bf16[6,3584]{1,0:T(8,128)(2,1)S(1)}, u32[]{:S(2)}, u32[]{:S(2)}) collective-permute-start(bf16[6,3584]{1,0:T(8,128)(2,1)S(1)} %get-tuple-element.6), channel_id=1, source_target_pairs={{0,6},{1,7},{2,4},{3,5},{4,2},{5,3},{6,0},{7,1},{8,14},{9,15},{10,... | collective-permute-start | bytes 129032 | tf_op jit(solution)/shard_map/ppermute | solution.py:93
  42.4 0.0 collective-permute-done.12
  42.4 1.4 %collective-permute-done.13 = bf16[6,3584]{1,0:T(8,128)(2,1)S(1)} collective-permute-done((bf16[6,3584]{1,0:T(8,128)(2,1)S(1)}, bf16[6,3584]{1,0:T(8,128)(2,1)S(1)}, u32[]{:S(2)}, u32[]{:S(2)}) %collective-permute-start.13) | collective-permute-done | bytes 43040 | tf_op jit(solution)/shard_map/ppermute | solution.py:93
  43.8 3.8 %collective-permute-done.14 = bf16[6,3584]{1,0:T(8,128)(2,1)S(1)} collective-permute-done((bf16[6,3584]{1,0:T(8,128)(2,1)S(1)}, bf16[6,3584]{1,0:T(8,128)(2,1)S(1)}, u32[]{:S(2)}, u32[]{:S(2)}) %collective-permute-start.14) | collective-permute-done | bytes 43040 | tf_op jit(solution)/shard_map/ppermute | solution.py:93
  47.6 0.7 %fusion = bf16[1,1,6,3584]{3,2,1,0:T(8,128)(2,1)} fusion(bf16[6,3584]{1,0:T(8,128)(2,1)S(1)} %collective-permute-done.14, bf16[6,3584]{1,0:T(8,128)(2,1)S(1)} %collective-permute-done.13, bf16[6,3584]{1,0:T(8,128)(2,1)S(1)} %collective-permute-done.12, bf16[24,3584]{1,0:T(8,128)(2,1)S(1)} %add_convert_fusion), kind=kLoop, calls=%fused_computation.4 | loop fusion | flops 172032 | bytes 215040 | tf_op jit(solution)/shard_map/reshape | solution.py:175
  (12 shorter events, 0.1 us)
Async XLA Ops:
  0.0 1.0 %copy-start.7 = (s32[1,1,6,8]{3,1,2,0:T(1,128)S(1)}, s32[1,1,6,8]{3,1,2,0:T(1,128)}, u32[]{:S(2)}) copy-start(s32[1,1,6,8]{3,1,2,0:T(1,128)} %param.7) | copy-start | bytes 580
  0.0 23.3 %collective-permute-start.3 = (bf16[3584,128]{1,0:T(8,128)(2,1)}, bf16[3584,128]{1,0:T(8,128)(2,1)S(1)}, u32[]{:S(2)}, u32[]{:S(2)}) collective-permute-start(bf16[3584,128]{1,0:T(8,128)(2,1)} %bitcast.12), channel_id=1, source_target_pairs={{0,1},{1,0},{2,3},{3,2},{4,5},{5,4},{6,7},{7,6},{8,9},{9,8},{10,11... | collective-permute-start | bytes 2752520 | tf_op jit(solution)/shard_map/ppermute | solution.py:89
  0.5 22.8 %collective-permute-start.4 = (bf16[3584,128]{1,0:T(8,128)(2,1)}, bf16[3584,128]{1,0:T(8,128)(2,1)S(1)}, u32[]{:S(2)}, u32[]{:S(2)}) collective-permute-start(bf16[3584,128]{1,0:T(8,128)(2,1)} %bitcast.17), channel_id=1, source_target_pairs={{0,1},{1,0},{2,3},{3,2},{4,5},{5,4},{6,7},{7,6},{8,9},{9,8},{10,11... | collective-permute-start | bytes 2752520 | tf_op jit(solution)/shard_map/ppermute | solution.py:89
  0.5 0.7 %copy-start.8 = (bf16[1,1,6,8]{3,2,1,0:T(8,128)(2,1)S(1)}, bf16[1,1,6,8]{3,2,1,0:T(8,128)(2,1)}, u32[]{:S(2)}) copy-start(bf16[1,1,6,8]{3,2,1,0:T(8,128)(2,1)} %param.8) | copy-start | bytes 292
  0.5 22.8 %collective-permute-start.5 = (bf16[128,3584]{1,0:T(8,128)(2,1)}, bf16[128,3584]{1,0:T(8,128)(2,1)S(1)}, u32[]{:S(2)}, u32[]{:S(2)}) collective-permute-start(bf16[128,3584]{1,0:T(8,128)(2,1)} %bitcast.22), channel_id=1, source_target_pairs={{0,1},{1,0},{2,3},{3,2},{4,5},{5,4},{6,7},{7,6},{8,9},{9,8},{10,11... | collective-permute-start | bytes 2752520 | tf_op jit(solution)/shard_map/ppermute | solution.py:89
  1.3 13.0 %copy-start.6 = (bf16[1,1,6,3584]{3,2,1,0:T(8,128)(2,1)S(1)}, bf16[1,1,6,3584]{3,2,1,0:T(8,128)(2,1)}, u32[]{:S(2)}) copy-start(bf16[1,1,6,3584]{3,2,1,0:T(8,128)(2,1)} %param.6) | copy-start | bytes 129028
  2.2 5.7 %collective-permute-start = (bf16[6,3712]{1,0:T(8,128)(2,1)S(1)}, bf16[6,3712]{1,0:T(8,128)(2,1)S(1)}, u32[]{:S(2)}, u32[]{:S(2)}) collective-permute-start(bf16[6,3712]{1,0:T(8,128)(2,1)S(1)} %pad_maximum_fusion.1), channel_id=1, source_target_pairs={{0,2},{1,3},{2,0},{3,1},{4,6},{5,7},{6,4},{7,5},{8,10},{9,11},{10,... | collective-permute-start | bytes 133640 | tf_op jit(solution)/shard_map/ppermute | solution.py:89
  5.3 6.9 %collective-permute-start.1 = (bf16[6,3712]{1,0:T(8,128)(2,1)S(1)}, bf16[6,3712]{1,0:T(8,128)(2,1)S(1)}, u32[]{:S(2)}, u32[]{:S(2)}) collective-permute-start(bf16[6,3712]{1,0:T(8,128)(2,1)S(1)} %pad_maximum_fusion.1), channel_id=1, source_target_pairs={{0,4},{1,5},{2,6},{3,7},{4,0},{5,1},{6,2},{7,3},{8,12},{9,13},{10,... | collective-permute-start | bytes 133640 | tf_op jit(solution)/shard_map/ppermute | solution.py:89
  7.9 6.4 %collective-permute-start.2 = (bf16[6,3712]{1,0:T(8,128)(2,1)S(1)}, bf16[6,3712]{1,0:T(8,128)(2,1)S(1)}, u32[]{:S(2)}, u32[]{:S(2)}) collective-permute-start(bf16[6,3712]{1,0:T(8,128)(2,1)S(1)} %pad_maximum_fusion.1), channel_id=1, source_target_pairs={{0,6},{1,7},{2,4},{3,5},{4,2},{5,3},{6,0},{7,1},{8,14},{9,15},{10,... | collective-permute-start | bytes 133640 | tf_op jit(solution)/shard_map/ppermute | solution.py:89
  14.4 7.3 %collective-permute-start.10 = (bf16[24,3712]{1,0:T(8,128)(2,1)S(1)}, bf16[24,3712]{1,0:T(8,128)(2,1)S(1)}, u32[]{:S(2)}, u32[]{:S(2)}) collective-permute-start(bf16[24,3712]{1,0:T(8,128)(2,1)S(1)} %pad_maximum_fusion.rows_ref), channel_id=1, source_target_pairs={{0,24},{8,16},{16,8},{24,0},{1,25},{9,17},{17,9},{25,1},{2,26},{10... | collective-permute-start | bytes 534536 | tf_op jit(solution)/shard_map/ppermute | solution.py:89
  16.9 12.5 %collective-permute-start.6 = (bf16[24,3712]{1,0:T(8,128)(2,1)S(1)}, bf16[24,3712]{1,0:T(8,128)(2,1)S(1)}, u32[]{:S(2)}, u32[]{:S(2)}) collective-permute-start(bf16[24,3712]{1,0:T(8,128)(2,1)S(1)} %pad_maximum_fusion.rows_ref), channel_id=1, source_target_pairs={{0,8},{8,0},{16,24},{24,16},{1,9},{9,1},{17,25},{25,17},{2,10},{10... | collective-permute-start | bytes 534536 | tf_op jit(solution)/shard_map/ppermute | solution.py:89
  21.8 9.5 %collective-permute-start.8 = (bf16[24,3712]{1,0:T(8,128)(2,1)S(1)}, bf16[24,3712]{1,0:T(8,128)(2,1)S(1)}, u32[]{:S(2)}, u32[]{:S(2)}) collective-permute-start(bf16[24,3712]{1,0:T(8,128)(2,1)S(1)} %pad_maximum_fusion.rows_ref), channel_id=1, source_target_pairs={{0,16},{8,24},{16,0},{24,8},{1,17},{9,25},{17,1},{25,9},{2,18},{10... | collective-permute-start | bytes 534536 | tf_op jit(solution)/shard_map/ppermute | solution.py:89
  23.3 1.2 %copy-start = (bf16[1,3584,128]{2,1,0:T(8,128)(2,1)S(1)}, bf16[1,3584,128]{2,1,0:T(8,128)(2,1)}, u32[]{:S(2)}) copy-start(bf16[1,3584,128]{2,1,0:T(8,128)(2,1)} %param.9) | copy-start | bytes 2752516
  24.5 1.2 %copy-start.2 = (bf16[1,3584,128]{2,1,0:T(8,128)(2,1)S(1)}, bf16[1,3584,128]{2,1,0:T(8,128)(2,1)}, u32[]{:S(2)}) copy-start(bf16[1,3584,128]{2,1,0:T(8,128)(2,1)} %param.10) | copy-start | bytes 2752516
  25.7 1.2 %copy-start.4 = (bf16[1,128,3584]{2,1,0:T(8,128)(2,1)S(1)}, bf16[1,128,3584]{2,1,0:T(8,128)(2,1)}, u32[]{:S(2)}) copy-start(bf16[1,128,3584]{2,1,0:T(8,128)(2,1)} %param.11) | copy-start | bytes 2752516
  26.8 2.6 %copy-start.1 = (bf16[1,3584,128]{2,1,0:T(8,128)(2,1)S(1)}, bf16[1,3584,128]{2,1,0:T(8,128)(2,1)}, u32[]{:S(2)}) copy-start(bf16[1,3584,128]{2,1,0:T(8,128)(2,1)} %param.9) | copy-start | bytes 2752516
  26.8 2.6 %copy-start.3 = (bf16[1,3584,128]{2,1,0:T(8,128)(2,1)S(1)}, bf16[1,3584,128]{2,1,0:T(8,128)(2,1)}, u32[]{:S(2)}) copy-start(bf16[1,3584,128]{2,1,0:T(8,128)(2,1)} %param.10) | copy-start | bytes 2752516
  26.8 2.6 %copy-start.5 = (bf16[1,128,3584]{2,1,0:T(8,128)(2,1)S(1)}, bf16[1,128,3584]{2,1,0:T(8,128)(2,1)}, u32[]{:S(2)}) copy-start(bf16[1,128,3584]{2,1,0:T(8,128)(2,1)} %param.11) | copy-start | bytes 2752516
  28.0 7.0 %collective-permute-start.11 = (bf16[24,3584]{1,0:T(8,128)(2,1)S(1)}, bf16[24,3584]{1,0:T(8,128)(2,1)S(1)}, u32[]{:S(2)}, u32[]{:S(2)}) collective-permute-start(bf16[24,3584]{1,0:T(8,128)(2,1)S(1)} %shard_map.67), channel_id=1, source_target_pairs={{0,24},{8,16},{16,8},{24,0},{1,25},{9,17},{17,9},{25,1},{2,26},{10... | collective-permute-start | bytes 516104 | tf_op jit(solution)/shard_map/ppermute | solution.py:93
  30.6 5.5 %collective-permute-start.7 = (bf16[24,3584]{1,0:T(8,128)(2,1)S(1)}, bf16[24,3584]{1,0:T(8,128)(2,1)S(1)}, u32[]{:S(2)}, u32[]{:S(2)}) collective-permute-start(bf16[24,3584]{1,0:T(8,128)(2,1)S(1)} %shard_map.65), channel_id=1, source_target_pairs={{0,8},{8,0},{16,24},{24,16},{1,9},{9,1},{17,25},{25,17},{2,10},{10... | collective-permute-start | bytes 516104 | tf_op jit(solution)/shard_map/ppermute | solution.py:93
  32.4 5.5 %collective-permute-start.9 = (bf16[24,3584]{1,0:T(8,128)(2,1)S(1)}, bf16[24,3584]{1,0:T(8,128)(2,1)S(1)}, u32[]{:S(2)}, u32[]{:S(2)}) collective-permute-start(bf16[24,3584]{1,0:T(8,128)(2,1)S(1)} %shard_map.66), channel_id=1, source_target_pairs={{0,16},{8,24},{16,0},{24,8},{1,17},{9,25},{17,1},{25,9},{2,18},{10... | collective-permute-start | bytes 516104 | tf_op jit(solution)/shard_map/ppermute | solution.py:93
  38.0 4.5 %collective-permute-start.12 = (bf16[6,3584]{1,0:T(8,128)(2,1)S(1)}, bf16[6,3584]{1,0:T(8,128)(2,1)S(1)}, u32[]{:S(2)}, u32[]{:S(2)}) collective-permute-start(bf16[6,3584]{1,0:T(8,128)(2,1)S(1)} %get-tuple-element.5), channel_id=1, source_target_pairs={{0,2},{1,3},{2,0},{3,1},{4,6},{5,7},{6,4},{7,5},{8,10},{9,11},{10,... | collective-permute-start | bytes 129032 | tf_op jit(solution)/shard_map/ppermute | solution.py:93
  38.0 5.7 %collective-permute-start.13 = (bf16[6,3584]{1,0:T(8,128)(2,1)S(1)}, bf16[6,3584]{1,0:T(8,128)(2,1)S(1)}, u32[]{:S(2)}, u32[]{:S(2)}) collective-permute-start(bf16[6,3584]{1,0:T(8,128)(2,1)S(1)} %get-tuple-element.7), channel_id=1, source_target_pairs={{0,4},{1,5},{2,6},{3,7},{4,0},{5,1},{6,2},{7,3},{8,12},{9,13},{10,... | collective-permute-start | bytes 129032 | tf_op jit(solution)/shard_map/ppermute | solution.py:93
  41.6 6.0 %collective-permute-start.14 = (bf16[6,3584]{1,0:T(8,128)(2,1)S(1)}, bf16[6,3584]{1,0:T(8,128)(2,1)S(1)}, u32[]{:S(2)}, u32[]{:S(2)}) collective-permute-start(bf16[6,3584]{1,0:T(8,128)(2,1)S(1)} %get-tuple-element.6), channel_id=1, source_target_pairs={{0,6},{1,7},{2,4},{3,5},{4,2},{5,3},{6,0},{7,1},{8,14},{9,15},{10,... | collective-permute-start | bytes 129032 | tf_op jit(solution)/shard_map/ppermute | solution.py:93

commit v3 on v2

--- a/solution.py
+++ b/solution.py
@@ -10,6 +10,7 @@
 EXP_GRP = 4
 CAP = 24
 LANES = 128
+SUBLANES = 8
 
 
 def packed_body(hidden_in, expert_ids, combine, w_gate, w_up, w_down):
@@ -85,16 +86,112 @@
     return [(i, i ^ distance) for i in range(size)]
 
 
-def spread(rows, axis, size, distances):
-    return [rows] + [lax.ppermute(rows, axis, pairs(size, d)) for d in distances]
-
-
-def fold(chunks, axis, size, distances):
-    arrived = [lax.ppermute(c, axis, pairs(size, d)) for c, d in zip(chunks[1:], distances)]
-    total = chunks[0].astype(jnp.float32)
-    for part in arrived:
-        total = total + part.astype(jnp.float32)
-    return total
+def swap(rows, axis, distance):
+    return lax.ppermute(rows, axis, pairs(lax.axis_size(axis), distance))
+
+
+def tails_per_row(tok_count):
+    return tok_count // (SUBLANES - tok_count)
+
+
+def tail_width(tok_count, feature):
+    return feature // (tails_per_row(tok_count) + 1)
+
+
+def can_pack(tok_count, feature):
+    spare = SUBLANES - tok_count
+    if spare <= 0 or tok_count % spare:
+        return False
+    return feature % (LANES * (tails_per_row(tok_count) + 1)) == 0
+
+
+def tail_places(tok_count, feature):
+    per_row, width = tails_per_row(tok_count), tail_width(tok_count, feature)
+    for t in range(tok_count):
+        yield t, tok_count + t // per_row, (t % per_row) * width, width
+
+
+def pack_rows(source, first, tok_count, feature, target):
+    body = feature - tail_width(tok_count, feature)
+    target[:tok_count, :body] = source[first : first + tok_count, :body]
+    for t, row, lane, width in tail_places(tok_count, feature):
+        target[row : row + 1, lane : lane + width] = source[first + t : first + t + 1, body:feature]
+
+
+def unpack_rows(source, target, first, tok_count, feature):
+    body = feature - tail_width(tok_count, feature)
+    target[first : first + tok_count, :body] = source[:tok_count, :body]
+    for t, row, lane, width in tail_places(tok_count, feature):
+        target[first + t : first + t + 1, body:feature] = source[row : row + 1, lane : lane + width]
+
+
+VMEM = pl.BlockSpec(memory_space=pltpu.VMEM)
+HBM = pl.BlockSpec(memory_space=pltpu.HBM)
+
+
+def in_hbm(array):
+    return pltpu.with_memory_space_constraint(array, pltpu.HBM)
+
+
+def call(kernel, outs, args, scratch=(), specs=None, flops=0, traffic=0):
+    return pl.pallas_call(
+        kernel,
+        out_shape=outs,
+        in_specs=specs or [VMEM] * len(args),
+        out_specs=jax.tree.map(lambda _: VMEM, outs),
+        scratch_shapes=list(scratch),
+        compiler_params=pltpu.CompilerParams(vmem_limit_bytes=24 * 1024 * 1024),
+        cost_estimate=pl.CostEstimate(flops=flops, bytes_accessed=traffic, transcendentals=0),
+    )(*args)
+
+
+def prepare_kernel(rows_hbm, ids_hbm, combine_hbm, out_ref, rows, ids, picks, wide, packed, sems):
+    copies = [
+        pltpu.make_async_copy(source, target, sems.at[i])
+        for i, (source, target) in enumerate(
+            ((rows_hbm, rows), (ids_hbm, ids), (combine_hbm, picks))
+        )
+    ]
+    for c in copies:
+        c.start()
+    for c in copies:
+        c.wait()
+    tok_count, feature = rows.shape
+    body = feature - tail_width(tok_count, feature)
+    wide[...] = rows[...].astype(jnp.float32)
+    packed[:, body:] = jnp.zeros((SUBLANES, LANES), jnp.float32)
+    pack_rows(wide, 0, tok_count, feature, packed)
+    weights = picks[...].astype(jnp.float32)
+    lanes = lax.broadcasted_iota(jnp.int32, (1, LANES), 1)
+    for t in range(tok_count):
+        chosen = ids[t]
+        row = jnp.zeros((1, LANES), jnp.float32)
+        for k in range(chosen.shape[1]):
+            row = row + jnp.where(lanes == chosen[:, k : k + 1], weights[t : t + 1, k : k + 1], 0.0)
+        packed[t : t + 1, body:] = row
+    out_ref[...] = packed[...].astype(jnp.bfloat16)
+
+
+def join_kernel(tok_count, feature, *refs):
+    pieces, out_ref, narrow, wide = refs[:-3], refs[-3], refs[-2], refs[-1]
+    body = feature - tail_width(tok_count, feature)
+    for i, piece in enumerate(pieces):
+        narrow[...] = piece[...].astype(jnp.float32)
+        unpack_rows(narrow, wide, i * tok_count, tok_count, feature)
+        wide[i * tok_count : (i + 1) * tok_count, feature:] = narrow[:tok_count, body:]
+    out_ref[...] = wide[...].astype(jnp.bfloat16)
+
+
+def fetch_kernel(*refs):
+    count = (len(refs) - 1) // 2
+    sems = refs[-1]
+    copies = [
+        pltpu.make_async_copy(refs[i], refs[count + i], sems.at[i]) for i in range(count)
+    ]
+    for c in copies:
+        c.start()
+    for c in copies:
+        c.wait()
 
 
 def expert_kernel(slices, rows_ref, *refs):
@@ -123,55 +220,108 @@
     out_ref[...] = (part * weight).astype(out_ref.dtype)
 
 
-def run_expert(rows, gates, ups, downs):
-    slices = len(gates)
-    feature = downs[0].shape[1]
-    count = rows.shape[0]
-    weight_elements = slices * 3 * gates[0].size
-    return pl.pallas_call(
-        functools.partial(expert_kernel, slices),
-        out_shape=jax.ShapeDtypeStruct((count, feature), jnp.bfloat16),
-        in_specs=[pl.BlockSpec(memory_space=pltpu.VMEM)] * (1 + 3 * slices),
-        out_specs=pl.BlockSpec(memory_space=pltpu.VMEM),
-        compiler_params=pltpu.CompilerParams(vmem_limit_bytes=32 * 1024 * 1024),
-        cost_estimate=pl.CostEstimate(
-            flops=2 * count * weight_elements,
-            bytes_accessed=2 * weight_elements,
-            transcendentals=count * slices * gates[0].shape[1],
-        ),
-    )(rows, *gates, *ups, *downs)
+def combine_kernel(tok_count, parts, *refs):
+    pieces, outs, wide, packed = refs[:parts], refs[parts:-2], refs[-2], refs[-1]
+    total = pieces[0][...].astype(jnp.float32)
+    for piece in pieces[1:]:
+        total = total + piece[...].astype(jnp.float32)
+    wide[...] = total
+    feature = wide.shape[1]
+    for i, out_ref in enumerate(outs):
+        pack_rows(wide, i * tok_count, tok_count, feature, packed)
+        out_ref[...] = packed[...].astype(out_ref.dtype)
+
+
+def finish_kernel(*refs):
+    pieces, out_ref, packed, wide = refs[:-3], refs[-3], refs[-2], refs[-1]
+    total = pieces[0][...].astype(jnp.float32)
+    for piece in pieces[1:]:
+        total = total + piece[...].astype(jnp.float32)
+    packed[...] = total
+    unpack_rows(packed, wide, 0, *wide.shape)
+    out_ref[...] = wide[...].astype(out_ref.dtype)
 
 
 def dense_body(hidden_in, expert_ids, combine, w_gate, w_up, w_down):
     group_count = lax.axis_size("grp")
-    loc_count = lax.axis_size("loc")
-    slices = loc_count // EXP_GRP
+    slices = lax.axis_size("loc") // EXP_GRP
     tok_count = hidden_in.shape[2]
     feature = hidden_in.shape[3]
     top_count = expert_ids.shape[3]
-    token_rows = hidden_in.reshape(tok_count, feature)
-    chosen = expert_ids.reshape(tok_count, top_count)
-    weights = combine.reshape(tok_count, top_count).astype(jnp.float32)
-    lanes = jnp.arange(LANES, dtype=jnp.int32)
-    table = jnp.sum(
-        jnp.where(chosen[:, :, None] == lanes[None, None, :], weights[:, :, None], 0.0), axis=1
-    ).astype(jnp.bfloat16)
-    rows = jnp.concatenate([token_rows, table], axis=1)
-
-    member_steps = [slices * k for k in range(1, EXP_GRP)]
-    group_steps = list(range(1, group_count))
-    slice_steps = list(range(1, slices))
-    gates, ups, downs = (
-        spread(w[0], "loc", loc_count, slice_steps) for w in (w_gate, w_up, w_down)
-    )
-    rows = jnp.concatenate(spread(rows, "loc", loc_count, member_steps), axis=0)
-    partials = [
-        run_expert(block, gates, ups, downs)
-        for block in spread(rows, "grp", group_count, group_steps)
-    ]
-    total = fold(partials, "grp", group_count, group_steps).astype(jnp.bfloat16)
-    chunks = list(total.reshape(EXP_GRP, tok_count, feature))
-    total = fold(chunks, "loc", loc_count, member_steps).astype(jnp.bfloat16)
+    gathered = EXP_GRP * tok_count
+    body = feature - tail_width(tok_count, feature)
+    bf16, f32 = jnp.bfloat16, jnp.float32
+    scratch = pltpu.VMEM
+
+    blocks = (w_gate[0], w_up[0], w_down[0])
+    own = call(
+        prepare_kernel,
+        jax.ShapeDtypeStruct((SUBLANES, body + LANES), bf16),
+        (
+            in_hbm(hidden_in.reshape(tok_count, feature)),
+            in_hbm(expert_ids.reshape(tok_count, 1, top_count)),
+            in_hbm(combine.reshape(tok_count, top_count)),
+        ),
+        [
+            scratch((tok_count, feature), bf16),
+            scratch((tok_count, 1, top_count), jnp.int32),
+            scratch((tok_count, top_count), bf16),
+            scratch((tok_count, feature), f32),
+            scratch((SUBLANES, body + LANES), f32),
+            pltpu.SemaphoreType.DMA((3,)),
+        ],
+        [HBM] * 3,
+    )
+    *blocks, own = lax.optimization_barrier((*blocks, own))
+    pieces = [own] + [swap(own, "loc", slices * k) for k in range(1, EXP_GRP)]
+    others = [[swap(w, "loc", k) for w in blocks] for k in range(1, slices)]
+    size = sum(w.size for w in blocks)
+    kept = call(
+        fetch_kernel,
+        [jax.ShapeDtypeStruct(w.shape, w.dtype) for w in blocks],
+        [in_hbm(w) for w in blocks],
+        [pltpu.SemaphoreType.DMA((len(blocks),))],
+        [HBM] * len(blocks),
+        traffic=2 * size,
+    )
+    pieces, others, kept = lax.optimization_barrier((pieces, others, kept))
+    gates, ups, downs = zip(kept, *others)
+    rows = call(
+        functools.partial(join_kernel, tok_count, feature),
+        jax.ShapeDtypeStruct((gathered, feature + LANES), bf16),
+        pieces,
+        [scratch((SUBLANES, body + LANES), f32), scratch((gathered, feature + LANES), f32)],
+    )
+
+    def run_expert(block):
+        return call(
+            functools.partial(expert_kernel, slices),
+            jax.ShapeDtypeStruct((gathered, feature), bf16),
+            (block, *gates, *ups, *downs),
+            flops=2 * gathered * size * slices,
+            traffic=2 * size * slices,
+        )
+
+    arrived = [swap(rows, "grp", k) for k in range(1, group_count)]
+    parts = [run_expert(rows)]
+    returned = []
+    for k, block in enumerate(arrived, 1):
+        parts.append(run_expert(block))
+        returned.append(swap(parts[-1], "grp", k))
+    packed = jax.ShapeDtypeStruct((SUBLANES, body), bf16)
+    sums = call(
+        functools.partial(combine_kernel, tok_count, group_count),
+        [jax.ShapeDtypeStruct(packed.shape, f32)] + [packed] * (EXP_GRP - 1),
+        (parts[0], *returned),
+        [scratch((gathered, feature), f32), scratch(packed.shape, f32)],
+    )
+    homeward = [swap(s, "loc", slices * k) for k, s in enumerate(sums[1:], 1)]
+    total = call(
+        finish_kernel,
+        jax.ShapeDtypeStruct((tok_count, feature), bf16),
+        (sums[0], *homeward),
+        [scratch(packed.shape, f32), scratch((tok_count, feature), f32)],
+    )
     return total.reshape(1, 1, tok_count, feature)
 
 
@@ -196,7 +346,8 @@
     )
 
     def layer(hidden_in, *others):
-        small = hidden_in.shape[1] * hidden_in.shape[2] <= CAP
+        tokens = hidden_in.shape[1] * hidden_in.shape[2]
+        small = tokens <= CAP and can_pack(*hidden_in.shape[2:])
         body = dense_body if dense_fits and small else packed_body
         return jax.shard_map(
             body, mesh=mesh, in_specs=placed, out_specs=P("loc", "grp", None, None), check_vma=False

time: 48.6 us -> 44 us (0.905)
  local copies, waits for them, and re-layouts: 3.83 us -> 0 us
  Pallas kernels: 4.5 us -> 8.3 us
  starting transfers between devices: 23.5 us -> 21.4 us
  other arithmetic: 1.84 us -> 0 us
    pallas_call x4 -> x9, Pallas kernels: 4.5 us -> 8.3 us  [call(): pl.pallas_call(kernel, out_shape=outs, in_specs=specs or [VMEM] * len(arg...]
    unnamed x19 -> x0, local copies, waits for them, and re-layouts: 3.78 us -> none
    ppermute x15, starting transfers between devices: 23.5 us -> 21.4 us  [swap(): return lax.ppermute(rows, axis, pairs(lax.axis_size(axis), distance))]
    concatenate x2 -> x0, other arithmetic: 0.99 us -> none  [the longest x1 0.9 us: dense_body(): rows = jnp.concatenate([token_rows, table], axis=1)]
    reshape x1 -> x0, other arithmetic: 0.65 us -> none  [dense_body(): return total.reshape(1, 1, tok_count, feature)]
  transfers between devices with their start and end apart: 15 -> 15, of which waited for: 6 -> 6; matrix products, arithmetic and copies ran while one was open for 2% -> 0% of each run, Pallas kernels for 9% -> 14%
where the time goes in v3:
time: 44 us; the launch traced here: 43.8 us
  starting transfers between devices  21.4 us (49%)
  waiting for transfers between devices  14.1 us (32%)
  Pallas kernels  8.3 us (19%)
    ppermute x15, starting transfers between devices, swap(): return lax.ppermute(rows, axis, pairs(lax.axis_size(axis), distance))  21.4 us
    ppermute x15, waiting for transfers between devices, swap(): return lax.ppermute(rows, axis, pairs(lax.axis_size(axis), distance))  14.1 us
    pallas_call x9, Pallas kernels, call(): pl.pallas_call(kernel, out_shape=outs, in_specs=specs or [VMEM] * len(arg...  8.3 us
  transfers between devices with their start and end apart: 15, of which 6 were waited for; matrix products, arithmetic and copies ran while one was open for 0% of the time, Pallas kernels for 14%

profile of v3, /device:TPU:0, one launch (start us, length us, event | category | flops | bytes accessed | tf_op | source)
XLA Modules:
  0.0 43.8 jit_solution(12254508740135992142)
XLA Ops:
  0.0 1.0 %shard_map.64.refs_0_ = bf16[8,2816]{1,0:T(8,128)(2,1)S(1)} custom-call(bf16[6,3584]{1,0:T(8,128)(2,1)} %bitcast.13, s32[6,1,8]{2,1,0:T(1,128)} %bitcast.14, bf16[6,8]{1,0:T(8,128)(2,1)} %bitcast.15), custom_call_target="tpu_custom_call" | custom-call | tf_op jit(solution)/shard_map/pallas_call | solution.py:137
  1.0 0.5 %collective-permute-start.3 = (bf16[3584,128]{1,0:T(8,128)(2,1)}, bf16[3584,128]{1,0:T(8,128)(2,1)S(1)}, u32[]{:S(2)}, u32[]{:S(2)}) collective-permute-start(bf16[3584,128]{1,0:T(8,128)(2,1)} %bitcast.7), channel_id=1, source_target_pairs={{0,1},{1,0},{2,3},{3,2},{4,5},{5,4},{6,7},{7,6},{8,9},{9,8},{10,11... | collective-permute-start | bytes 2752520 | tf_op jit(solution)/shard_map/ppermute | solution.py:90
  1.6 0.1 collective-permute-start.4
  1.6 0.4 collective-permute-start.5
  2.1 2.7 %collective-permute-start = (bf16[8,2816]{1,0:T(8,128)(2,1)S(1)}, bf16[8,2816]{1,0:T(8,128)(2,1)S(1)}, u32[]{:S(2)}, u32[]{:S(2)}) collective-permute-start(bf16[8,2816]{1,0:T(8,128)(2,1)S(1)} %shard_map.64.refs_0_), channel_id=1, source_target_pairs={{0,2},{1,3},{2,0},{3,1},{4,6},{5,7},{6,4},{7,5},{8,10},{9,11},{10,... | collective-permute-start | bytes 135176 | tf_op jit(solution)/shard_map/ppermute | solution.py:90
  4.7 2.6 %collective-permute-start.1 = (bf16[8,2816]{1,0:T(8,128)(2,1)S(1)}, bf16[8,2816]{1,0:T(8,128)(2,1)S(1)}, u32[]{:S(2)}, u32[]{:S(2)}) collective-permute-start(bf16[8,2816]{1,0:T(8,128)(2,1)S(1)} %shard_map.64.refs_0_), channel_id=1, source_target_pairs={{0,4},{1,5},{2,6},{3,7},{4,0},{5,1},{6,2},{7,3},{8,12},{9,13},{10,... | collective-permute-start | bytes 135176 | tf_op jit(solution)/shard_map/ppermute | solution.py:90
  7.3 0.0 collective-permute-done.refs_1_
  7.3 3.5 %collective-permute-start.2 = (bf16[8,2816]{1,0:T(8,128)(2,1)S(1)}, bf16[8,2816]{1,0:T(8,128)(2,1)S(1)}, u32[]{:S(2)}, u32[]{:S(2)}) collective-permute-start(bf16[8,2816]{1,0:T(8,128)(2,1)S(1)} %shard_map.64.refs_0_), channel_id=1, source_target_pairs={{0,6},{1,7},{2,4},{3,5},{4,2},{5,3},{6,0},{7,1},{8,14},{9,15},{10,... | collective-permute-start | bytes 135176 | tf_op jit(solution)/shard_map/ppermute | solution.py:90
  10.8 1.8 %shard_map.65 = (bf16[3584,128]{1,0:T(8,128)(2,1)S(1)}, bf16[3584,128]{1,0:T(8,128)(2,1)S(1)}, bf16[128,3584]{1,0:T(8,128)(2,1)S(1)}) custom-call(bf16[3584,128]{1,0:T(8,128)(2,1)} %bitcast.8, bf16[3584,128]{1,0:T(8,128)(2,1)} %bitcast.10, bf16[128,3584]{1,0:T(8,128)(2,1)} %bitcast.12), custom_call_target="tpu_custom_call" | custom-call | bytes 2752512 | tf_op jit(solution)/shard_map/pallas_call | solution.py:137
  12.6 0.0 collective-permute-done.1.refs_2_
  12.6 0.6 %collective-permute-done.2.refs_3_ = bf16[8,2816]{1,0:T(8,128)(2,1)S(1)} collective-permute-done((bf16[8,2816]{1,0:T(8,128)(2,1)S(1)}, bf16[8,2816]{1,0:T(8,128)(2,1)S(1)}, u32[]{:S(2)}, u32[]{:S(2)}) %collective-permute-start.2) | collective-permute-done | bytes 45088 | tf_op jit(solution)/shard_map/ppermute | solution.py:90
  13.2 0.0 collective-permute-done.3.refs_1_
  13.2 0.0 collective-permute-done.4.refs_3_
  13.2 0.0 collective-permute-done.5.refs_5_
  13.2 0.1 shard_map.66.rows_ref
  13.3 2.5 %collective-permute-start.10 = (bf16[24,3712]{1,0:T(8,128)(2,1)S(1)}, bf16[24,3712]{1,0:T(8,128)(2,1)S(1)}, u32[]{:S(2)}, u32[]{:S(2)}) collective-permute-start(bf16[24,3712]{1,0:T(8,128)(2,1)S(1)} %shard_map.66.rows_ref), channel_id=1, source_target_pairs={{0,24},{8,16},{16,8},{24,0},{1,25},{9,17},{17,9},{25,1},{2,26},{10... | collective-permute-start | bytes 534536 | tf_op jit(solution)/shard_map/ppermute | solution.py:90
  15.8 0.5 %collective-permute-start.8 = (bf16[24,3712]{1,0:T(8,128)(2,1)S(1)}, bf16[24,3712]{1,0:T(8,128)(2,1)S(1)}, u32[]{:S(2)}, u32[]{:S(2)}) collective-permute-start(bf16[24,3712]{1,0:T(8,128)(2,1)S(1)} %shard_map.66.rows_ref), channel_id=1, source_target_pairs={{0,16},{8,24},{16,0},{24,8},{1,17},{9,25},{17,1},{25,9},{2,18},{10... | collective-permute-start | bytes 534536 | tf_op jit(solution)/shard_map/ppermute | solution.py:90
  16.3 0.5 %collective-permute-start.6 = (bf16[24,3712]{1,0:T(8,128)(2,1)S(1)}, bf16[24,3712]{1,0:T(8,128)(2,1)S(1)}, u32[]{:S(2)}, u32[]{:S(2)}) collective-permute-start(bf16[24,3712]{1,0:T(8,128)(2,1)S(1)} %shard_map.66.rows_ref), channel_id=1, source_target_pairs={{0,8},{8,0},{16,24},{24,16},{1,9},{9,1},{17,25},{25,17},{2,10},{10... | collective-permute-start | bytes 534536 | tf_op jit(solution)/shard_map/ppermute | solution.py:90
  16.8 4.5 %collective-permute-done.10.rows_ref = bf16[24,3712]{1,0:T(8,128)(2,1)S(1)} collective-permute-done((bf16[24,3712]{1,0:T(8,128)(2,1)S(1)}, bf16[24,3712]{1,0:T(8,128)(2,1)S(1)}, u32[]{:S(2)}, u32[]{:S(2)}) %collective-permute-start.10) | collective-permute-done | bytes 178208 | tf_op jit(solution)/shard_map/ppermute | solution.py:90
  21.4 1.1 %shard_map.70 = bf16[24,3584]{1,0:T(8,128)(2,1)S(1)} custom-call(bf16[24,3712]{1,0:T(8,128)(2,1)S(1)} %collective-permute-done.10.rows_ref, bf16[3584,128]{1,0:T(8,128)(2,1)S(1)} %get-tuple-element.37.refs_0_, bf16[3584,128]{1,0:T(8,128)(2,1)S(1)} %collective-permute-done.3.refs_1_, bf16[3584,128]{1,0:T(8,128)(2,1)S(1)} %get-tuple-element.39.refs_2_, ...), custom_call_target="tpu_custom_call" | custom-call | flops 132120576 | bytes 5505024 | tf_op jit(solution)/shard_map/pallas_call | solution.py:137
  22.5 2.5 %collective-permute-start.11 = (bf16[24,3584]{1,0:T(8,128)(2,1)S(1)}, bf16[24,3584]{1,0:T(8,128)(2,1)S(1)}, u32[]{:S(2)}, u32[]{:S(2)}) collective-permute-start(bf16[24,3584]{1,0:T(8,128)(2,1)S(1)} %shard_map.70), channel_id=1, source_target_pairs={{0,24},{8,16},{16,8},{24,0},{1,25},{9,17},{17,9},{25,1},{2,26},{10... | collective-permute-start | bytes 516104 | tf_op jit(solution)/shard_map/ppermute | solution.py:90
  25.0 0.0 collective-permute-done.8.rows_ref
  25.0 1.1 %shard_map.69 = bf16[24,3584]{1,0:T(8,128)(2,1)S(1)} custom-call(bf16[24,3712]{1,0:T(8,128)(2,1)S(1)} %collective-permute-done.8.rows_ref, bf16[3584,128]{1,0:T(8,128)(2,1)S(1)} %get-tuple-element.37.refs_0_, bf16[3584,128]{1,0:T(8,128)(2,1)S(1)} %collective-permute-done.3.refs_1_, bf16[3584,128]{1,0:T(8,128)(2,1)S(1)} %get-tuple-element.39.refs_2_, ...), custom_call_target="tpu_custom_call" | custom-call | flops 132120576 | bytes 5505024 | tf_op jit(solution)/shard_map/pallas_call | solution.py:137
  26.2 0.8 %collective-permute-start.9 = (bf16[24,3584]{1,0:T(8,128)(2,1)S(1)}, bf16[24,3584]{1,0:T(8,128)(2,1)S(1)}, u32[]{:S(2)}, u32[]{:S(2)}) collective-permute-start(bf16[24,3584]{1,0:T(8,128)(2,1)S(1)} %shard_map.69), channel_id=1, source_target_pairs={{0,16},{8,24},{16,0},{24,8},{1,17},{9,25},{17,1},{25,9},{2,18},{10... | collective-permute-start | bytes 516104 | tf_op jit(solution)/shard_map/ppermute | solution.py:90
  27.0 0.0 collective-permute-done.6.rows_ref
  27.0 1.1 %shard_map.68 = bf16[24,3584]{1,0:T(8,128)(2,1)S(1)} custom-call(bf16[24,3712]{1,0:T(8,128)(2,1)S(1)} %collective-permute-done.6.rows_ref, bf16[3584,128]{1,0:T(8,128)(2,1)S(1)} %get-tuple-element.37.refs_0_, bf16[3584,128]{1,0:T(8,128)(2,1)S(1)} %collective-permute-done.3.refs_1_, bf16[3584,128]{1,0:T(8,128)(2,1)S(1)} %get-tuple-element.39.refs_2_, ...), custom_call_target="tpu_custom_call" | custom-call | flops 132120576 | bytes 5505024 | tf_op jit(solution)/shard_map/pallas_call | solution.py:137
  28.1 0.3 collective-permute-start.7
  28.4 1.1 %shard_map.67.refs_0_ = bf16[24,3584]{1,0:T(8,128)(2,1)S(1)} custom-call(bf16[24,3712]{1,0:T(8,128)(2,1)S(1)} %shard_map.66.rows_ref, bf16[3584,128]{1,0:T(8,128)(2,1)S(1)} %get-tuple-element.37.refs_0_, bf16[3584,128]{1,0:T(8,128)(2,1)S(1)} %collective-permute-done.3.refs_1_, bf16[3584,128]{1,0:T(8,128)(2,1)S(1)} %get-tuple-element.39.refs_2_, ...), custom_call_target="tpu_custom_call" | custom-call | flops 132120576 | bytes 5505024 | tf_op jit(solution)/shard_map/pallas_call | solution.py:137
  29.5 0.0 collective-permute-done.11.refs_3_
  29.6 2.6 %collective-permute-done.9.refs_2_ = bf16[24,3584]{1,0:T(8,128)(2,1)S(1)} collective-permute-done((bf16[24,3584]{1,0:T(8,128)(2,1)S(1)}, bf16[24,3584]{1,0:T(8,128)(2,1)S(1)}, u32[]{:S(2)}, u32[]{:S(2)}) %collective-permute-start.9) | collective-permute-done | bytes 172064 | tf_op jit(solution)/shard_map/ppermute | solution.py:90
  32.2 1.4 %collective-permute-done.7.refs_1_ = bf16[24,3584]{1,0:T(8,128)(2,1)S(1)} collective-permute-done((bf16[24,3584]{1,0:T(8,128)(2,1)S(1)}, bf16[24,3584]{1,0:T(8,128)(2,1)S(1)}, u32[]{:S(2)}, u32[]{:S(2)}) %collective-permute-start.7) | collective-permute-done | bytes 172064 | tf_op jit(solution)/shard_map/ppermute | solution.py:90
  33.6 0.2 shard_map.71
  33.8 0.1 collective-permute-start.12
  33.9 3.4 %collective-permute-start.13 = (bf16[8,2688]{1,0:T(8,128)(2,1)S(1)}, bf16[8,2688]{1,0:T(8,128)(2,1)S(1)}, u32[]{:S(2)}, u32[]{:S(2)}) collective-permute-start(bf16[8,2688]{1,0:T(8,128)(2,1)S(1)} %get-tuple-element.45), channel_id=1, source_target_pairs={{0,4},{1,5},{2,6},{3,7},{4,0},{5,1},{6,2},{7,3},{8,12},{9,13},{10,... | collective-permute-start | bytes 129032 | tf_op jit(solution)/shard_map/ppermute | solution.py:90
  37.3 0.9 %collective-permute-start.14 = (bf16[8,2688]{1,0:T(8,128)(2,1)S(1)}, bf16[8,2688]{1,0:T(8,128)(2,1)S(1)}, u32[]{:S(2)}, u32[]{:S(2)}) collective-permute-start(bf16[8,2688]{1,0:T(8,128)(2,1)S(1)} %get-tuple-element.46), channel_id=1, source_target_pairs={{0,6},{1,7},{2,4},{3,5},{4,2},{5,3},{6,0},{7,1},{8,14},{9,15},{10,... | collective-permute-start | bytes 129032 | tf_op jit(solution)/shard_map/ppermute | solution.py:90
  38.3 0.0 collective-permute-done.12.refs_1_
  38.3 1.4 %collective-permute-done.13.refs_2_ = bf16[8,2688]{1,0:T(8,128)(2,1)S(1)} collective-permute-done((bf16[8,2688]{1,0:T(8,128)(2,1)S(1)}, bf16[8,2688]{1,0:T(8,128)(2,1)S(1)}, u32[]{:S(2)}, u32[]{:S(2)}) %collective-permute-start.13) | collective-permute-done | bytes 43040 | tf_op jit(solution)/shard_map/ppermute | solution.py:90
  39.6 3.5 %collective-permute-done.14.refs_3_ = bf16[8,2688]{1,0:T(8,128)(2,1)S(1)} collective-permute-done((bf16[8,2688]{1,0:T(8,128)(2,1)S(1)}, bf16[8,2688]{1,0:T(8,128)(2,1)S(1)}, u32[]{:S(2)}, u32[]{:S(2)}) %collective-permute-start.14) | collective-permute-done | bytes 43040 | tf_op jit(solution)/shard_map/ppermute | solution.py:90
  43.2 0.7 %shard_map.72 = bf16[6,3584]{1,0:T(8,128)(2,1)} custom-call(f32[8,2688]{1,0:T(8,128)S(1)} %get-tuple-element.43.refs_0_, bf16[8,2688]{1,0:T(8,128)(2,1)S(1)} %collective-permute-done.12.refs_1_, bf16[8,2688]{1,0:T(8,128)(2,1)S(1)} %collective-permute-done.13.refs_2_, bf16[8,2688]{1,0:T(8,128)(2,1)S(1)} %collective-permute-done.14.refs_3_), custom_call_target="tpu_custom_call" | custom-call | tf_op jit(solution)/shard_map/pallas_call | solution.py:137
Async XLA Ops:
  1.0 12.1 %collective-permute-start.3 = (bf16[3584,128]{1,0:T(8,128)(2,1)}, bf16[3584,128]{1,0:T(8,128)(2,1)S(1)}, u32[]{:S(2)}, u32[]{:S(2)}) collective-permute-start(bf16[3584,128]{1,0:T(8,128)(2,1)} %bitcast.7), channel_id=1, source_target_pairs={{0,1},{1,0},{2,3},{3,2},{4,5},{5,4},{6,7},{7,6},{8,9},{9,8},{10,11... | collective-permute-start | bytes 2752520 | tf_op jit(solution)/shard_map/ppermute | solution.py:90
  1.6 11.6 %collective-permute-start.4 = (bf16[3584,128]{1,0:T(8,128)(2,1)}, bf16[3584,128]{1,0:T(8,128)(2,1)S(1)}, u32[]{:S(2)}, u32[]{:S(2)}) collective-permute-start(bf16[3584,128]{1,0:T(8,128)(2,1)} %bitcast.9), channel_id=1, source_target_pairs={{0,1},{1,0},{2,3},{3,2},{4,5},{5,4},{6,7},{7,6},{8,9},{9,8},{10,11... | collective-permute-start | bytes 2752520 | tf_op jit(solution)/shard_map/ppermute | solution.py:90
  1.6 11.5 %collective-permute-start.5 = (bf16[128,3584]{1,0:T(8,128)(2,1)}, bf16[128,3584]{1,0:T(8,128)(2,1)S(1)}, u32[]{:S(2)}, u32[]{:S(2)}) collective-permute-start(bf16[128,3584]{1,0:T(8,128)(2,1)} %bitcast.11), channel_id=1, source_target_pairs={{0,1},{1,0},{2,3},{3,2},{4,5},{5,4},{6,7},{7,6},{8,9},{9,8},{10,11... | collective-permute-start | bytes 2752520 | tf_op jit(solution)/shard_map/ppermute | solution.py:90
  2.1 5.2 %collective-permute-start = (bf16[8,2816]{1,0:T(8,128)(2,1)S(1)}, bf16[8,2816]{1,0:T(8,128)(2,1)S(1)}, u32[]{:S(2)}, u32[]{:S(2)}) collective-permute-start(bf16[8,2816]{1,0:T(8,128)(2,1)S(1)} %shard_map.64.refs_0_), channel_id=1, source_target_pairs={{0,2},{1,3},{2,0},{3,1},{4,6},{5,7},{6,4},{7,5},{8,10},{9,11},{10,... | collective-permute-start | bytes 135176 | tf_op jit(solution)/shard_map/ppermute | solution.py:90
  4.7 7.8 %collective-permute-start.1 = (bf16[8,2816]{1,0:T(8,128)(2,1)S(1)}, bf16[8,2816]{1,0:T(8,128)(2,1)S(1)}, u32[]{:S(2)}, u32[]{:S(2)}) collective-permute-start(bf16[8,2816]{1,0:T(8,128)(2,1)S(1)} %shard_map.64.refs_0_), channel_id=1, source_target_pairs={{0,4},{1,5},{2,6},{3,7},{4,0},{5,1},{6,2},{7,3},{8,12},{9,13},{10,... | collective-permute-start | bytes 135176 | tf_op jit(solution)/shard_map/ppermute | solution.py:90
  7.3 5.8 %collective-permute-start.2 = (bf16[8,2816]{1,0:T(8,128)(2,1)S(1)}, bf16[8,2816]{1,0:T(8,128)(2,1)S(1)}, u32[]{:S(2)}, u32[]{:S(2)}) collective-permute-start(bf16[8,2816]{1,0:T(8,128)(2,1)S(1)} %shard_map.64.refs_0_), channel_id=1, source_target_pairs={{0,6},{1,7},{2,4},{3,5},{4,2},{5,3},{6,0},{7,1},{8,14},{9,15},{10,... | collective-permute-start | bytes 135176 | tf_op jit(solution)/shard_map/ppermute | solution.py:90
  13.3 8.1 %collective-permute-start.10 = (bf16[24,3712]{1,0:T(8,128)(2,1)S(1)}, bf16[24,3712]{1,0:T(8,128)(2,1)S(1)}, u32[]{:S(2)}, u32[]{:S(2)}) collective-permute-start(bf16[24,3712]{1,0:T(8,128)(2,1)S(1)} %shard_map.66.rows_ref), channel_id=1, source_target_pairs={{0,24},{8,16},{16,8},{24,0},{1,25},{9,17},{17,9},{25,1},{2,26},{10... | collective-permute-start | bytes 534536 | tf_op jit(solution)/shard_map/ppermute | solution.py:90
  15.8 9.2 %collective-permute-start.8 = (bf16[24,3712]{1,0:T(8,128)(2,1)S(1)}, bf16[24,3712]{1,0:T(8,128)(2,1)S(1)}, u32[]{:S(2)}, u32[]{:S(2)}) collective-permute-start(bf16[24,3712]{1,0:T(8,128)(2,1)S(1)} %shard_map.66.rows_ref), channel_id=1, source_target_pairs={{0,16},{8,24},{16,0},{24,8},{1,17},{9,25},{17,1},{25,9},{2,18},{10... | collective-permute-start | bytes 534536 | tf_op jit(solution)/shard_map/ppermute | solution.py:90
  16.3 10.7 %collective-permute-start.6 = (bf16[24,3712]{1,0:T(8,128)(2,1)S(1)}, bf16[24,3712]{1,0:T(8,128)(2,1)S(1)}, u32[]{:S(2)}, u32[]{:S(2)}) collective-permute-start(bf16[24,3712]{1,0:T(8,128)(2,1)S(1)} %shard_map.66.rows_ref), channel_id=1, source_target_pairs={{0,8},{8,0},{16,24},{24,16},{1,9},{9,1},{17,25},{25,17},{2,10},{10... | collective-permute-start | bytes 534536 | tf_op jit(solution)/shard_map/ppermute | solution.py:90
  22.5 7.0 %collective-permute-start.11 = (bf16[24,3584]{1,0:T(8,128)(2,1)S(1)}, bf16[24,3584]{1,0:T(8,128)(2,1)S(1)}, u32[]{:S(2)}, u32[]{:S(2)}) collective-permute-start(bf16[24,3584]{1,0:T(8,128)(2,1)S(1)} %shard_map.70), channel_id=1, source_target_pairs={{0,24},{8,16},{16,8},{24,0},{1,25},{9,17},{17,9},{25,1},{2,26},{10... | collective-permute-start | bytes 516104 | tf_op jit(solution)/shard_map/ppermute | solution.py:90
  26.2 6.0 %collective-permute-start.9 = (bf16[24,3584]{1,0:T(8,128)(2,1)S(1)}, bf16[24,3584]{1,0:T(8,128)(2,1)S(1)}, u32[]{:S(2)}, u32[]{:S(2)}) collective-permute-start(bf16[24,3584]{1,0:T(8,128)(2,1)S(1)} %shard_map.69), channel_id=1, source_target_pairs={{0,16},{8,24},{16,0},{24,8},{1,17},{9,25},{17,1},{25,9},{2,18},{10... | collective-permute-start | bytes 516104 | tf_op jit(solution)/shard_map/ppermute | solution.py:90
  28.1 5.5 %collective-permute-start.7 = (bf16[24,3584]{1,0:T(8,128)(2,1)S(1)}, bf16[24,3584]{1,0:T(8,128)(2,1)S(1)}, u32[]{:S(2)}, u32[]{:S(2)}) collective-permute-start(bf16[24,3584]{1,0:T(8,128)(2,1)S(1)} %shard_map.68), channel_id=1, source_target_pairs={{0,8},{8,0},{16,24},{24,16},{1,9},{9,1},{17,25},{25,17},{2,10},{10... | collective-permute-start | bytes 516104 | tf_op jit(solution)/shard_map/ppermute | solution.py:90
  33.8 4.5 %collective-permute-start.12 = (bf16[8,2688]{1,0:T(8,128)(2,1)S(1)}, bf16[8,2688]{1,0:T(8,128)(2,1)S(1)}, u32[]{:S(2)}, u32[]{:S(2)}) collective-permute-start(bf16[8,2688]{1,0:T(8,128)(2,1)S(1)} %get-tuple-element.44), channel_id=1, source_target_pairs={{0,2},{1,3},{2,0},{3,1},{4,6},{5,7},{6,4},{7,5},{8,10},{9,11},{10,... | collective-permute-start | bytes 129032 | tf_op jit(solution)/shard_map/ppermute | solution.py:90
  33.9 5.8 %collective-permute-start.13 = (bf16[8,2688]{1,0:T(8,128)(2,1)S(1)}, bf16[8,2688]{1,0:T(8,128)(2,1)S(1)}, u32[]{:S(2)}, u32[]{:S(2)}) collective-permute-start(bf16[8,2688]{1,0:T(8,128)(2,1)S(1)} %get-tuple-element.45), channel_id=1, source_target_pairs={{0,4},{1,5},{2,6},{3,7},{4,0},{5,1},{6,2},{7,3},{8,12},{9,13},{10,... | collective-permute-start | bytes 129032 | tf_op jit(solution)/shard_map/ppermute | solution.py:90
  37.3 5.8 %collective-permute-start.14 = (bf16[8,2688]{1,0:T(8,128)(2,1)S(1)}, bf16[8,2688]{1,0:T(8,128)(2,1)S(1)}, u32[]{:S(2)}, u32[]{:S(2)}) collective-permute-start(bf16[8,2688]{1,0:T(8,128)(2,1)S(1)} %get-tuple-element.46), channel_id=1, source_target_pairs={{0,6},{1,7},{2,4},{3,5},{4,2},{5,3},{6,0},{7,1},{8,14},{9,15},{10,... | collective-permute-start | bytes 129032 | tf_op jit(solution)/shard_map/ppermute | solution.py:90

commit v4 on v3

--- a/solution.py
+++ b/solution.py
@@ -90,6 +90,21 @@
     return lax.ppermute(rows, axis, pairs(lax.axis_size(axis), distance))
 
 
+def slide(rows, distance):
+    count = lax.axis_size("loc")
+    return lax.ppermute(rows, "loc", [(i, (i + distance) % count) for i in range(count)])
+
+
+def turn(rows, steps):
+    loc_count = lax.axis_size("loc")
+    moves = [
+        (g * loc_count + l, (g ^ steps[l % len(steps)]) * loc_count + l)
+        for g in range(lax.axis_size("grp"))
+        for l in range(loc_count)
+    ]
+    return lax.ppermute(rows, ("grp", "loc"), moves)
+
+
 def tails_per_row(tok_count):
     return tok_count // (SUBLANES - tok_count)
 
@@ -172,21 +187,25 @@
     out_ref[...] = packed[...].astype(jnp.bfloat16)
 
 
-def join_kernel(tok_count, feature, *refs):
-    pieces, out_ref, narrow, wide = refs[:-3], refs[-3], refs[-2], refs[-1]
-    body = feature - tail_width(tok_count, feature)
-    for i, piece in enumerate(pieces):
-        narrow[...] = piece[...].astype(jnp.float32)
-        unpack_rows(narrow, wide, i * tok_count, tok_count, feature)
-        wide[i * tok_count : (i + 1) * tok_count, feature:] = narrow[:tok_count, body:]
-    out_ref[...] = wide[...].astype(jnp.bfloat16)
-
-
-def fetch_kernel(*refs):
-    count = (len(refs) - 1) // 2
-    sems = refs[-1]
+def join_kernel(*refs):
+    pieces, out_ref = refs[:-1], refs[-1]
+    out_ref[...] = jnp.concatenate([piece[...] for piece in pieces], axis=0)
+
+
+def fetch_kernel(gate_hbm, up_hbm, down_hbm, out_ref, sems):
+    feature, units = gate_hbm.shape
     copies = [
-        pltpu.make_async_copy(refs[i], refs[count + i], sems.at[i]) for i in range(count)
+        (gate_hbm, out_ref.at[:feature]),
+        (up_hbm, out_ref.at[feature : 2 * feature]),
+    ]
+    for i in range(feature // LANES):
+        lowest = 2 * feature + i * units
+        copies.append(
+            (down_hbm.at[:, i * LANES : (i + 1) * LANES], out_ref.at[lowest : lowest + units])
+        )
+    copies = [
+        pltpu.make_async_copy(source, target, sems.at[i])
+        for i, (source, target) in enumerate(copies)
     ]
     for c in copies:
         c.start()
@@ -194,42 +213,52 @@
         c.wait()
 
 
-def expert_kernel(slices, rows_ref, *refs):
-    gates, ups, downs, out_ref = refs[:slices], refs[slices : 2 * slices], refs[2 * slices : -1], refs[-1]
-    feature = out_ref.shape[1]
+def expert_kernel(tok_count, slices, rows_ref, *refs):
+    weights, (out_ref, narrow, wide) = refs[:slices], refs[slices:]
+    units = LANES
+    feature = wide.shape[1] - LANES
+    body = feature - tail_width(tok_count, feature)
     own_expert = lax.axis_index("grp") * EXP_GRP + lax.axis_index("loc") // slices
-    features = rows_ref[:, :feature]
-    table = rows_ref[:, feature:].astype(jnp.float32)
+    for i in range(EXP_GRP):
+        narrow[...] = rows_ref[i * SUBLANES : (i + 1) * SUBLANES, :].astype(jnp.float32)
+        unpack_rows(narrow, wide, i * tok_count, tok_count, feature)
+        wide[i * tok_count : (i + 1) * tok_count, feature:] = narrow[:tok_count, body:]
+    features = wide[:, :feature].astype(jnp.bfloat16)
+    table = wide[:, feature:]
     lanes = lax.broadcasted_iota(jnp.int32, table.shape, 1)
     weight = jnp.sum(jnp.where(lanes == own_expert, table, 0.0), axis=1, keepdims=True)
-    hidden = []
-    for gate_ref, up_ref in zip(gates, ups):
-        units = gate_ref.shape[1]
+    hidden, downs = [], []
+    for w in weights:
         both = jnp.dot(
             features,
-            jnp.concatenate([gate_ref[...], up_ref[...]], axis=1),
+            jnp.concatenate([w[:feature], w[feature : 2 * feature]], axis=1),
             preferred_element_type=jnp.float32,
         )
         gate_out, up_out = both[:, :units], both[:, units:]
         hidden.append((gate_out / (1.0 + jnp.exp(-gate_out)) * up_out).astype(jnp.bfloat16))
+        blocks = [
+            w[2 * feature + i * units : 2 * feature + (i + 1) * units]
+            for i in range(feature // LANES)
+        ]
+        downs.append(jnp.concatenate(blocks, axis=1))
     part = jnp.dot(
         jnp.concatenate(hidden, axis=1),
-        jnp.concatenate([d[...] for d in downs], axis=0),
+        jnp.concatenate(downs, axis=0),
         preferred_element_type=jnp.float32,
     )
-    out_ref[...] = (part * weight).astype(out_ref.dtype)
-
-
-def combine_kernel(tok_count, parts, *refs):
-    pieces, outs, wide, packed = refs[:parts], refs[parts:-2], refs[-2], refs[-1]
+    wide[:, :feature] = part * weight
+    for i in range(EXP_GRP):
+        pack_rows(wide, i * tok_count, tok_count, feature, narrow)
+        out_ref[i * SUBLANES : (i + 1) * SUBLANES, :] = narrow[:, :body].astype(out_ref.dtype)
+
+
+def combine_kernel(*refs):
+    pieces, outs = refs[:EXP_GRP], refs[EXP_GRP:]
     total = pieces[0][...].astype(jnp.float32)
     for piece in pieces[1:]:
         total = total + piece[...].astype(jnp.float32)
-    wide[...] = total
-    feature = wide.shape[1]
     for i, out_ref in enumerate(outs):
-        pack_rows(wide, i * tok_count, tok_count, feature, packed)
-        out_ref[...] = packed[...].astype(out_ref.dtype)
+        out_ref[...] = total[i * SUBLANES : (i + 1) * SUBLANES].astype(out_ref.dtype)
 
 
 def finish_kernel(*refs):
@@ -243,7 +272,6 @@
 
 
 def dense_body(hidden_in, expert_ids, combine, w_gate, w_up, w_down):
-    group_count = lax.axis_size("grp")
     slices = lax.axis_size("loc") // EXP_GRP
     tok_count = hidden_in.shape[2]
     feature = hidden_in.shape[3]
@@ -272,55 +300,54 @@
         ],
         [HBM] * 3,
     )
-    *blocks, own = lax.optimization_barrier((*blocks, own))
-    pieces = [own] + [swap(own, "loc", slices * k) for k in range(1, EXP_GRP)]
-    others = [[swap(w, "loc", k) for w in blocks] for k in range(1, slices)]
+    steps = range(1, EXP_GRP)
+    pieces = [own] + [slide(own, slices * k) for k in steps]
+    *blocks, pieces[0] = lax.optimization_barrier((*blocks, pieces[0]))
     size = sum(w.size for w in blocks)
     kept = call(
         fetch_kernel,
-        [jax.ShapeDtypeStruct(w.shape, w.dtype) for w in blocks],
+        jax.ShapeDtypeStruct((3 * feature, LANES), bf16),
         [in_hbm(w) for w in blocks],
-        [pltpu.SemaphoreType.DMA((len(blocks),))],
-        [HBM] * len(blocks),
+        [pltpu.SemaphoreType.DMA((2 + feature // LANES,))],
+        [HBM] * 3,
         traffic=2 * size,
     )
-    pieces, others, kept = lax.optimization_barrier((pieces, others, kept))
-    gates, ups, downs = zip(kept, *others)
-    rows = call(
-        functools.partial(join_kernel, tok_count, feature),
-        jax.ShapeDtypeStruct((gathered, feature + LANES), bf16),
-        pieces,
-        [scratch((SUBLANES, body + LANES), f32), scratch((gathered, feature + LANES), f32)],
-    )
-
-    def run_expert(block):
+    kept, pieces = lax.optimization_barrier((kept, pieces))
+    weights = [kept] + [swap(kept, "loc", k) for k in range(1, slices)]
+
+    def run_expert(rows, dtype):
         return call(
-            functools.partial(expert_kernel, slices),
-            jax.ShapeDtypeStruct((gathered, feature), bf16),
-            (block, *gates, *ups, *downs),
+            functools.partial(expert_kernel, tok_count, slices),
+            jax.ShapeDtypeStruct((EXP_GRP * SUBLANES, body), dtype),
+            (rows, *weights),
+            [scratch((SUBLANES, body + LANES), f32), scratch((gathered, feature + LANES), f32)],
             flops=2 * gathered * size * slices,
             traffic=2 * size * slices,
         )
 
-    arrived = [swap(rows, "grp", k) for k in range(1, group_count)]
-    parts = [run_expert(rows)]
-    returned = []
-    for k, block in enumerate(arrived, 1):
-        parts.append(run_expert(block))
-        returned.append(swap(parts[-1], "grp", k))
-    packed = jax.ShapeDtypeStruct((SUBLANES, body), bf16)
+    rows = call(
+        join_kernel, jax.ShapeDtypeStruct((EXP_GRP * SUBLANES, body + LANES), bf16), pieces
+    )
+    first, second = [1 + i % 2 for i in range(slices)], [2 - i % 2 for i in range(slices)]
+    beside, above = turn(rows, first), turn(rows, second)
+    across = turn(beside, second)
+    returned = (
+        turn(run_expert(beside, bf16), first),
+        turn(run_expert(above, bf16), second),
+        swap(run_expert(across, bf16), "grp", 3),
+    )
+    packed = (SUBLANES, body)
     sums = call(
-        functools.partial(combine_kernel, tok_count, group_count),
-        [jax.ShapeDtypeStruct(packed.shape, f32)] + [packed] * (EXP_GRP - 1),
-        (parts[0], *returned),
-        [scratch((gathered, feature), f32), scratch(packed.shape, f32)],
-    )
-    homeward = [swap(s, "loc", slices * k) for k, s in enumerate(sums[1:], 1)]
+        combine_kernel,
+        [jax.ShapeDtypeStruct(packed, f32)] + [jax.ShapeDtypeStruct(packed, bf16)] * len(steps),
+        (run_expert(rows, f32), *returned),
+    )
+    homeward = [slide(sums[k], -slices * k) for k in steps]
     total = call(
         finish_kernel,
         jax.ShapeDtypeStruct((tok_count, feature), bf16),
         (sums[0], *homeward),
-        [scratch(packed.shape, f32), scratch((tok_count, feature), f32)],
+        [scratch(packed, f32), scratch((tok_count, feature), f32)],
     )
     return total.reshape(1, 1, tok_count, feature)
 
@@ -339,15 +366,12 @@
         P(("grp", "loc"), None, None),
         P(("grp", "loc"), None, None),
     )
-    dense_fits = (
-        power_of_two(group_count)
-        and power_of_two(loc_count)
-        and group_count * EXP_GRP <= LANES
-    )
+    dense_fits = group_count == EXP_GRP == 4 and power_of_two(loc_count)
 
     def layer(hidden_in, *others):
         tokens = hidden_in.shape[1] * hidden_in.shape[2]
-        small = tokens <= CAP and can_pack(*hidden_in.shape[2:])
+        units = others[2].shape[2]
+        small = tokens <= CAP and units == LANES and can_pack(*hidden_in.shape[2:])
         body = dense_body if dense_fits and small else packed_body
         return jax.shard_map(
             body, mesh=mesh, in_specs=placed, out_specs=P("loc", "grp", None, None), check_vma=False

time: 44 us -> 42 us (0.955)
  starting transfers between devices: 21.4 us -> 18.9 us
    ppermute x15 -> x2, starting transfers between devices: 21.4 us -> 2.88 us  [swap(): return lax.ppermute(rows, axis, pairs(lax.axis_size(axis), distance))]
    ppermute x0 -> x11, starting transfers between devices: none -> 16.1 us  [the longest x6 9.31 us: slide(): lax.ppermute(rows, 'loc', [(i, (i + distance) % count) for i in range(cou...]
    ppermute x0 -> x11, waiting for transfers between devices: none -> 14.3 us  [the longest x5 7.45 us: turn(): return lax.ppermute(rows, ('grp', 'loc'), moves)]
    ppermute x15 -> x2, waiting for transfers between devices: 14.1 us -> 0.01 us  [swap(): return lax.ppermute(rows, axis, pairs(lax.axis_size(axis), distance))]
  transfers between devices with their start and end apart: 15 -> 13, of which waited for: 6 -> 8; matrix products, arithmetic and copies ran while one was open for 0% -> 0% of each run, Pallas kernels for 14% -> 16%
where the time goes in v4:
time: 42 us; the launch traced here: 41.8 us
  starting transfers between devices  18.9 us (45%)
  waiting for transfers between devices  14.3 us (34%)
  Pallas kernels  8.49 us (20%)
    ppermute x6, starting transfers between devices, slide(): lax.ppermute(rows, 'loc', [(i, (i + distance) % count) for i in range(cou...  9.31 us
    pallas_call x9, Pallas kernels, call(): pl.pallas_call(kernel, out_shape=outs, in_specs=specs or [VMEM] * len(arg...  8.49 us
    ppermute x5, waiting for transfers between devices, turn(): return lax.ppermute(rows, ('grp', 'loc'), moves)  7.45 us
    ppermute x6, waiting for transfers between devices, slide(): lax.ppermute(rows, 'loc', [(i, (i + distance) % count) for i in range(cou...  6.8 us
    ppermute x5, starting transfers between devices, turn(): return lax.ppermute(rows, ('grp', 'loc'), moves)  6.75 us
    ppermute x2, starting transfers between devices, swap(): return lax.ppermute(rows, axis, pairs(lax.axis_size(axis), distance))  2.88 us
  transfers between devices with their start and end apart: 13, of which 8 were waited for; matrix products, arithmetic and copies ran while one was open for 0% of the time, Pallas kernels for 16%

profile of v4, /device:TPU:0, one launch (start us, length us, event | category | flops | bytes accessed | tf_op | source)
XLA Modules:
  0.0 41.8 jit_solution(4308496838333367107)
XLA Ops:
  0.0 1.0 %shard_map.64.refs_0_ = bf16[8,2816]{1,0:T(8,128)(2,1)S(1)} custom-call(bf16[6,3584]{1,0:T(8,128)(2,1)} %bitcast.10, s32[6,1,8]{2,1,0:T(1,128)} %bitcast.11, bf16[6,8]{1,0:T(8,128)(2,1)} %bitcast.12), custom_call_target="tpu_custom_call" | custom-call | tf_op jit(solution)/shard_map/pallas_call | solution.py:152
  1.0 5.1 %collective-permute-start.2 = (bf16[8,2816]{1,0:T(8,128)(2,1)S(1)}, bf16[8,2816]{1,0:T(8,128)(2,1)S(1)}, u32[]{:S(2)}, u32[]{:S(2)}) collective-permute-start(bf16[8,2816]{1,0:T(8,128)(2,1)S(1)} %shard_map.64.refs_0_), channel_id=1, source_target_pairs={{0,6},{1,7},{2,0},{3,1},{4,2},{5,3},{6,4},{7,5},{8,14},{9,15},{10,... | collective-permute-start | bytes 135176 | tf_op jit(solution)/shard_map/ppermute | solution.py:95
  6.1 0.0 collective-permute-start.1
  6.1 1.0 %collective-permute-start = (bf16[8,2816]{1,0:T(8,128)(2,1)S(1)}, bf16[8,2816]{1,0:T(8,128)(2,1)S(1)}, u32[]{:S(2)}, u32[]{:S(2)}) collective-permute-start(bf16[8,2816]{1,0:T(8,128)(2,1)S(1)} %shard_map.64.refs_0_), channel_id=1, source_target_pairs={{0,2},{1,3},{2,4},{3,5},{4,6},{5,7},{6,0},{7,1},{8,10},{9,11},{10,... | collective-permute-start | bytes 135176 | tf_op jit(solution)/shard_map/ppermute | solution.py:95
  7.2 1.9 %shard_map.65.refs_0_ = bf16[10752,128]{1,0:T(8,128)(2,1)S(1)} custom-call(bf16[3584,128]{1,0:T(8,128)(2,1)} %bitcast.7, bf16[3584,128]{1,0:T(8,128)(2,1)} %bitcast.8, bf16[128,3584]{1,0:T(8,128)(2,1)} %bitcast.9), custom_call_target="tpu_custom_call" | custom-call | bytes 2752512 | tf_op jit(solution)/shard_map/pallas_call | solution.py:152
  9.1 0.0 collective-permute-done.2.refs_3_
  9.1 2.0 %collective-permute-done.1.refs_2_ = bf16[8,2816]{1,0:T(8,128)(2,1)S(1)} collective-permute-done((bf16[8,2816]{1,0:T(8,128)(2,1)S(1)}, bf16[8,2816]{1,0:T(8,128)(2,1)S(1)}, u32[]{:S(2)}, u32[]{:S(2)}) %collective-permute-start.1) | collective-permute-done | bytes 45088 | tf_op jit(solution)/shard_map/ppermute | solution.py:95
  11.1 0.9 %collective-permute-done.refs_1_ = bf16[8,2816]{1,0:T(8,128)(2,1)S(1)} collective-permute-done((bf16[8,2816]{1,0:T(8,128)(2,1)S(1)}, bf16[8,2816]{1,0:T(8,128)(2,1)S(1)}, u32[]{:S(2)}, u32[]{:S(2)}) %collective-permute-start) | collective-permute-done | bytes 45088 | tf_op jit(solution)/shard_map/ppermute | solution.py:95
  12.0 0.0 collective-permute-start.3
  12.0 1.6 %collective-permute-start.4 = (bf16[32,2816]{1,0:T(8,128)(2,1)S(1)}, bf16[32,2816]{1,0:T(8,128)(2,1)S(1)}, u32[]{:S(2)}, u32[]{:S(2)}) collective-permute-start(bf16[32,2816]{1,0:T(8,128)(2,1)S(1)} %shard_map.66.rows_ref), channel_id=1, source_target_pairs={{0,8},{1,17},{2,10},{3,19},{4,12},{5,21},{6,14},{7,23},{8,0},{9,25... | collective-permute-start | bytes 540680 | tf_op jit(solution)/shard_map/ppermute | solution.py:105
  13.6 1.5 %collective-permute-start.6 = (bf16[32,2816]{1,0:T(8,128)(2,1)S(1)}, bf16[32,2816]{1,0:T(8,128)(2,1)S(1)}, u32[]{:S(2)}, u32[]{:S(2)}) collective-permute-start(bf16[32,2816]{1,0:T(8,128)(2,1)S(1)} %shard_map.66.rows_ref), channel_id=1, source_target_pairs={{0,16},{1,9},{2,18},{3,11},{4,20},{5,13},{6,22},{7,15},{8,24},{9,1... | collective-permute-start | bytes 540680 | tf_op jit(solution)/shard_map/ppermute | solution.py:105
  15.1 3.7 %collective-permute-done.4.rows_ref = bf16[32,2816]{1,0:T(8,128)(2,1)S(1)} collective-permute-done((bf16[32,2816]{1,0:T(8,128)(2,1)S(1)}, bf16[32,2816]{1,0:T(8,128)(2,1)S(1)}, u32[]{:S(2)}, u32[]{:S(2)}) %collective-permute-start.4) | collective-permute-done | bytes 180256 | tf_op jit(solution)/shard_map/ppermute | solution.py:105
  18.8 2.0 %collective-permute-start.8 = (bf16[32,2816]{1,0:T(8,128)(2,1)S(1)}, bf16[32,2816]{1,0:T(8,128)(2,1)S(1)}, u32[]{:S(2)}, u32[]{:S(2)}) collective-permute-start(bf16[32,2816]{1,0:T(8,128)(2,1)S(1)} %collective-permute-done.4.rows_ref), channel_id=1, source_target_pairs={{0,16},{1,9},{2,18},{3,11},{4,20},{5,13},{6,22},{7,15},{8,24},{9,1... | collective-permute-start | bytes 540680 | tf_op jit(solution)/shard_map/ppermute | solution.py:105
  20.8 0.0 collective-permute-done.3.refs_1_
  20.8 1.2 %shard_map.68 = bf16[32,2688]{1,0:T(8,128)(2,1)S(1)} custom-call(bf16[32,2816]{1,0:T(8,128)(2,1)S(1)} %collective-permute-done.4.rows_ref, bf16[10752,128]{1,0:T(8,128)(2,1)S(1)} %shard_map.65.refs_0_, bf16[10752,128]{1,0:T(8,128)(2,1)S(1)} %collective-permute-done.3.refs_1_), custom_call_target="tpu_custom_call" | custom-call | flops 132120576 | bytes 5505024 | tf_op jit(solution)/shard_map/pallas_call | solution.py:152
  22.0 1.6 %collective-permute-start.5 = (bf16[32,2688]{1,0:T(8,128)(2,1)S(1)}, bf16[32,2688]{1,0:T(8,128)(2,1)S(1)}, u32[]{:S(2)}, u32[]{:S(2)}) collective-permute-start(bf16[32,2688]{1,0:T(8,128)(2,1)S(1)} %shard_map.68), channel_id=1, source_target_pairs={{0,8},{1,17},{2,10},{3,19},{4,12},{5,21},{6,14},{7,23},{8,0},{9,25... | collective-permute-start | bytes 516104 | tf_op jit(solution)/shard_map/ppermute | solution.py:105
  23.6 0.0 collective-permute-done.6.rows_ref
  23.6 1.2 %shard_map.69 = bf16[32,2688]{1,0:T(8,128)(2,1)S(1)} custom-call(bf16[32,2816]{1,0:T(8,128)(2,1)S(1)} %collective-permute-done.6.rows_ref, bf16[10752,128]{1,0:T(8,128)(2,1)S(1)} %shard_map.65.refs_0_, bf16[10752,128]{1,0:T(8,128)(2,1)S(1)} %collective-permute-done.3.refs_1_), custom_call_target="tpu_custom_call" | custom-call | flops 132120576 | bytes 5505024 | tf_op jit(solution)/shard_map/pallas_call | solution.py:152
  24.8 0.1 collective-permute-start.7
  24.9 0.6 %collective-permute-done.8.rows_ref = bf16[32,2816]{1,0:T(8,128)(2,1)S(1)} collective-permute-done((bf16[32,2816]{1,0:T(8,128)(2,1)S(1)}, bf16[32,2816]{1,0:T(8,128)(2,1)S(1)}, u32[]{:S(2)}, u32[]{:S(2)}) %collective-permute-start.8) | collective-permute-done | bytes 180256 | tf_op jit(solution)/shard_map/ppermute | solution.py:105
  25.4 1.2 %shard_map.70 = bf16[32,2688]{1,0:T(8,128)(2,1)S(1)} custom-call(bf16[32,2816]{1,0:T(8,128)(2,1)S(1)} %collective-permute-done.8.rows_ref, bf16[10752,128]{1,0:T(8,128)(2,1)S(1)} %shard_map.65.refs_0_, bf16[10752,128]{1,0:T(8,128)(2,1)S(1)} %collective-permute-done.3.refs_1_), custom_call_target="tpu_custom_call" | custom-call | flops 132120576 | bytes 5505024 | tf_op jit(solution)/shard_map/pallas_call | solution.py:152
  26.6 2.9 %collective-permute-start.9 = (bf16[32,2688]{1,0:T(8,128)(2,1)S(1)}, bf16[32,2688]{1,0:T(8,128)(2,1)S(1)}, u32[]{:S(2)}, u32[]{:S(2)}) collective-permute-start(bf16[32,2688]{1,0:T(8,128)(2,1)S(1)} %shard_map.70), channel_id=1, source_target_pairs={{0,24},{8,16},{16,8},{24,0},{1,25},{9,17},{17,9},{25,1},{2,26},{10... | collective-permute-start | bytes 516104 | tf_op jit(solution)/shard_map/ppermute | solution.py:90
  29.5 1.2 %shard_map.67.refs_0_ = f32[32,2688]{1,0:T(8,128)S(1)} custom-call(bf16[32,2816]{1,0:T(8,128)(2,1)S(1)} %shard_map.66.rows_ref, bf16[10752,128]{1,0:T(8,128)(2,1)S(1)} %shard_map.65.refs_0_, bf16[10752,128]{1,0:T(8,128)(2,1)S(1)} %collective-permute-done.3.refs_1_), custom_call_target="tpu_custom_call" | custom-call | flops 132120576 | bytes 5505024 | tf_op jit(solution)/shard_map/pallas_call | solution.py:152
  30.7 0.0 collective-permute-done.5.refs_1_
  30.7 3.2 %collective-permute-done.7.refs_2_ = bf16[32,2688]{1,0:T(8,128)(2,1)S(1)} collective-permute-done((bf16[32,2688]{1,0:T(8,128)(2,1)S(1)}, bf16[32,2688]{1,0:T(8,128)(2,1)S(1)}, u32[]{:S(2)}, u32[]{:S(2)}) %collective-permute-start.7) | collective-permute-done | bytes 172064 | tf_op jit(solution)/shard_map/ppermute | solution.py:105
  33.9 0.0 collective-permute-done.9.refs_3_
  33.9 0.1 shard_map.71
  34.0 1.0 %collective-permute-start.10 = (bf16[8,2688]{1,0:T(8,128)(2,1)S(1)}, bf16[8,2688]{1,0:T(8,128)(2,1)S(1)}, u32[]{:S(2)}, u32[]{:S(2)}) collective-permute-start(bf16[8,2688]{1,0:T(8,128)(2,1)S(1)} %get-tuple-element.28), channel_id=1, source_target_pairs={{0,6},{1,7},{2,0},{3,1},{4,2},{5,3},{6,4},{7,5},{8,14},{9,15},{10,... | collective-permute-start | bytes 129032 | tf_op jit(solution)/shard_map/ppermute | solution.py:95
  35.0 0.3 collective-permute-start.11
  35.3 1.9 %collective-permute-start.12 = (bf16[8,2688]{1,0:T(8,128)(2,1)S(1)}, bf16[8,2688]{1,0:T(8,128)(2,1)S(1)}, u32[]{:S(2)}, u32[]{:S(2)}) collective-permute-start(bf16[8,2688]{1,0:T(8,128)(2,1)S(1)} %get-tuple-element.30), channel_id=1, source_target_pairs={{0,2},{1,3},{2,4},{3,5},{4,6},{5,7},{6,0},{7,1},{8,10},{9,11},{10,... | collective-permute-start | bytes 129032 | tf_op jit(solution)/shard_map/ppermute | solution.py:95
  37.2 0.9 %collective-permute-done.10.refs_1_ = bf16[8,2688]{1,0:T(8,128)(2,1)S(1)} collective-permute-done((bf16[8,2688]{1,0:T(8,128)(2,1)S(1)}, bf16[8,2688]{1,0:T(8,128)(2,1)S(1)}, u32[]{:S(2)}, u32[]{:S(2)}) %collective-permute-start.10) | collective-permute-done | bytes 43040 | tf_op jit(solution)/shard_map/ppermute | solution.py:95
  38.1 1.8 %collective-permute-done.11.refs_2_ = bf16[8,2688]{1,0:T(8,128)(2,1)S(1)} collective-permute-done((bf16[8,2688]{1,0:T(8,128)(2,1)S(1)}, bf16[8,2688]{1,0:T(8,128)(2,1)S(1)}, u32[]{:S(2)}, u32[]{:S(2)}) %collective-permute-start.11) | collective-permute-done | bytes 43040 | tf_op jit(solution)/shard_map/ppermute | solution.py:95
  39.9 1.2 %collective-permute-done.12.refs_3_ = bf16[8,2688]{1,0:T(8,128)(2,1)S(1)} collective-permute-done((bf16[8,2688]{1,0:T(8,128)(2,1)S(1)}, bf16[8,2688]{1,0:T(8,128)(2,1)S(1)}, u32[]{:S(2)}, u32[]{:S(2)}) %collective-permute-start.12) | collective-permute-done | bytes 43040 | tf_op jit(solution)/shard_map/ppermute | solution.py:95
  41.1 0.7 %shard_map.72 = bf16[6,3584]{1,0:T(8,128)(2,1)} custom-call(f32[8,2688]{1,0:T(8,128)S(1)} %get-tuple-element.27.refs_0_, bf16[8,2688]{1,0:T(8,128)(2,1)S(1)} %collective-permute-done.10.refs_1_, bf16[8,2688]{1,0:T(8,128)(2,1)S(1)} %collective-permute-done.11.refs_2_, bf16[8,2688]{1,0:T(8,128)(2,1)S(1)} %collective-permute-done.12.refs_3_), custom_call_target="tpu_custom_call" | custom-call | tf_op jit(solution)/shard_map/pallas_call | solution.py:152
  (1 shorter events, 0.0 us)
Async XLA Ops:
  1.0 8.0 %collective-permute-start.2 = (bf16[8,2816]{1,0:T(8,128)(2,1)S(1)}, bf16[8,2816]{1,0:T(8,128)(2,1)S(1)}, u32[]{:S(2)}, u32[]{:S(2)}) collective-permute-start(bf16[8,2816]{1,0:T(8,128)(2,1)S(1)} %shard_map.64.refs_0_), channel_id=1, source_target_pairs={{0,6},{1,7},{2,0},{3,1},{4,2},{5,3},{6,4},{7,5},{8,14},{9,15},{10,... | collective-permute-start | bytes 135176 | tf_op jit(solution)/shard_map/ppermute | solution.py:95
  6.1 4.9 %collective-permute-start.1 = (bf16[8,2816]{1,0:T(8,128)(2,1)S(1)}, bf16[8,2816]{1,0:T(8,128)(2,1)S(1)}, u32[]{:S(2)}, u32[]{:S(2)}) collective-permute-start(bf16[8,2816]{1,0:T(8,128)(2,1)S(1)} %shard_map.64.refs_0_), channel_id=1, source_target_pairs={{0,4},{1,5},{2,6},{3,7},{4,0},{5,1},{6,2},{7,3},{8,12},{9,13},{10,... | collective-permute-start | bytes 135176 | tf_op jit(solution)/shard_map/ppermute | solution.py:95
  6.1 5.8 %collective-permute-start = (bf16[8,2816]{1,0:T(8,128)(2,1)S(1)}, bf16[8,2816]{1,0:T(8,128)(2,1)S(1)}, u32[]{:S(2)}, u32[]{:S(2)}) collective-permute-start(bf16[8,2816]{1,0:T(8,128)(2,1)S(1)} %shard_map.64.refs_0_), channel_id=1, source_target_pairs={{0,2},{1,3},{2,4},{3,5},{4,6},{5,7},{6,0},{7,1},{8,10},{9,11},{10,... | collective-permute-start | bytes 135176 | tf_op jit(solution)/shard_map/ppermute | solution.py:95
  12.0 8.8 %collective-permute-start.3 = (bf16[10752,128]{1,0:T(8,128)(2,1)S(1)}, bf16[10752,128]{1,0:T(8,128)(2,1)S(1)}, u32[]{:S(2)}, u32[]{:S(2)}) collective-permute-start(bf16[10752,128]{1,0:T(8,128)(2,1)S(1)} %shard_map.65.refs_0_), channel_id=1, source_target_pairs={{0,1},{1,0},{2,3},{3,2},{4,5},{5,4},{6,7},{7,6},{8,9},{9,8},{10,11... | collective-permute-start | bytes 8257544 | tf_op jit(solution)/shard_map/ppermute | solution.py:90
  12.0 6.7 %collective-permute-start.4 = (bf16[32,2816]{1,0:T(8,128)(2,1)S(1)}, bf16[32,2816]{1,0:T(8,128)(2,1)S(1)}, u32[]{:S(2)}, u32[]{:S(2)}) collective-permute-start(bf16[32,2816]{1,0:T(8,128)(2,1)S(1)} %shard_map.66.rows_ref), channel_id=1, source_target_pairs={{0,8},{1,17},{2,10},{3,19},{4,12},{5,21},{6,14},{7,23},{8,0},{9,25... | collective-permute-start | bytes 540680 | tf_op jit(solution)/shard_map/ppermute | solution.py:105
  13.6 10.0 %collective-permute-start.6 = (bf16[32,2816]{1,0:T(8,128)(2,1)S(1)}, bf16[32,2816]{1,0:T(8,128)(2,1)S(1)}, u32[]{:S(2)}, u32[]{:S(2)}) collective-permute-start(bf16[32,2816]{1,0:T(8,128)(2,1)S(1)} %shard_map.66.rows_ref), channel_id=1, source_target_pairs={{0,16},{1,9},{2,18},{3,11},{4,20},{5,13},{6,22},{7,15},{8,24},{9,1... | collective-permute-start | bytes 540680 | tf_op jit(solution)/shard_map/ppermute | solution.py:105
  18.8 6.7 %collective-permute-start.8 = (bf16[32,2816]{1,0:T(8,128)(2,1)S(1)}, bf16[32,2816]{1,0:T(8,128)(2,1)S(1)}, u32[]{:S(2)}, u32[]{:S(2)}) collective-permute-start(bf16[32,2816]{1,0:T(8,128)(2,1)S(1)} %collective-permute-done.4.rows_ref), channel_id=1, source_target_pairs={{0,16},{1,9},{2,18},{3,11},{4,20},{5,13},{6,22},{7,15},{8,24},{9,1... | collective-permute-start | bytes 540680 | tf_op jit(solution)/shard_map/ppermute | solution.py:105
  22.0 8.7 %collective-permute-start.5 = (bf16[32,2688]{1,0:T(8,128)(2,1)S(1)}, bf16[32,2688]{1,0:T(8,128)(2,1)S(1)}, u32[]{:S(2)}, u32[]{:S(2)}) collective-permute-start(bf16[32,2688]{1,0:T(8,128)(2,1)S(1)} %shard_map.68), channel_id=1, source_target_pairs={{0,8},{1,17},{2,10},{3,19},{4,12},{5,21},{6,14},{7,23},{8,0},{9,25... | collective-permute-start | bytes 516104 | tf_op jit(solution)/shard_map/ppermute | solution.py:105
  24.8 9.2 %collective-permute-start.7 = (bf16[32,2688]{1,0:T(8,128)(2,1)S(1)}, bf16[32,2688]{1,0:T(8,128)(2,1)S(1)}, u32[]{:S(2)}, u32[]{:S(2)}) collective-permute-start(bf16[32,2688]{1,0:T(8,128)(2,1)S(1)} %shard_map.69), channel_id=1, source_target_pairs={{0,16},{1,9},{2,18},{3,11},{4,20},{5,13},{6,22},{7,15},{8,24},{9,1... | collective-permute-start | bytes 516104 | tf_op jit(solution)/shard_map/ppermute | solution.py:105
  26.6 7.3 %collective-permute-start.9 = (bf16[32,2688]{1,0:T(8,128)(2,1)S(1)}, bf16[32,2688]{1,0:T(8,128)(2,1)S(1)}, u32[]{:S(2)}, u32[]{:S(2)}) collective-permute-start(bf16[32,2688]{1,0:T(8,128)(2,1)S(1)} %shard_map.70), channel_id=1, source_target_pairs={{0,24},{8,16},{16,8},{24,0},{1,25},{9,17},{17,9},{25,1},{2,26},{10... | collective-permute-start | bytes 516104 | tf_op jit(solution)/shard_map/ppermute | solution.py:90
  34.0 4.1 %collective-permute-start.10 = (bf16[8,2688]{1,0:T(8,128)(2,1)S(1)}, bf16[8,2688]{1,0:T(8,128)(2,1)S(1)}, u32[]{:S(2)}, u32[]{:S(2)}) collective-permute-start(bf16[8,2688]{1,0:T(8,128)(2,1)S(1)} %get-tuple-element.28), channel_id=1, source_target_pairs={{0,6},{1,7},{2,0},{3,1},{4,2},{5,3},{6,4},{7,5},{8,14},{9,15},{10,... | collective-permute-start | bytes 129032 | tf_op jit(solution)/shard_map/ppermute | solution.py:95
  35.0 4.9 %collective-permute-start.11 = (bf16[8,2688]{1,0:T(8,128)(2,1)S(1)}, bf16[8,2688]{1,0:T(8,128)(2,1)S(1)}, u32[]{:S(2)}, u32[]{:S(2)}) collective-permute-start(bf16[8,2688]{1,0:T(8,128)(2,1)S(1)} %get-tuple-element.29), channel_id=1, source_target_pairs={{0,4},{1,5},{2,6},{3,7},{4,0},{5,1},{6,2},{7,3},{8,12},{9,13},{10,... | collective-permute-start | bytes 129032 | tf_op jit(solution)/shard_map/ppermute | solution.py:95
  35.3 5.8 %collective-permute-start.12 = (bf16[8,2688]{1,0:T(8,128)(2,1)S(1)}, bf16[8,2688]{1,0:T(8,128)(2,1)S(1)}, u32[]{:S(2)}, u32[]{:S(2)}) collective-permute-start(bf16[8,2688]{1,0:T(8,128)(2,1)S(1)} %get-tuple-element.30), channel_id=1, source_target_pairs={{0,2},{1,3},{2,4},{3,5},{4,6},{5,7},{6,0},{7,1},{8,10},{9,11},{10,... | collective-permute-start | bytes 129032 | tf_op jit(solution)/shard_map/ppermute | solution.py:95

commit v5 on v4

--- a/solution.py
+++ b/solution.py
@@ -189,7 +189,8 @@
 
 def join_kernel(*refs):
     pieces, out_ref = refs[:-1], refs[-1]
-    out_ref[...] = jnp.concatenate([piece[...] for piece in pieces], axis=0)
+    whole = jnp.concatenate([piece[...].astype(jnp.float32) for piece in pieces], axis=0)
+    out_ref[...] = whole.astype(jnp.bfloat16)
 
 
 def fetch_kernel(gate_hbm, up_hbm, down_hbm, out_ref, sems):
@@ -214,15 +215,16 @@
 
 
 def expert_kernel(tok_count, slices, rows_ref, *refs):
-    weights, (out_ref, narrow, wide) = refs[:slices], refs[slices:]
+    weights, (out_ref, packed, wide) = refs[:slices], refs[slices:]
     units = LANES
     feature = wide.shape[1] - LANES
     body = feature - tail_width(tok_count, feature)
     own_expert = lax.axis_index("grp") * EXP_GRP + lax.axis_index("loc") // slices
+    packed[...] = rows_ref[...].astype(jnp.float32)
     for i in range(EXP_GRP):
-        narrow[...] = rows_ref[i * SUBLANES : (i + 1) * SUBLANES, :].astype(jnp.float32)
-        unpack_rows(narrow, wide, i * tok_count, tok_count, feature)
-        wide[i * tok_count : (i + 1) * tok_count, feature:] = narrow[:tok_count, body:]
+        piece = packed.at[i * SUBLANES : (i + 1) * SUBLANES]
+        unpack_rows(piece, wide, i * tok_count, tok_count, feature)
+        wide[i * tok_count : (i + 1) * tok_count, feature:] = piece[:tok_count, body:]
     features = wide[:, :feature].astype(jnp.bfloat16)
     table = wide[:, feature:]
     lanes = lax.broadcasted_iota(jnp.int32, table.shape, 1)
@@ -248,8 +250,9 @@
     )
     wide[:, :feature] = part * weight
     for i in range(EXP_GRP):
-        pack_rows(wide, i * tok_count, tok_count, feature, narrow)
-        out_ref[i * SUBLANES : (i + 1) * SUBLANES, :] = narrow[:, :body].astype(out_ref.dtype)
+        piece = packed.at[i * SUBLANES : (i + 1) * SUBLANES]
+        pack_rows(wide, i * tok_count, tok_count, feature, piece)
+    out_ref[...] = packed[:, :body].astype(out_ref.dtype)
 
 
 def combine_kernel(*refs):
@@ -320,7 +323,7 @@
             functools.partial(expert_kernel, tok_count, slices),
             jax.ShapeDtypeStruct((EXP_GRP * SUBLANES, body), dtype),
             (rows, *weights),
-            [scratch((SUBLANES, body + LANES), f32), scratch((gathered, feature + LANES), f32)],
+            [scratch(rows.shape, f32), scratch((gathered, feature + LANES), f32)],
             flops=2 * gathered * size * slices,
             traffic=2 * size * slices,
         )
@@ -330,7 +333,7 @@
     )
     first, second = [1 + i % 2 for i in range(slices)], [2 - i % 2 for i in range(slices)]
     beside, above = turn(rows, first), turn(rows, second)
-    across = turn(beside, second)
+    across = swap(rows, "grp", 3)
     returned = (
         turn(run_expert(beside, bf16), first),
         turn(run_expert(above, bf16), second),

time: 42 us -> 40.4 us (0.962)
  starting transfers between devices: 18.9 us -> 17 us
  waiting for transfers between devices: 14.3 us -> 15 us
    ppermute x2 -> x3, starting transfers between devices: 2.88 us -> 0.73 us  [swap(): return lax.ppermute(rows, axis, pairs(lax.axis_size(axis), distance))]
    ppermute x2 -> x3, waiting for transfers between devices: 0.01 us -> 0.88 us  [swap(): return lax.ppermute(rows, axis, pairs(lax.axis_size(axis), distance))]
    ppermute x5 -> x4, starting transfers between devices: 6.75 us -> 6.96 us  [turn(): return lax.ppermute(rows, ('grp', 'loc'), moves)]
    ppermute x5 -> x4, waiting for transfers between devices: 7.45 us -> 7.31 us  [turn(): return lax.ppermute(rows, ('grp', 'loc'), moves)]
where the time goes in v5:
time: 40.4 us; the launch traced here: 40.2 us
  starting transfers between devices  17 us (42%)
  waiting for transfers between devices  15 us (37%)
  Pallas kernels  8.12 us (20%)
    ppermute x6, starting transfers between devices, slide(): lax.ppermute(rows, 'loc', [(i, (i + distance) % count) for i in range(cou...  9.32 us
    pallas_call x9, Pallas kernels, call(): pl.pallas_call(kernel, out_shape=outs, in_specs=specs or [VMEM] * len(arg...  8.12 us
    ppermute x4, waiting for transfers between devices, turn(): return lax.ppermute(rows, ('grp', 'loc'), moves)  7.31 us
    ppermute x4, starting transfers between devices, turn(): return lax.ppermute(rows, ('grp', 'loc'), moves)  6.96 us
    ppermute x6, waiting for transfers between devices, slide(): lax.ppermute(rows, 'loc', [(i, (i + distance) % count) for i in range(cou...  6.8 us
    ppermute x3, waiting for transfers between devices, swap(): return lax.ppermute(rows, axis, pairs(lax.axis_size(axis), distance))  0.88 us
  transfers between devices with their start and end apart: 13, of which 8 were waited for; matrix products, arithmetic and copies ran while one was open for 0% of the time, Pallas kernels for 16%

profile of v5, /device:TPU:0, one launch (start us, length us, event | category | flops | bytes accessed | tf_op | source)
XLA Modules:
  0.0 40.2 jit_solution(13400584659350262772)
XLA Ops:
  0.0 1.0 %shard_map.64.refs_0_ = bf16[8,2816]{1,0:T(8,128)(2,1)S(1)} custom-call(bf16[6,3584]{1,0:T(8,128)(2,1)} %bitcast.10, s32[6,1,8]{2,1,0:T(1,128)} %bitcast.11, bf16[6,8]{1,0:T(8,128)(2,1)} %bitcast.12), custom_call_target="tpu_custom_call" | custom-call | tf_op jit(solution)/shard_map/pallas_call | solution.py:152
  1.0 5.1 %collective-permute-start.2 = (bf16[8,2816]{1,0:T(8,128)(2,1)S(1)}, bf16[8,2816]{1,0:T(8,128)(2,1)S(1)}, u32[]{:S(2)}, u32[]{:S(2)}) collective-permute-start(bf16[8,2816]{1,0:T(8,128)(2,1)S(1)} %shard_map.64.refs_0_), channel_id=1, source_target_pairs={{0,6},{1,7},{2,0},{3,1},{4,2},{5,3},{6,4},{7,5},{8,14},{9,15},{10,... | collective-permute-start | bytes 135176 | tf_op jit(solution)/shard_map/ppermute | solution.py:95
  6.1 0.0 collective-permute-start.1
  6.1 1.0 %collective-permute-start = (bf16[8,2816]{1,0:T(8,128)(2,1)S(1)}, bf16[8,2816]{1,0:T(8,128)(2,1)S(1)}, u32[]{:S(2)}, u32[]{:S(2)}) collective-permute-start(bf16[8,2816]{1,0:T(8,128)(2,1)S(1)} %shard_map.64.refs_0_), channel_id=1, source_target_pairs={{0,2},{1,3},{2,4},{3,5},{4,6},{5,7},{6,0},{7,1},{8,10},{9,11},{10,... | collective-permute-start | bytes 135176 | tf_op jit(solution)/shard_map/ppermute | solution.py:95
  7.2 1.9 %shard_map.65.refs_0_ = bf16[10752,128]{1,0:T(8,128)(2,1)S(1)} custom-call(bf16[3584,128]{1,0:T(8,128)(2,1)} %bitcast.7, bf16[3584,128]{1,0:T(8,128)(2,1)} %bitcast.8, bf16[128,3584]{1,0:T(8,128)(2,1)} %bitcast.9), custom_call_target="tpu_custom_call" | custom-call | bytes 2752512 | tf_op jit(solution)/shard_map/pallas_call | solution.py:152
  9.1 0.0 collective-permute-done.2.refs_3_
  9.1 2.0 %collective-permute-done.1.refs_2_ = bf16[8,2816]{1,0:T(8,128)(2,1)S(1)} collective-permute-done((bf16[8,2816]{1,0:T(8,128)(2,1)S(1)}, bf16[8,2816]{1,0:T(8,128)(2,1)S(1)}, u32[]{:S(2)}, u32[]{:S(2)}) %collective-permute-start.1) | collective-permute-done | bytes 45088 | tf_op jit(solution)/shard_map/ppermute | solution.py:95
  11.1 0.9 %collective-permute-done.refs_1_ = bf16[8,2816]{1,0:T(8,128)(2,1)S(1)} collective-permute-done((bf16[8,2816]{1,0:T(8,128)(2,1)S(1)}, bf16[8,2816]{1,0:T(8,128)(2,1)S(1)}, u32[]{:S(2)}, u32[]{:S(2)}) %collective-permute-start) | collective-permute-done | bytes 45088 | tf_op jit(solution)/shard_map/ppermute | solution.py:95
  12.0 0.0 collective-permute-start.3
  12.0 1.6 %collective-permute-start.4 = (bf16[32,2816]{1,0:T(8,128)(2,1)S(1)}, bf16[32,2816]{1,0:T(8,128)(2,1)S(1)}, u32[]{:S(2)}, u32[]{:S(2)}) collective-permute-start(bf16[32,2816]{1,0:T(8,128)(2,1)S(1)} %shard_map.66.rows_ref), channel_id=1, source_target_pairs={{0,8},{1,17},{2,10},{3,19},{4,12},{5,21},{6,14},{7,23},{8,0},{9,25... | collective-permute-start | bytes 540680 | tf_op jit(solution)/shard_map/ppermute | solution.py:105
  13.6 1.5 %collective-permute-start.6 = (bf16[32,2816]{1,0:T(8,128)(2,1)S(1)}, bf16[32,2816]{1,0:T(8,128)(2,1)S(1)}, u32[]{:S(2)}, u32[]{:S(2)}) collective-permute-start(bf16[32,2816]{1,0:T(8,128)(2,1)S(1)} %shard_map.66.rows_ref), channel_id=1, source_target_pairs={{0,16},{1,9},{2,18},{3,11},{4,20},{5,13},{6,22},{7,15},{8,24},{9,1... | collective-permute-start | bytes 540680 | tf_op jit(solution)/shard_map/ppermute | solution.py:105
  15.1 0.5 %collective-permute-start.8 = (bf16[32,2816]{1,0:T(8,128)(2,1)S(1)}, bf16[32,2816]{1,0:T(8,128)(2,1)S(1)}, u32[]{:S(2)}, u32[]{:S(2)}) collective-permute-start(bf16[32,2816]{1,0:T(8,128)(2,1)S(1)} %shard_map.66.rows_ref), channel_id=1, source_target_pairs={{0,24},{8,16},{16,8},{24,0},{1,25},{9,17},{17,9},{25,1},{2,26},{10... | collective-permute-start | bytes 540680 | tf_op jit(solution)/shard_map/ppermute | solution.py:90
  15.6 3.2 %collective-permute-done.4.rows_ref = bf16[32,2816]{1,0:T(8,128)(2,1)S(1)} collective-permute-done((bf16[32,2816]{1,0:T(8,128)(2,1)S(1)}, bf16[32,2816]{1,0:T(8,128)(2,1)S(1)}, u32[]{:S(2)}, u32[]{:S(2)}) %collective-permute-start.4) | collective-permute-done | bytes 180256 | tf_op jit(solution)/shard_map/ppermute | solution.py:105
  18.8 0.0 collective-permute-done.3.refs_1_
  18.8 1.1 %shard_map.68 = bf16[32,2688]{1,0:T(8,128)(2,1)S(1)} custom-call(bf16[32,2816]{1,0:T(8,128)(2,1)S(1)} %collective-permute-done.4.rows_ref, bf16[10752,128]{1,0:T(8,128)(2,1)S(1)} %shard_map.65.refs_0_, bf16[10752,128]{1,0:T(8,128)(2,1)S(1)} %collective-permute-done.3.refs_1_), custom_call_target="tpu_custom_call" | custom-call | flops 132120576 | bytes 5505024 | tf_op jit(solution)/shard_map/pallas_call | solution.py:152
  19.9 1.6 %collective-permute-start.5 = (bf16[32,2688]{1,0:T(8,128)(2,1)S(1)}, bf16[32,2688]{1,0:T(8,128)(2,1)S(1)}, u32[]{:S(2)}, u32[]{:S(2)}) collective-permute-start(bf16[32,2688]{1,0:T(8,128)(2,1)S(1)} %shard_map.68), channel_id=1, source_target_pairs={{0,8},{1,17},{2,10},{3,19},{4,12},{5,21},{6,14},{7,23},{8,0},{9,25... | collective-permute-start | bytes 516104 | tf_op jit(solution)/shard_map/ppermute | solution.py:105
  21.4 0.0 collective-permute-done.6.rows_ref
  21.4 1.1 %shard_map.69 = bf16[32,2688]{1,0:T(8,128)(2,1)S(1)} custom-call(bf16[32,2816]{1,0:T(8,128)(2,1)S(1)} %collective-permute-done.6.rows_ref, bf16[10752,128]{1,0:T(8,128)(2,1)S(1)} %shard_map.65.refs_0_, bf16[10752,128]{1,0:T(8,128)(2,1)S(1)} %collective-permute-done.3.refs_1_), custom_call_target="tpu_custom_call" | custom-call | flops 132120576 | bytes 5505024 | tf_op jit(solution)/shard_map/pallas_call | solution.py:152
  22.5 2.3 %collective-permute-start.7 = (bf16[32,2688]{1,0:T(8,128)(2,1)S(1)}, bf16[32,2688]{1,0:T(8,128)(2,1)S(1)}, u32[]{:S(2)}, u32[]{:S(2)}) collective-permute-start(bf16[32,2688]{1,0:T(8,128)(2,1)S(1)} %shard_map.69), channel_id=1, source_target_pairs={{0,16},{1,9},{2,18},{3,11},{4,20},{5,13},{6,22},{7,15},{8,24},{9,1... | collective-permute-start | bytes 516104 | tf_op jit(solution)/shard_map/ppermute | solution.py:105
  24.9 0.0 collective-permute-done.8.rows_ref
  24.9 1.1 %shard_map.70 = bf16[32,2688]{1,0:T(8,128)(2,1)S(1)} custom-call(bf16[32,2816]{1,0:T(8,128)(2,1)S(1)} %collective-permute-done.8.rows_ref, bf16[10752,128]{1,0:T(8,128)(2,1)S(1)} %shard_map.65.refs_0_, bf16[10752,128]{1,0:T(8,128)(2,1)S(1)} %collective-permute-done.3.refs_1_), custom_call_target="tpu_custom_call" | custom-call | flops 132120576 | bytes 5505024 | tf_op jit(solution)/shard_map/pallas_call | solution.py:152
  26.0 0.3 collective-permute-start.9
  26.3 1.1 %shard_map.67.refs_0_ = f32[32,2688]{1,0:T(8,128)S(1)} custom-call(bf16[32,2816]{1,0:T(8,128)(2,1)S(1)} %shard_map.66.rows_ref, bf16[10752,128]{1,0:T(8,128)(2,1)S(1)} %shard_map.65.refs_0_, bf16[10752,128]{1,0:T(8,128)(2,1)S(1)} %collective-permute-done.3.refs_1_), custom_call_target="tpu_custom_call" | custom-call | flops 132120576 | bytes 5505024 | tf_op jit(solution)/shard_map/pallas_call | solution.py:152
  27.4 0.0 collective-permute-done.5.refs_1_
  27.4 4.1 %collective-permute-done.7.refs_2_ = bf16[32,2688]{1,0:T(8,128)(2,1)S(1)} collective-permute-done((bf16[32,2688]{1,0:T(8,128)(2,1)S(1)}, bf16[32,2688]{1,0:T(8,128)(2,1)S(1)}, u32[]{:S(2)}, u32[]{:S(2)}) %collective-permute-start.7) | collective-permute-done | bytes 172064 | tf_op jit(solution)/shard_map/ppermute | solution.py:105
  31.5 0.9 %collective-permute-done.9.refs_3_ = bf16[32,2688]{1,0:T(8,128)(2,1)S(1)} collective-permute-done((bf16[32,2688]{1,0:T(8,128)(2,1)S(1)}, bf16[32,2688]{1,0:T(8,128)(2,1)S(1)}, u32[]{:S(2)}, u32[]{:S(2)}) %collective-permute-start.9) | collective-permute-done | bytes 172064 | tf_op jit(solution)/shard_map/ppermute | solution.py:90
  32.4 0.1 shard_map.71
  32.5 1.0 %collective-permute-start.10 = (bf16[8,2688]{1,0:T(8,128)(2,1)S(1)}, bf16[8,2688]{1,0:T(8,128)(2,1)S(1)}, u32[]{:S(2)}, u32[]{:S(2)}) collective-permute-start(bf16[8,2688]{1,0:T(8,128)(2,1)S(1)} %get-tuple-element.28), channel_id=1, source_target_pairs={{0,6},{1,7},{2,0},{3,1},{4,2},{5,3},{6,4},{7,5},{8,14},{9,15},{10,... | collective-permute-start | bytes 129032 | tf_op jit(solution)/shard_map/ppermute | solution.py:95
  33.4 0.3 collective-permute-start.11
  33.7 1.9 %collective-permute-start.12 = (bf16[8,2688]{1,0:T(8,128)(2,1)S(1)}, bf16[8,2688]{1,0:T(8,128)(2,1)S(1)}, u32[]{:S(2)}, u32[]{:S(2)}) collective-permute-start(bf16[8,2688]{1,0:T(8,128)(2,1)S(1)} %get-tuple-element.30), channel_id=1, source_target_pairs={{0,2},{1,3},{2,4},{3,5},{4,6},{5,7},{6,0},{7,1},{8,10},{9,11},{10,... | collective-permute-start | bytes 129032 | tf_op jit(solution)/shard_map/ppermute | solution.py:95
  35.7 1.2 %collective-permute-done.10.refs_1_ = bf16[8,2688]{1,0:T(8,128)(2,1)S(1)} collective-permute-done((bf16[8,2688]{1,0:T(8,128)(2,1)S(1)}, bf16[8,2688]{1,0:T(8,128)(2,1)S(1)}, u32[]{:S(2)}, u32[]{:S(2)}) %collective-permute-start.10) | collective-permute-done | bytes 43040 | tf_op jit(solution)/shard_map/ppermute | solution.py:95
  36.9 1.5 %collective-permute-done.11.refs_2_ = bf16[8,2688]{1,0:T(8,128)(2,1)S(1)} collective-permute-done((bf16[8,2688]{1,0:T(8,128)(2,1)S(1)}, bf16[8,2688]{1,0:T(8,128)(2,1)S(1)}, u32[]{:S(2)}, u32[]{:S(2)}) %collective-permute-start.11) | collective-permute-done | bytes 43040 | tf_op jit(solution)/shard_map/ppermute | solution.py:95
  38.4 1.2 %collective-permute-done.12.refs_3_ = bf16[8,2688]{1,0:T(8,128)(2,1)S(1)} collective-permute-done((bf16[8,2688]{1,0:T(8,128)(2,1)S(1)}, bf16[8,2688]{1,0:T(8,128)(2,1)S(1)}, u32[]{:S(2)}, u32[]{:S(2)}) %collective-permute-start.12) | collective-permute-done | bytes 43040 | tf_op jit(solution)/shard_map/ppermute | solution.py:95
  39.5 0.7 %shard_map.72 = bf16[6,3584]{1,0:T(8,128)(2,1)} custom-call(f32[8,2688]{1,0:T(8,128)S(1)} %get-tuple-element.27.refs_0_, bf16[8,2688]{1,0:T(8,128)(2,1)S(1)} %collective-permute-done.10.refs_1_, bf16[8,2688]{1,0:T(8,128)(2,1)S(1)} %collective-permute-done.11.refs_2_, bf16[8,2688]{1,0:T(8,128)(2,1)S(1)} %collective-permute-done.12.refs_3_), custom_call_target="tpu_custom_call" | custom-call | tf_op jit(solution)/shard_map/pallas_call | solution.py:152
  (1 shorter events, 0.0 us)
Async XLA Ops:
  1.0 8.0 %collective-permute-start.2 = (bf16[8,2816]{1,0:T(8,128)(2,1)S(1)}, bf16[8,2816]{1,0:T(8,128)(2,1)S(1)}, u32[]{:S(2)}, u32[]{:S(2)}) collective-permute-start(bf16[8,2816]{1,0:T(8,128)(2,1)S(1)} %shard_map.64.refs_0_), channel_id=1, source_target_pairs={{0,6},{1,7},{2,0},{3,1},{4,2},{5,3},{6,4},{7,5},{8,14},{9,15},{10,... | collective-permute-start | bytes 135176 | tf_op jit(solution)/shard_map/ppermute | solution.py:95
  6.1 4.9 %collective-permute-start.1 = (bf16[8,2816]{1,0:T(8,128)(2,1)S(1)}, bf16[8,2816]{1,0:T(8,128)(2,1)S(1)}, u32[]{:S(2)}, u32[]{:S(2)}) collective-permute-start(bf16[8,2816]{1,0:T(8,128)(2,1)S(1)} %shard_map.64.refs_0_), channel_id=1, source_target_pairs={{0,4},{1,5},{2,6},{3,7},{4,0},{5,1},{6,2},{7,3},{8,12},{9,13},{10,... | collective-permute-start | bytes 135176 | tf_op jit(solution)/shard_map/ppermute | solution.py:95
  6.1 5.8 %collective-permute-start = (bf16[8,2816]{1,0:T(8,128)(2,1)S(1)}, bf16[8,2816]{1,0:T(8,128)(2,1)S(1)}, u32[]{:S(2)}, u32[]{:S(2)}) collective-permute-start(bf16[8,2816]{1,0:T(8,128)(2,1)S(1)} %shard_map.64.refs_0_), channel_id=1, source_target_pairs={{0,2},{1,3},{2,4},{3,5},{4,6},{5,7},{6,0},{7,1},{8,10},{9,11},{10,... | collective-permute-start | bytes 135176 | tf_op jit(solution)/shard_map/ppermute | solution.py:95
  12.0 6.8 %collective-permute-start.3 = (bf16[10752,128]{1,0:T(8,128)(2,1)S(1)}, bf16[10752,128]{1,0:T(8,128)(2,1)S(1)}, u32[]{:S(2)}, u32[]{:S(2)}) collective-permute-start(bf16[10752,128]{1,0:T(8,128)(2,1)S(1)} %shard_map.65.refs_0_), channel_id=1, source_target_pairs={{0,1},{1,0},{2,3},{3,2},{4,5},{5,4},{6,7},{7,6},{8,9},{9,8},{10,11... | collective-permute-start | bytes 8257544 | tf_op jit(solution)/shard_map/ppermute | solution.py:90
  12.0 6.7 %collective-permute-start.4 = (bf16[32,2816]{1,0:T(8,128)(2,1)S(1)}, bf16[32,2816]{1,0:T(8,128)(2,1)S(1)}, u32[]{:S(2)}, u32[]{:S(2)}) collective-permute-start(bf16[32,2816]{1,0:T(8,128)(2,1)S(1)} %shard_map.66.rows_ref), channel_id=1, source_target_pairs={{0,8},{1,17},{2,10},{3,19},{4,12},{5,21},{6,14},{7,23},{8,0},{9,25... | collective-permute-start | bytes 540680 | tf_op jit(solution)/shard_map/ppermute | solution.py:105
  13.6 7.9 %collective-permute-start.6 = (bf16[32,2816]{1,0:T(8,128)(2,1)S(1)}, bf16[32,2816]{1,0:T(8,128)(2,1)S(1)}, u32[]{:S(2)}, u32[]{:S(2)}) collective-permute-start(bf16[32,2816]{1,0:T(8,128)(2,1)S(1)} %shard_map.66.rows_ref), channel_id=1, source_target_pairs={{0,16},{1,9},{2,18},{3,11},{4,20},{5,13},{6,22},{7,15},{8,24},{9,1... | collective-permute-start | bytes 540680 | tf_op jit(solution)/shard_map/ppermute | solution.py:105
  15.1 9.8 %collective-permute-start.8 = (bf16[32,2816]{1,0:T(8,128)(2,1)S(1)}, bf16[32,2816]{1,0:T(8,128)(2,1)S(1)}, u32[]{:S(2)}, u32[]{:S(2)}) collective-permute-start(bf16[32,2816]{1,0:T(8,128)(2,1)S(1)} %shard_map.66.rows_ref), channel_id=1, source_target_pairs={{0,24},{8,16},{16,8},{24,0},{1,25},{9,17},{17,9},{25,1},{2,26},{10... | collective-permute-start | bytes 540680 | tf_op jit(solution)/shard_map/ppermute | solution.py:90
  19.9 7.5 %collective-permute-start.5 = (bf16[32,2688]{1,0:T(8,128)(2,1)S(1)}, bf16[32,2688]{1,0:T(8,128)(2,1)S(1)}, u32[]{:S(2)}, u32[]{:S(2)}) collective-permute-start(bf16[32,2688]{1,0:T(8,128)(2,1)S(1)} %shard_map.68), channel_id=1, source_target_pairs={{0,8},{1,17},{2,10},{3,19},{4,12},{5,21},{6,14},{7,23},{8,0},{9,25... | collective-permute-start | bytes 516104 | tf_op jit(solution)/shard_map/ppermute | solution.py:105
  22.5 8.9 %collective-permute-start.7 = (bf16[32,2688]{1,0:T(8,128)(2,1)S(1)}, bf16[32,2688]{1,0:T(8,128)(2,1)S(1)}, u32[]{:S(2)}, u32[]{:S(2)}) collective-permute-start(bf16[32,2688]{1,0:T(8,128)(2,1)S(1)} %shard_map.69), channel_id=1, source_target_pairs={{0,16},{1,9},{2,18},{3,11},{4,20},{5,13},{6,22},{7,15},{8,24},{9,1... | collective-permute-start | bytes 516104 | tf_op jit(solution)/shard_map/ppermute | solution.py:105
  26.0 6.4 %collective-permute-start.9 = (bf16[32,2688]{1,0:T(8,128)(2,1)S(1)}, bf16[32,2688]{1,0:T(8,128)(2,1)S(1)}, u32[]{:S(2)}, u32[]{:S(2)}) collective-permute-start(bf16[32,2688]{1,0:T(8,128)(2,1)S(1)} %shard_map.70), channel_id=1, source_target_pairs={{0,24},{8,16},{16,8},{24,0},{1,25},{9,17},{17,9},{25,1},{2,26},{10... | collective-permute-start | bytes 516104 | tf_op jit(solution)/shard_map/ppermute | solution.py:90
  32.5 4.4 %collective-permute-start.10 = (bf16[8,2688]{1,0:T(8,128)(2,1)S(1)}, bf16[8,2688]{1,0:T(8,128)(2,1)S(1)}, u32[]{:S(2)}, u32[]{:S(2)}) collective-permute-start(bf16[8,2688]{1,0:T(8,128)(2,1)S(1)} %get-tuple-element.28), channel_id=1, source_target_pairs={{0,6},{1,7},{2,0},{3,1},{4,2},{5,3},{6,4},{7,5},{8,14},{9,15},{10,... | collective-permute-start | bytes 129032 | tf_op jit(solution)/shard_map/ppermute | solution.py:95
  33.4 4.9 %collective-permute-start.11 = (bf16[8,2688]{1,0:T(8,128)(2,1)S(1)}, bf16[8,2688]{1,0:T(8,128)(2,1)S(1)}, u32[]{:S(2)}, u32[]{:S(2)}) collective-permute-start(bf16[8,2688]{1,0:T(8,128)(2,1)S(1)} %get-tuple-element.29), channel_id=1, source_target_pairs={{0,4},{1,5},{2,6},{3,7},{4,0},{5,1},{6,2},{7,3},{8,12},{9,13},{10,... | collective-permute-start | bytes 129032 | tf_op jit(solution)/shard_map/ppermute | solution.py:95
  33.7 5.8 %collective-permute-start.12 = (bf16[8,2688]{1,0:T(8,128)(2,1)S(1)}, bf16[8,2688]{1,0:T(8,128)(2,1)S(1)}, u32[]{:S(2)}, u32[]{:S(2)}) collective-permute-start(bf16[8,2688]{1,0:T(8,128)(2,1)S(1)} %get-tuple-element.30), channel_id=1, source_target_pairs={{0,2},{1,3},{2,4},{3,5},{4,6},{5,7},{6,0},{7,1},{8,10},{9,11},{10,... | collective-permute-start | bytes 129032 | tf_op jit(solution)/shard_map/ppermute | solution.py:95

commit v6 on v5

--- a/solution.py
+++ b/solution.py
@@ -177,13 +177,12 @@
     packed[:, body:] = jnp.zeros((SUBLANES, LANES), jnp.float32)
     pack_rows(wide, 0, tok_count, feature, packed)
     weights = picks[...].astype(jnp.float32)
-    lanes = lax.broadcasted_iota(jnp.int32, (1, LANES), 1)
-    for t in range(tok_count):
-        chosen = ids[t]
-        row = jnp.zeros((1, LANES), jnp.float32)
-        for k in range(chosen.shape[1]):
-            row = row + jnp.where(lanes == chosen[:, k : k + 1], weights[t : t + 1, k : k + 1], 0.0)
-        packed[t : t + 1, body:] = row
+    chosen = jnp.concatenate([ids[t] for t in range(tok_count)], axis=0)
+    lanes = lax.broadcasted_iota(jnp.int32, (tok_count, LANES), 1)
+    table = jnp.zeros((tok_count, LANES), jnp.float32)
+    for k in range(chosen.shape[1]):
+        table = table + jnp.where(lanes == chosen[:, k : k + 1], weights[:, k : k + 1], 0.0)
+    packed[:tok_count, body:] = table
     out_ref[...] = packed[...].astype(jnp.bfloat16)
 
 
@@ -304,7 +303,8 @@
         [HBM] * 3,
     )
     steps = range(1, EXP_GRP)
-    pieces = [own] + [slide(own, slices * k) for k in steps]
+    got = {k: slide(own, slices * k) for k in reversed(steps)}
+    pieces = [own] + [got[k] for k in steps]
     *blocks, pieces[0] = lax.optimization_barrier((*blocks, pieces[0]))
     size = sum(w.size for w in blocks)
     kept = call(
@@ -345,7 +345,7 @@
         [jax.ShapeDtypeStruct(packed, f32)] + [jax.ShapeDtypeStruct(packed, bf16)] * len(steps),
         (run_expert(rows, f32), *returned),
     )
-    homeward = [slide(sums[k], -slices * k) for k in steps]
+    homeward = [slide(sums[k], -slices * k) for k in reversed(steps)]
     total = call(
         finish_kernel,
         jax.ShapeDtypeStruct((tok_count, feature), bf16),

time: 40.4 us -> 39.7 us (0.983)
  waiting for transfers between devices: 15 us -> 13.4 us
  starting transfers between devices: 17 us -> 17.9 us
    ppermute x6, waiting for transfers between devices: 6.8 us -> 5.26 us  [slide(): lax.ppermute(rows, 'loc', [(i, (i + distance) % count) for i in range(cou...]
    ppermute x6, starting transfers between devices: 9.32 us -> 10.2 us  [slide(): lax.ppermute(rows, 'loc', [(i, (i + distance) % count) for i in range(cou...]
  transfers between devices with their start and end apart: 13 -> 13, of which waited for: 8 -> 7; matrix products, arithmetic and copies ran while one was open for 0% -> 0% of each run, Pallas kernels for 16% -> 16%
where the time goes in v6:
time: 39.7 us; the launch traced here: 39.5 us
  starting transfers between devices  17.9 us (45%)
  waiting for transfers between devices  13.4 us (34%)
  Pallas kernels  8.04 us (20%)
    ppermute x6, starting transfers between devices, slide(): lax.ppermute(rows, 'loc', [(i, (i + distance) % count) for i in range(cou...  10.2 us
    pallas_call x9, Pallas kernels, call(): pl.pallas_call(kernel, out_shape=outs, in_specs=specs or [VMEM] * len(arg...  8.04 us
    ppermute x4, waiting for transfers between devices, turn(): return lax.ppermute(rows, ('grp', 'loc'), moves)  7.3 us
    ppermute x4, starting transfers between devices, turn(): return lax.ppermute(rows, ('grp', 'loc'), moves)  6.96 us
    ppermute x6, waiting for transfers between devices, slide(): lax.ppermute(rows, 'loc', [(i, (i + distance) % count) for i in range(cou...  5.26 us
    ppermute x3, waiting for transfers between devices, swap(): return lax.ppermute(rows, axis, pairs(lax.axis_size(axis), distance))  0.88 us
  transfers between devices with their start and end apart: 13, of which 7 were waited for; matrix products, arithmetic and copies ran while one was open for 0% of the time, Pallas kernels for 16%

profile of v6, /device:TPU:0, one launch (start us, length us, event | category | flops | bytes accessed | tf_op | source)
XLA Modules:
  0.0 39.5 jit_solution(18246753769112608381)
XLA Ops:
  0.0 1.0 %shard_map.64.refs_0_ = bf16[8,2816]{1,0:T(8,128)(2,1)S(1)} custom-call(bf16[6,3584]{1,0:T(8,128)(2,1)} %bitcast.10, s32[6,1,8]{2,1,0:T(1,128)} %bitcast.11, bf16[6,8]{1,0:T(8,128)(2,1)} %bitcast.12), custom_call_target="tpu_custom_call" | custom-call | tf_op jit(solution)/shard_map/pallas_call | solution.py:152
  1.0 5.1 %collective-permute-start.2 = (bf16[8,2816]{1,0:T(8,128)(2,1)S(1)}, bf16[8,2816]{1,0:T(8,128)(2,1)S(1)}, u32[]{:S(2)}, u32[]{:S(2)}) collective-permute-start(bf16[8,2816]{1,0:T(8,128)(2,1)S(1)} %shard_map.64.refs_0_), channel_id=1, source_target_pairs={{0,6},{1,7},{2,0},{3,1},{4,2},{5,3},{6,4},{7,5},{8,14},{9,15},{10,... | collective-permute-start | bytes 135176 | tf_op jit(solution)/shard_map/ppermute | solution.py:95
  6.1 0.0 collective-permute-start.1
  6.1 1.0 %collective-permute-start = (bf16[8,2816]{1,0:T(8,128)(2,1)S(1)}, bf16[8,2816]{1,0:T(8,128)(2,1)S(1)}, u32[]{:S(2)}, u32[]{:S(2)}) collective-permute-start(bf16[8,2816]{1,0:T(8,128)(2,1)S(1)} %shard_map.64.refs_0_), channel_id=1, source_target_pairs={{0,2},{1,3},{2,4},{3,5},{4,6},{5,7},{6,0},{7,1},{8,10},{9,11},{10,... | collective-permute-start | bytes 135176 | tf_op jit(solution)/shard_map/ppermute | solution.py:95
  7.1 1.9 %shard_map.65.refs_0_ = bf16[10752,128]{1,0:T(8,128)(2,1)S(1)} custom-call(bf16[3584,128]{1,0:T(8,128)(2,1)} %bitcast.7, bf16[3584,128]{1,0:T(8,128)(2,1)} %bitcast.8, bf16[128,3584]{1,0:T(8,128)(2,1)} %bitcast.9), custom_call_target="tpu_custom_call" | custom-call | bytes 2752512 | tf_op jit(solution)/shard_map/pallas_call | solution.py:152
  9.0 0.0 collective-permute-done.2.refs_3_
  9.0 2.0 %collective-permute-done.1.refs_2_ = bf16[8,2816]{1,0:T(8,128)(2,1)S(1)} collective-permute-done((bf16[8,2816]{1,0:T(8,128)(2,1)S(1)}, bf16[8,2816]{1,0:T(8,128)(2,1)S(1)}, u32[]{:S(2)}, u32[]{:S(2)}) %collective-permute-start.1) | collective-permute-done | bytes 45088 | tf_op jit(solution)/shard_map/ppermute | solution.py:95
  11.0 0.9 %collective-permute-done.refs_1_ = bf16[8,2816]{1,0:T(8,128)(2,1)S(1)} collective-permute-done((bf16[8,2816]{1,0:T(8,128)(2,1)S(1)}, bf16[8,2816]{1,0:T(8,128)(2,1)S(1)}, u32[]{:S(2)}, u32[]{:S(2)}) %collective-permute-start) | collective-permute-done | bytes 45088 | tf_op jit(solution)/shard_map/ppermute | solution.py:95
  11.9 0.0 collective-permute-start.3
  11.9 1.6 %collective-permute-start.4 = (bf16[32,2816]{1,0:T(8,128)(2,1)S(1)}, bf16[32,2816]{1,0:T(8,128)(2,1)S(1)}, u32[]{:S(2)}, u32[]{:S(2)}) collective-permute-start(bf16[32,2816]{1,0:T(8,128)(2,1)S(1)} %shard_map.66.rows_ref), channel_id=1, source_target_pairs={{0,8},{1,17},{2,10},{3,19},{4,12},{5,21},{6,14},{7,23},{8,0},{9,25... | collective-permute-start | bytes 540680 | tf_op jit(solution)/shard_map/ppermute | solution.py:105
  13.5 1.5 %collective-permute-start.6 = (bf16[32,2816]{1,0:T(8,128)(2,1)S(1)}, bf16[32,2816]{1,0:T(8,128)(2,1)S(1)}, u32[]{:S(2)}, u32[]{:S(2)}) collective-permute-start(bf16[32,2816]{1,0:T(8,128)(2,1)S(1)} %shard_map.66.rows_ref), channel_id=1, source_target_pairs={{0,16},{1,9},{2,18},{3,11},{4,20},{5,13},{6,22},{7,15},{8,24},{9,1... | collective-permute-start | bytes 540680 | tf_op jit(solution)/shard_map/ppermute | solution.py:105
  15.0 0.5 %collective-permute-start.8 = (bf16[32,2816]{1,0:T(8,128)(2,1)S(1)}, bf16[32,2816]{1,0:T(8,128)(2,1)S(1)}, u32[]{:S(2)}, u32[]{:S(2)}) collective-permute-start(bf16[32,2816]{1,0:T(8,128)(2,1)S(1)} %shard_map.66.rows_ref), channel_id=1, source_target_pairs={{0,24},{8,16},{16,8},{24,0},{1,25},{9,17},{17,9},{25,1},{2,26},{10... | collective-permute-start | bytes 540680 | tf_op jit(solution)/shard_map/ppermute | solution.py:90
  15.5 3.2 %collective-permute-done.4.rows_ref = bf16[32,2816]{1,0:T(8,128)(2,1)S(1)} collective-permute-done((bf16[32,2816]{1,0:T(8,128)(2,1)S(1)}, bf16[32,2816]{1,0:T(8,128)(2,1)S(1)}, u32[]{:S(2)}, u32[]{:S(2)}) %collective-permute-start.4) | collective-permute-done | bytes 180256 | tf_op jit(solution)/shard_map/ppermute | solution.py:105
  18.7 0.0 collective-permute-done.3.refs_1_
  18.7 1.1 %shard_map.68 = bf16[32,2688]{1,0:T(8,128)(2,1)S(1)} custom-call(bf16[32,2816]{1,0:T(8,128)(2,1)S(1)} %collective-permute-done.4.rows_ref, bf16[10752,128]{1,0:T(8,128)(2,1)S(1)} %shard_map.65.refs_0_, bf16[10752,128]{1,0:T(8,128)(2,1)S(1)} %collective-permute-done.3.refs_1_), custom_call_target="tpu_custom_call" | custom-call | flops 132120576 | bytes 5505024 | tf_op jit(solution)/shard_map/pallas_call | solution.py:152
  19.8 1.6 %collective-permute-start.5 = (bf16[32,2688]{1,0:T(8,128)(2,1)S(1)}, bf16[32,2688]{1,0:T(8,128)(2,1)S(1)}, u32[]{:S(2)}, u32[]{:S(2)}) collective-permute-start(bf16[32,2688]{1,0:T(8,128)(2,1)S(1)} %shard_map.68), channel_id=1, source_target_pairs={{0,8},{1,17},{2,10},{3,19},{4,12},{5,21},{6,14},{7,23},{8,0},{9,25... | collective-permute-start | bytes 516104 | tf_op jit(solution)/shard_map/ppermute | solution.py:105
  21.3 0.0 collective-permute-done.6.rows_ref
  21.4 1.1 %shard_map.69 = bf16[32,2688]{1,0:T(8,128)(2,1)S(1)} custom-call(bf16[32,2816]{1,0:T(8,128)(2,1)S(1)} %collective-permute-done.6.rows_ref, bf16[10752,128]{1,0:T(8,128)(2,1)S(1)} %shard_map.65.refs_0_, bf16[10752,128]{1,0:T(8,128)(2,1)S(1)} %collective-permute-done.3.refs_1_), custom_call_target="tpu_custom_call" | custom-call | flops 132120576 | bytes 5505024 | tf_op jit(solution)/shard_map/pallas_call | solution.py:152
  22.5 2.3 %collective-permute-start.7 = (bf16[32,2688]{1,0:T(8,128)(2,1)S(1)}, bf16[32,2688]{1,0:T(8,128)(2,1)S(1)}, u32[]{:S(2)}, u32[]{:S(2)}) collective-permute-start(bf16[32,2688]{1,0:T(8,128)(2,1)S(1)} %shard_map.69), channel_id=1, source_target_pairs={{0,16},{1,9},{2,18},{3,11},{4,20},{5,13},{6,22},{7,15},{8,24},{9,1... | collective-permute-start | bytes 516104 | tf_op jit(solution)/shard_map/ppermute | solution.py:105
  24.8 0.0 collective-permute-done.8.rows_ref
  24.8 1.1 %shard_map.70 = bf16[32,2688]{1,0:T(8,128)(2,1)S(1)} custom-call(bf16[32,2816]{1,0:T(8,128)(2,1)S(1)} %collective-permute-done.8.rows_ref, bf16[10752,128]{1,0:T(8,128)(2,1)S(1)} %shard_map.65.refs_0_, bf16[10752,128]{1,0:T(8,128)(2,1)S(1)} %collective-permute-done.3.refs_1_), custom_call_target="tpu_custom_call" | custom-call | flops 132120576 | bytes 5505024 | tf_op jit(solution)/shard_map/pallas_call | solution.py:152
  25.9 0.3 collective-permute-start.9
  26.2 1.1 %shard_map.67.refs_0_ = f32[32,2688]{1,0:T(8,128)S(1)} custom-call(bf16[32,2816]{1,0:T(8,128)(2,1)S(1)} %shard_map.66.rows_ref, bf16[10752,128]{1,0:T(8,128)(2,1)S(1)} %shard_map.65.refs_0_, bf16[10752,128]{1,0:T(8,128)(2,1)S(1)} %collective-permute-done.3.refs_1_), custom_call_target="tpu_custom_call" | custom-call | flops 132120576 | bytes 5505024 | tf_op jit(solution)/shard_map/pallas_call | solution.py:152
  27.3 0.0 collective-permute-done.5.refs_1_
  27.3 4.1 %collective-permute-done.7.refs_2_ = bf16[32,2688]{1,0:T(8,128)(2,1)S(1)} collective-permute-done((bf16[32,2688]{1,0:T(8,128)(2,1)S(1)}, bf16[32,2688]{1,0:T(8,128)(2,1)S(1)}, u32[]{:S(2)}, u32[]{:S(2)}) %collective-permute-start.7) | collective-permute-done | bytes 172064 | tf_op jit(solution)/shard_map/ppermute | solution.py:105
  31.4 0.9 %collective-permute-done.9.refs_3_ = bf16[32,2688]{1,0:T(8,128)(2,1)S(1)} collective-permute-done((bf16[32,2688]{1,0:T(8,128)(2,1)S(1)}, bf16[32,2688]{1,0:T(8,128)(2,1)S(1)}, u32[]{:S(2)}, u32[]{:S(2)}) %collective-permute-start.9) | collective-permute-done | bytes 172064 | tf_op jit(solution)/shard_map/ppermute | solution.py:90
  32.3 0.1 shard_map.71
  32.4 0.1 collective-permute-start.10
  32.4 1.5 %collective-permute-start.11 = (bf16[8,2688]{1,0:T(8,128)(2,1)S(1)}, bf16[8,2688]{1,0:T(8,128)(2,1)S(1)}, u32[]{:S(2)}, u32[]{:S(2)}) collective-permute-start(bf16[8,2688]{1,0:T(8,128)(2,1)S(1)} %get-tuple-element.29), channel_id=1, source_target_pairs={{0,4},{1,5},{2,6},{3,7},{4,0},{5,1},{6,2},{7,3},{8,12},{9,13},{10,... | collective-permute-start | bytes 129032 | tf_op jit(solution)/shard_map/ppermute | solution.py:95
  33.9 2.6 %collective-permute-start.12 = (bf16[8,2688]{1,0:T(8,128)(2,1)S(1)}, bf16[8,2688]{1,0:T(8,128)(2,1)S(1)}, u32[]{:S(2)}, u32[]{:S(2)}) collective-permute-start(bf16[8,2688]{1,0:T(8,128)(2,1)S(1)} %get-tuple-element.30), channel_id=1, source_target_pairs={{0,6},{1,7},{2,0},{3,1},{4,2},{5,3},{6,4},{7,5},{8,14},{9,15},{10,... | collective-permute-start | bytes 129032 | tf_op jit(solution)/shard_map/ppermute | solution.py:95
  36.5 1.8 %collective-permute-done.10.refs_1_ = bf16[8,2688]{1,0:T(8,128)(2,1)S(1)} collective-permute-done((bf16[8,2688]{1,0:T(8,128)(2,1)S(1)}, bf16[8,2688]{1,0:T(8,128)(2,1)S(1)}, u32[]{:S(2)}, u32[]{:S(2)}) %collective-permute-start.10) | collective-permute-done | bytes 43040 | tf_op jit(solution)/shard_map/ppermute | solution.py:95
  38.2 0.0 collective-permute-done.11.refs_2_
  38.3 0.6 %collective-permute-done.12.refs_3_ = bf16[8,2688]{1,0:T(8,128)(2,1)S(1)} collective-permute-done((bf16[8,2688]{1,0:T(8,128)(2,1)S(1)}, bf16[8,2688]{1,0:T(8,128)(2,1)S(1)}, u32[]{:S(2)}, u32[]{:S(2)}) %collective-permute-start.12) | collective-permute-done | bytes 43040 | tf_op jit(solution)/shard_map/ppermute | solution.py:95
  38.8 0.7 %shard_map.72 = bf16[6,3584]{1,0:T(8,128)(2,1)} custom-call(f32[8,2688]{1,0:T(8,128)S(1)} %get-tuple-element.27.refs_0_, bf16[8,2688]{1,0:T(8,128)(2,1)S(1)} %collective-permute-done.10.refs_1_, bf16[8,2688]{1,0:T(8,128)(2,1)S(1)} %collective-permute-done.11.refs_2_, bf16[8,2688]{1,0:T(8,128)(2,1)S(1)} %collective-permute-done.12.refs_3_), custom_call_target="tpu_custom_call" | custom-call | tf_op jit(solution)/shard_map/pallas_call | solution.py:152
  (1 shorter events, 0.0 us)
Async XLA Ops:
  1.0 8.0 %collective-permute-start.2 = (bf16[8,2816]{1,0:T(8,128)(2,1)S(1)}, bf16[8,2816]{1,0:T(8,128)(2,1)S(1)}, u32[]{:S(2)}, u32[]{:S(2)}) collective-permute-start(bf16[8,2816]{1,0:T(8,128)(2,1)S(1)} %shard_map.64.refs_0_), channel_id=1, source_target_pairs={{0,6},{1,7},{2,0},{3,1},{4,2},{5,3},{6,4},{7,5},{8,14},{9,15},{10,... | collective-permute-start | bytes 135176 | tf_op jit(solution)/shard_map/ppermute | solution.py:95
  6.1 4.9 %collective-permute-start.1 = (bf16[8,2816]{1,0:T(8,128)(2,1)S(1)}, bf16[8,2816]{1,0:T(8,128)(2,1)S(1)}, u32[]{:S(2)}, u32[]{:S(2)}) collective-permute-start(bf16[8,2816]{1,0:T(8,128)(2,1)S(1)} %shard_map.64.refs_0_), channel_id=1, source_target_pairs={{0,4},{1,5},{2,6},{3,7},{4,0},{5,1},{6,2},{7,3},{8,12},{9,13},{10,... | collective-permute-start | bytes 135176 | tf_op jit(solution)/shard_map/ppermute | solution.py:95
  6.1 5.8 %collective-permute-start = (bf16[8,2816]{1,0:T(8,128)(2,1)S(1)}, bf16[8,2816]{1,0:T(8,128)(2,1)S(1)}, u32[]{:S(2)}, u32[]{:S(2)}) collective-permute-start(bf16[8,2816]{1,0:T(8,128)(2,1)S(1)} %shard_map.64.refs_0_), channel_id=1, source_target_pairs={{0,2},{1,3},{2,4},{3,5},{4,6},{5,7},{6,0},{7,1},{8,10},{9,11},{10,... | collective-permute-start | bytes 135176 | tf_op jit(solution)/shard_map/ppermute | solution.py:95
  11.9 6.8 %collective-permute-start.3 = (bf16[10752,128]{1,0:T(8,128)(2,1)S(1)}, bf16[10752,128]{1,0:T(8,128)(2,1)S(1)}, u32[]{:S(2)}, u32[]{:S(2)}) collective-permute-start(bf16[10752,128]{1,0:T(8,128)(2,1)S(1)} %shard_map.65.refs_0_), channel_id=1, source_target_pairs={{0,1},{1,0},{2,3},{3,2},{4,5},{5,4},{6,7},{7,6},{8,9},{9,8},{10,11... | collective-permute-start | bytes 8257544 | tf_op jit(solution)/shard_map/ppermute | solution.py:90
  11.9 6.7 %collective-permute-start.4 = (bf16[32,2816]{1,0:T(8,128)(2,1)S(1)}, bf16[32,2816]{1,0:T(8,128)(2,1)S(1)}, u32[]{:S(2)}, u32[]{:S(2)}) collective-permute-start(bf16[32,2816]{1,0:T(8,128)(2,1)S(1)} %shard_map.66.rows_ref), channel_id=1, source_target_pairs={{0,8},{1,17},{2,10},{3,19},{4,12},{5,21},{6,14},{7,23},{8,0},{9,25... | collective-permute-start | bytes 540680 | tf_op jit(solution)/shard_map/ppermute | solution.py:105
  13.5 7.9 %collective-permute-start.6 = (bf16[32,2816]{1,0:T(8,128)(2,1)S(1)}, bf16[32,2816]{1,0:T(8,128)(2,1)S(1)}, u32[]{:S(2)}, u32[]{:S(2)}) collective-permute-start(bf16[32,2816]{1,0:T(8,128)(2,1)S(1)} %shard_map.66.rows_ref), channel_id=1, source_target_pairs={{0,16},{1,9},{2,18},{3,11},{4,20},{5,13},{6,22},{7,15},{8,24},{9,1... | collective-permute-start | bytes 540680 | tf_op jit(solution)/shard_map/ppermute | solution.py:105
  15.0 9.8 %collective-permute-start.8 = (bf16[32,2816]{1,0:T(8,128)(2,1)S(1)}, bf16[32,2816]{1,0:T(8,128)(2,1)S(1)}, u32[]{:S(2)}, u32[]{:S(2)}) collective-permute-start(bf16[32,2816]{1,0:T(8,128)(2,1)S(1)} %shard_map.66.rows_ref), channel_id=1, source_target_pairs={{0,24},{8,16},{16,8},{24,0},{1,25},{9,17},{17,9},{25,1},{2,26},{10... | collective-permute-start | bytes 540680 | tf_op jit(solution)/shard_map/ppermute | solution.py:90
  19.8 7.5 %collective-permute-start.5 = (bf16[32,2688]{1,0:T(8,128)(2,1)S(1)}, bf16[32,2688]{1,0:T(8,128)(2,1)S(1)}, u32[]{:S(2)}, u32[]{:S(2)}) collective-permute-start(bf16[32,2688]{1,0:T(8,128)(2,1)S(1)} %shard_map.68), channel_id=1, source_target_pairs={{0,8},{1,17},{2,10},{3,19},{4,12},{5,21},{6,14},{7,23},{8,0},{9,25... | collective-permute-start | bytes 516104 | tf_op jit(solution)/shard_map/ppermute | solution.py:105
  22.5 8.9 %collective-permute-start.7 = (bf16[32,2688]{1,0:T(8,128)(2,1)S(1)}, bf16[32,2688]{1,0:T(8,128)(2,1)S(1)}, u32[]{:S(2)}, u32[]{:S(2)}) collective-permute-start(bf16[32,2688]{1,0:T(8,128)(2,1)S(1)} %shard_map.69), channel_id=1, source_target_pairs={{0,16},{1,9},{2,18},{3,11},{4,20},{5,13},{6,22},{7,15},{8,24},{9,1... | collective-permute-start | bytes 516104 | tf_op jit(solution)/shard_map/ppermute | solution.py:105
  25.9 6.4 %collective-permute-start.9 = (bf16[32,2688]{1,0:T(8,128)(2,1)S(1)}, bf16[32,2688]{1,0:T(8,128)(2,1)S(1)}, u32[]{:S(2)}, u32[]{:S(2)}) collective-permute-start(bf16[32,2688]{1,0:T(8,128)(2,1)S(1)} %shard_map.70), channel_id=1, source_target_pairs={{0,24},{8,16},{16,8},{24,0},{1,25},{9,17},{17,9},{25,1},{2,26},{10... | collective-permute-start | bytes 516104 | tf_op jit(solution)/shard_map/ppermute | solution.py:90
  32.4 5.9 %collective-permute-start.10 = (bf16[8,2688]{1,0:T(8,128)(2,1)S(1)}, bf16[8,2688]{1,0:T(8,128)(2,1)S(1)}, u32[]{:S(2)}, u32[]{:S(2)}) collective-permute-start(bf16[8,2688]{1,0:T(8,128)(2,1)S(1)} %get-tuple-element.28), channel_id=1, source_target_pairs={{0,2},{1,3},{2,4},{3,5},{4,6},{5,7},{6,0},{7,1},{8,10},{9,11},{10,... | collective-permute-start | bytes 129032 | tf_op jit(solution)/shard_map/ppermute | solution.py:95
  32.4 5.8 %collective-permute-start.11 = (bf16[8,2688]{1,0:T(8,128)(2,1)S(1)}, bf16[8,2688]{1,0:T(8,128)(2,1)S(1)}, u32[]{:S(2)}, u32[]{:S(2)}) collective-permute-start(bf16[8,2688]{1,0:T(8,128)(2,1)S(1)} %get-tuple-element.29), channel_id=1, source_target_pairs={{0,4},{1,5},{2,6},{3,7},{4,0},{5,1},{6,2},{7,3},{8,12},{9,13},{10,... | collective-permute-start | bytes 129032 | tf_op jit(solution)/shard_map/ppermute | solution.py:95
  33.9 4.9 %collective-permute-start.12 = (bf16[8,2688]{1,0:T(8,128)(2,1)S(1)}, bf16[8,2688]{1,0:T(8,128)(2,1)S(1)}, u32[]{:S(2)}, u32[]{:S(2)}) collective-permute-start(bf16[8,2688]{1,0:T(8,128)(2,1)S(1)} %get-tuple-element.30), channel_id=1, source_target_pairs={{0,6},{1,7},{2,0},{3,1},{4,2},{5,3},{6,4},{7,5},{8,14},{9,15},{10,... | collective-permute-start | bytes 129032 | tf_op jit(solution)/shard_map/ppermute | solution.py:95

commit v7 on v6

--- a/solution.py
+++ b/solution.py
@@ -92,7 +92,7 @@
 
 def slide(rows, distance):
     count = lax.axis_size("loc")
-    return lax.ppermute(rows, "loc", [(i, (i + distance) % count) for i in range(count)])
+    return lax.ppermute(rows, "loc", [(i, (i - distance) % count) for i in range(count)])
 
 
 def turn(rows, steps):
@@ -254,13 +254,17 @@
     out_ref[...] = packed[:, :body].astype(out_ref.dtype)
 
 
-def combine_kernel(*refs):
-    pieces, outs = refs[:EXP_GRP], refs[EXP_GRP:]
-    total = pieces[0][...].astype(jnp.float32)
+def combine_kernel(slices, *refs):
+    pieces, outs, total = refs[:EXP_GRP], refs[EXP_GRP:-1], refs[-1]
+    summed = pieces[0][...].astype(jnp.float32)
     for piece in pieces[1:]:
-        total = total + piece[...].astype(jnp.float32)
-    for i, out_ref in enumerate(outs):
-        out_ref[...] = total[i * SUBLANES : (i + 1) * SUBLANES].astype(out_ref.dtype)
+        summed = summed + piece[...].astype(jnp.float32)
+    total[...] = summed
+    member = lax.axis_index("loc") // slices
+    for k, out_ref in enumerate(outs):
+        slot = member ^ ((member + EXP_GRP - k) % EXP_GRP)
+        lowest = pl.multiple_of(slot * SUBLANES, SUBLANES)
+        out_ref[...] = total[pl.ds(lowest, SUBLANES), :].astype(out_ref.dtype)
 
 
 def finish_kernel(*refs):
@@ -303,7 +307,7 @@
         [HBM] * 3,
     )
     steps = range(1, EXP_GRP)
-    got = {k: slide(own, slices * k) for k in reversed(steps)}
+    got = {k: swap(own, "loc", slices * k) for k in reversed(steps)}
     pieces = [own] + [got[k] for k in steps]
     *blocks, pieces[0] = lax.optimization_barrier((*blocks, pieces[0]))
     size = sum(w.size for w in blocks)
@@ -341,11 +345,12 @@
     )
     packed = (SUBLANES, body)
     sums = call(
-        combine_kernel,
+        functools.partial(combine_kernel, slices),
         [jax.ShapeDtypeStruct(packed, f32)] + [jax.ShapeDtypeStruct(packed, bf16)] * len(steps),
         (run_expert(rows, f32), *returned),
-    )
-    homeward = [slide(sums[k], -slices * k) for k in reversed(steps)]
+        [scratch((EXP_GRP * SUBLANES, body), f32)],
+    )
+    homeward = [slide(sums[k], slices * k) for k in reversed(steps)]
     total = call(
         finish_kernel,
         jax.ShapeDtypeStruct((tok_count, feature), bf16),

time: 39.7 us -> 39.1 us (0.985)
  waiting for transfers between devices: 13.4 us -> 12.3 us
  starting transfers between devices: 17.9 us -> 18.5 us
    ppermute x3 -> x6, starting transfers between devices: 0.74 us -> 6.49 us  [swap(): return lax.ppermute(rows, axis, pairs(lax.axis_size(axis), distance))]
    ppermute x6 -> x3, starting transfers between devices: 10.2 us -> 5 us  [slide(): lax.ppermute(rows, 'loc', [(i, (i - distance) % count) for i in range(cou...]
    ppermute x6 -> x3, waiting for transfers between devices: 5.26 us -> 1.69 us  [slide(): lax.ppermute(rows, 'loc', [(i, (i - distance) % count) for i in range(cou...]
    ppermute x3 -> x6, waiting for transfers between devices: 0.88 us -> 3.28 us  [swap(): return lax.ppermute(rows, axis, pairs(lax.axis_size(axis), distance))]
  transfers between devices with their start and end apart: 13 -> 13, of which waited for: 7 -> 6; matrix products, arithmetic and copies ran while one was open for 0% -> 0% of each run, Pallas kernels for 16% -> 16%
where the time goes in v7:
time: 39.1 us; the launch traced here: 38.9 us
  starting transfers between devices  18.5 us (47%)
  waiting for transfers between devices  12.3 us (31%)
  Pallas kernels  8.08 us (21%)
    pallas_call x9, Pallas kernels, call(): pl.pallas_call(kernel, out_shape=outs, in_specs=specs or [VMEM] * len(arg...  8.08 us
    ppermute x4, waiting for transfers between devices, turn(): return lax.ppermute(rows, ('grp', 'loc'), moves)  7.3 us
    ppermute x4, starting transfers between devices, turn(): return lax.ppermute(rows, ('grp', 'loc'), moves)  6.96 us
    ppermute x6, starting transfers between devices, swap(): return lax.ppermute(rows, axis, pairs(lax.axis_size(axis), distance))  6.49 us
    ppermute x3, starting transfers between devices, slide(): lax.ppermute(rows, 'loc', [(i, (i - distance) % count) for i in range(cou...  5 us
    ppermute x6, waiting for transfers between devices, swap(): return lax.ppermute(rows, axis, pairs(lax.axis_size(axis), distance))  3.28 us
    ppermute x3, waiting for transfers between devices, slide(): lax.ppermute(rows, 'loc', [(i, (i - distance) % count) for i in range(cou...  1.69 us
  transfers between devices with their start and end apart: 13, of which 6 were waited for; matrix products, arithmetic and copies ran while one was open for 0% of the time, Pallas kernels for 16%

profile of v7, /device:TPU:0, one launch (start us, length us, event | category | flops | bytes accessed | tf_op | source)
XLA Modules:
  0.0 38.9 jit_solution(11332478675911852075)
XLA Ops:
  0.0 1.0 %shard_map.64.refs_0_ = bf16[8,2816]{1,0:T(8,128)(2,1)S(1)} custom-call(bf16[6,3584]{1,0:T(8,128)(2,1)} %bitcast.10, s32[6,1,8]{2,1,0:T(1,128)} %bitcast.11, bf16[6,8]{1,0:T(8,128)(2,1)} %bitcast.12), custom_call_target="tpu_custom_call" | custom-call | tf_op jit(solution)/shard_map/pallas_call | solution.py:152
  1.0 5.1 %collective-permute-start.2 = (bf16[8,2816]{1,0:T(8,128)(2,1)S(1)}, bf16[8,2816]{1,0:T(8,128)(2,1)S(1)}, u32[]{:S(2)}, u32[]{:S(2)}) collective-permute-start(bf16[8,2816]{1,0:T(8,128)(2,1)S(1)} %shard_map.64.refs_0_), channel_id=1, source_target_pairs={{0,6},{1,7},{2,4},{3,5},{4,2},{5,3},{6,0},{7,1},{8,14},{9,15},{10,... | collective-permute-start | bytes 135176 | tf_op jit(solution)/shard_map/ppermute | solution.py:90
  6.1 0.0 collective-permute-start.1
  6.1 0.6 %collective-permute-start = (bf16[8,2816]{1,0:T(8,128)(2,1)S(1)}, bf16[8,2816]{1,0:T(8,128)(2,1)S(1)}, u32[]{:S(2)}, u32[]{:S(2)}) collective-permute-start(bf16[8,2816]{1,0:T(8,128)(2,1)S(1)} %shard_map.64.refs_0_), channel_id=1, source_target_pairs={{0,2},{1,3},{2,0},{3,1},{4,6},{5,7},{6,4},{7,5},{8,10},{9,11},{10,... | collective-permute-start | bytes 135176 | tf_op jit(solution)/shard_map/ppermute | solution.py:90
  6.7 1.9 %shard_map.65.refs_0_ = bf16[10752,128]{1,0:T(8,128)(2,1)S(1)} custom-call(bf16[3584,128]{1,0:T(8,128)(2,1)} %bitcast.7, bf16[3584,128]{1,0:T(8,128)(2,1)} %bitcast.8, bf16[128,3584]{1,0:T(8,128)(2,1)} %bitcast.9), custom_call_target="tpu_custom_call" | custom-call | bytes 2752512 | tf_op jit(solution)/shard_map/pallas_call | solution.py:152
  8.6 0.0 collective-permute-done.2.refs_3_
  8.6 2.4 %collective-permute-done.1.refs_2_ = bf16[8,2816]{1,0:T(8,128)(2,1)S(1)} collective-permute-done((bf16[8,2816]{1,0:T(8,128)(2,1)S(1)}, bf16[8,2816]{1,0:T(8,128)(2,1)S(1)}, u32[]{:S(2)}, u32[]{:S(2)}) %collective-permute-start.1) | collective-permute-done | bytes 45088 | tf_op jit(solution)/shard_map/ppermute | solution.py:90
  11.0 0.0 collective-permute-done.refs_1_
  11.0 0.0 collective-permute-start.3
  11.0 1.6 %collective-permute-start.4 = (bf16[32,2816]{1,0:T(8,128)(2,1)S(1)}, bf16[32,2816]{1,0:T(8,128)(2,1)S(1)}, u32[]{:S(2)}, u32[]{:S(2)}) collective-permute-start(bf16[32,2816]{1,0:T(8,128)(2,1)S(1)} %shard_map.66.rows_ref), channel_id=1, source_target_pairs={{0,8},{1,17},{2,10},{3,19},{4,12},{5,21},{6,14},{7,23},{8,0},{9,25... | collective-permute-start | bytes 540680 | tf_op jit(solution)/shard_map/ppermute | solution.py:105
  12.6 1.5 %collective-permute-start.6 = (bf16[32,2816]{1,0:T(8,128)(2,1)S(1)}, bf16[32,2816]{1,0:T(8,128)(2,1)S(1)}, u32[]{:S(2)}, u32[]{:S(2)}) collective-permute-start(bf16[32,2816]{1,0:T(8,128)(2,1)S(1)} %shard_map.66.rows_ref), channel_id=1, source_target_pairs={{0,16},{1,9},{2,18},{3,11},{4,20},{5,13},{6,22},{7,15},{8,24},{9,1... | collective-permute-start | bytes 540680 | tf_op jit(solution)/shard_map/ppermute | solution.py:105
  14.1 0.5 %collective-permute-start.8 = (bf16[32,2816]{1,0:T(8,128)(2,1)S(1)}, bf16[32,2816]{1,0:T(8,128)(2,1)S(1)}, u32[]{:S(2)}, u32[]{:S(2)}) collective-permute-start(bf16[32,2816]{1,0:T(8,128)(2,1)S(1)} %shard_map.66.rows_ref), channel_id=1, source_target_pairs={{0,24},{8,16},{16,8},{24,0},{1,25},{9,17},{17,9},{25,1},{2,26},{10... | collective-permute-start | bytes 540680 | tf_op jit(solution)/shard_map/ppermute | solution.py:90
  14.6 3.2 %collective-permute-done.4.rows_ref = bf16[32,2816]{1,0:T(8,128)(2,1)S(1)} collective-permute-done((bf16[32,2816]{1,0:T(8,128)(2,1)S(1)}, bf16[32,2816]{1,0:T(8,128)(2,1)S(1)}, u32[]{:S(2)}, u32[]{:S(2)}) %collective-permute-start.4) | collective-permute-done | bytes 180256 | tf_op jit(solution)/shard_map/ppermute | solution.py:105
  17.8 0.0 collective-permute-done.3.refs_1_
  17.8 1.1 %shard_map.68 = bf16[32,2688]{1,0:T(8,128)(2,1)S(1)} custom-call(bf16[32,2816]{1,0:T(8,128)(2,1)S(1)} %collective-permute-done.4.rows_ref, bf16[10752,128]{1,0:T(8,128)(2,1)S(1)} %shard_map.65.refs_0_, bf16[10752,128]{1,0:T(8,128)(2,1)S(1)} %collective-permute-done.3.refs_1_), custom_call_target="tpu_custom_call" | custom-call | flops 132120576 | bytes 5505024 | tf_op jit(solution)/shard_map/pallas_call | solution.py:152
  18.9 1.6 %collective-permute-start.5 = (bf16[32,2688]{1,0:T(8,128)(2,1)S(1)}, bf16[32,2688]{1,0:T(8,128)(2,1)S(1)}, u32[]{:S(2)}, u32[]{:S(2)}) collective-permute-start(bf16[32,2688]{1,0:T(8,128)(2,1)S(1)} %shard_map.68), channel_id=1, source_target_pairs={{0,8},{1,17},{2,10},{3,19},{4,12},{5,21},{6,14},{7,23},{8,0},{9,25... | collective-permute-start | bytes 516104 | tf_op jit(solution)/shard_map/ppermute | solution.py:105
  20.5 0.0 collective-permute-done.6.rows_ref
  20.5 1.1 %shard_map.69 = bf16[32,2688]{1,0:T(8,128)(2,1)S(1)} custom-call(bf16[32,2816]{1,0:T(8,128)(2,1)S(1)} %collective-permute-done.6.rows_ref, bf16[10752,128]{1,0:T(8,128)(2,1)S(1)} %shard_map.65.refs_0_, bf16[10752,128]{1,0:T(8,128)(2,1)S(1)} %collective-permute-done.3.refs_1_), custom_call_target="tpu_custom_call" | custom-call | flops 132120576 | bytes 5505024 | tf_op jit(solution)/shard_map/pallas_call | solution.py:152
  21.6 2.3 %collective-permute-start.7 = (bf16[32,2688]{1,0:T(8,128)(2,1)S(1)}, bf16[32,2688]{1,0:T(8,128)(2,1)S(1)}, u32[]{:S(2)}, u32[]{:S(2)}) collective-permute-start(bf16[32,2688]{1,0:T(8,128)(2,1)S(1)} %shard_map.69), channel_id=1, source_target_pairs={{0,16},{1,9},{2,18},{3,11},{4,20},{5,13},{6,22},{7,15},{8,24},{9,1... | collective-permute-start | bytes 516104 | tf_op jit(solution)/shard_map/ppermute | solution.py:105
  23.9 0.0 collective-permute-done.8.rows_ref
  23.9 1.1 %shard_map.70 = bf16[32,2688]{1,0:T(8,128)(2,1)S(1)} custom-call(bf16[32,2816]{1,0:T(8,128)(2,1)S(1)} %collective-permute-done.8.rows_ref, bf16[10752,128]{1,0:T(8,128)(2,1)S(1)} %shard_map.65.refs_0_, bf16[10752,128]{1,0:T(8,128)(2,1)S(1)} %collective-permute-done.3.refs_1_), custom_call_target="tpu_custom_call" | custom-call | flops 132120576 | bytes 5505024 | tf_op jit(solution)/shard_map/pallas_call | solution.py:152
  25.0 0.3 collective-permute-start.9
  25.3 1.1 %shard_map.67.refs_0_ = f32[32,2688]{1,0:T(8,128)S(1)} custom-call(bf16[32,2816]{1,0:T(8,128)(2,1)S(1)} %shard_map.66.rows_ref, bf16[10752,128]{1,0:T(8,128)(2,1)S(1)} %shard_map.65.refs_0_, bf16[10752,128]{1,0:T(8,128)(2,1)S(1)} %collective-permute-done.3.refs_1_), custom_call_target="tpu_custom_call" | custom-call | flops 132120576 | bytes 5505024 | tf_op jit(solution)/shard_map/pallas_call | solution.py:152
  26.4 0.0 collective-permute-done.5.refs_1_
  26.4 4.1 %collective-permute-done.7.refs_2_ = bf16[32,2688]{1,0:T(8,128)(2,1)S(1)} collective-permute-done((bf16[32,2688]{1,0:T(8,128)(2,1)S(1)}, bf16[32,2688]{1,0:T(8,128)(2,1)S(1)}, u32[]{:S(2)}, u32[]{:S(2)}) %collective-permute-start.7) | collective-permute-done | bytes 172064 | tf_op jit(solution)/shard_map/ppermute | solution.py:105
  30.5 0.9 %collective-permute-done.9.refs_3_ = bf16[32,2688]{1,0:T(8,128)(2,1)S(1)} collective-permute-done((bf16[32,2688]{1,0:T(8,128)(2,1)S(1)}, bf16[32,2688]{1,0:T(8,128)(2,1)S(1)}, u32[]{:S(2)}, u32[]{:S(2)}) %collective-permute-start.9) | collective-permute-done | bytes 172064 | tf_op jit(solution)/shard_map/ppermute | solution.py:90
  31.4 0.1 shard_map.71
  31.5 0.4 %collective-permute-start.10 = (bf16[8,2688]{1,0:T(8,128)(2,1)S(1)}, bf16[8,2688]{1,0:T(8,128)(2,1)S(1)}, u32[]{:S(2)}, u32[]{:S(2)}) collective-permute-start(bf16[8,2688]{1,0:T(8,128)(2,1)S(1)} %get-tuple-element.28), channel_id=1, source_target_pairs={{0,2},{1,3},{2,4},{3,5},{4,6},{5,7},{6,0},{7,1},{8,10},{9,11},{10,... | collective-permute-start | bytes 129032 | tf_op jit(solution)/shard_map/ppermute | solution.py:95
  32.0 2.0 %collective-permute-start.11 = (bf16[8,2688]{1,0:T(8,128)(2,1)S(1)}, bf16[8,2688]{1,0:T(8,128)(2,1)S(1)}, u32[]{:S(2)}, u32[]{:S(2)}) collective-permute-start(bf16[8,2688]{1,0:T(8,128)(2,1)S(1)} %get-tuple-element.29), channel_id=1, source_target_pairs={{0,4},{1,5},{2,6},{3,7},{4,0},{5,1},{6,2},{7,3},{8,12},{9,13},{10,... | collective-permute-start | bytes 129032 | tf_op jit(solution)/shard_map/ppermute | solution.py:95
  34.0 2.5 %collective-permute-start.12 = (bf16[8,2688]{1,0:T(8,128)(2,1)S(1)}, bf16[8,2688]{1,0:T(8,128)(2,1)S(1)}, u32[]{:S(2)}, u32[]{:S(2)}) collective-permute-start(bf16[8,2688]{1,0:T(8,128)(2,1)S(1)} %get-tuple-element.30), channel_id=1, source_target_pairs={{0,6},{1,7},{2,0},{3,1},{4,2},{5,3},{6,4},{7,5},{8,14},{9,15},{10,... | collective-permute-start | bytes 129032 | tf_op jit(solution)/shard_map/ppermute | solution.py:95
  36.5 0.9 %collective-permute-done.10.refs_1_ = bf16[8,2688]{1,0:T(8,128)(2,1)S(1)} collective-permute-done((bf16[8,2688]{1,0:T(8,128)(2,1)S(1)}, bf16[8,2688]{1,0:T(8,128)(2,1)S(1)}, u32[]{:S(2)}, u32[]{:S(2)}) %collective-permute-start.10) | collective-permute-done | bytes 43040 | tf_op jit(solution)/shard_map/ppermute | solution.py:95
  37.4 0.0 collective-permute-done.11.refs_2_
  37.4 0.8 %collective-permute-done.12.refs_3_ = bf16[8,2688]{1,0:T(8,128)(2,1)S(1)} collective-permute-done((bf16[8,2688]{1,0:T(8,128)(2,1)S(1)}, bf16[8,2688]{1,0:T(8,128)(2,1)S(1)}, u32[]{:S(2)}, u32[]{:S(2)}) %collective-permute-start.12) | collective-permute-done | bytes 43040 | tf_op jit(solution)/shard_map/ppermute | solution.py:95
  38.2 0.7 %shard_map.72 = bf16[6,3584]{1,0:T(8,128)(2,1)} custom-call(f32[8,2688]{1,0:T(8,128)S(1)} %get-tuple-element.27.refs_0_, bf16[8,2688]{1,0:T(8,128)(2,1)S(1)} %collective-permute-done.10.refs_1_, bf16[8,2688]{1,0:T(8,128)(2,1)S(1)} %collective-permute-done.11.refs_2_, bf16[8,2688]{1,0:T(8,128)(2,1)S(1)} %collective-permute-done.12.refs_3_), custom_call_target="tpu_custom_call" | custom-call | tf_op jit(solution)/shard_map/pallas_call | solution.py:152
  (1 shorter events, 0.0 us)
Async XLA Ops:
  1.0 7.7 %collective-permute-start.2 = (bf16[8,2816]{1,0:T(8,128)(2,1)S(1)}, bf16[8,2816]{1,0:T(8,128)(2,1)S(1)}, u32[]{:S(2)}, u32[]{:S(2)}) collective-permute-start(bf16[8,2816]{1,0:T(8,128)(2,1)S(1)} %shard_map.64.refs_0_), channel_id=1, source_target_pairs={{0,6},{1,7},{2,4},{3,5},{4,2},{5,3},{6,0},{7,1},{8,14},{9,15},{10,... | collective-permute-start | bytes 135176 | tf_op jit(solution)/shard_map/ppermute | solution.py:90
  6.1 4.9 %collective-permute-start.1 = (bf16[8,2816]{1,0:T(8,128)(2,1)S(1)}, bf16[8,2816]{1,0:T(8,128)(2,1)S(1)}, u32[]{:S(2)}, u32[]{:S(2)}) collective-permute-start(bf16[8,2816]{1,0:T(8,128)(2,1)S(1)} %shard_map.64.refs_0_), channel_id=1, source_target_pairs={{0,4},{1,5},{2,6},{3,7},{4,0},{5,1},{6,2},{7,3},{8,12},{9,13},{10,... | collective-permute-start | bytes 135176 | tf_op jit(solution)/shard_map/ppermute | solution.py:90
  6.1 4.9 %collective-permute-start = (bf16[8,2816]{1,0:T(8,128)(2,1)S(1)}, bf16[8,2816]{1,0:T(8,128)(2,1)S(1)}, u32[]{:S(2)}, u32[]{:S(2)}) collective-permute-start(bf16[8,2816]{1,0:T(8,128)(2,1)S(1)} %shard_map.64.refs_0_), channel_id=1, source_target_pairs={{0,2},{1,3},{2,0},{3,1},{4,6},{5,7},{6,4},{7,5},{8,10},{9,11},{10,... | collective-permute-start | bytes 135176 | tf_op jit(solution)/shard_map/ppermute | solution.py:90
  11.0 6.8 %collective-permute-start.3 = (bf16[10752,128]{1,0:T(8,128)(2,1)S(1)}, bf16[10752,128]{1,0:T(8,128)(2,1)S(1)}, u32[]{:S(2)}, u32[]{:S(2)}) collective-permute-start(bf16[10752,128]{1,0:T(8,128)(2,1)S(1)} %shard_map.65.refs_0_), channel_id=1, source_target_pairs={{0,1},{1,0},{2,3},{3,2},{4,5},{5,4},{6,7},{7,6},{8,9},{9,8},{10,11... | collective-permute-start | bytes 8257544 | tf_op jit(solution)/shard_map/ppermute | solution.py:90
  11.0 6.7 %collective-permute-start.4 = (bf16[32,2816]{1,0:T(8,128)(2,1)S(1)}, bf16[32,2816]{1,0:T(8,128)(2,1)S(1)}, u32[]{:S(2)}, u32[]{:S(2)}) collective-permute-start(bf16[32,2816]{1,0:T(8,128)(2,1)S(1)} %shard_map.66.rows_ref), channel_id=1, source_target_pairs={{0,8},{1,17},{2,10},{3,19},{4,12},{5,21},{6,14},{7,23},{8,0},{9,25... | collective-permute-start | bytes 540680 | tf_op jit(solution)/shard_map/ppermute | solution.py:105
  12.6 7.9 %collective-permute-start.6 = (bf16[32,2816]{1,0:T(8,128)(2,1)S(1)}, bf16[32,2816]{1,0:T(8,128)(2,1)S(1)}, u32[]{:S(2)}, u32[]{:S(2)}) collective-permute-start(bf16[32,2816]{1,0:T(8,128)(2,1)S(1)} %shard_map.66.rows_ref), channel_id=1, source_target_pairs={{0,16},{1,9},{2,18},{3,11},{4,20},{5,13},{6,22},{7,15},{8,24},{9,1... | collective-permute-start | bytes 540680 | tf_op jit(solution)/shard_map/ppermute | solution.py:105
  14.1 9.8 %collective-permute-start.8 = (bf16[32,2816]{1,0:T(8,128)(2,1)S(1)}, bf16[32,2816]{1,0:T(8,128)(2,1)S(1)}, u32[]{:S(2)}, u32[]{:S(2)}) collective-permute-start(bf16[32,2816]{1,0:T(8,128)(2,1)S(1)} %shard_map.66.rows_ref), channel_id=1, source_target_pairs={{0,24},{8,16},{16,8},{24,0},{1,25},{9,17},{17,9},{25,1},{2,26},{10... | collective-permute-start | bytes 540680 | tf_op jit(solution)/shard_map/ppermute | solution.py:90
  18.9 7.5 %collective-permute-start.5 = (bf16[32,2688]{1,0:T(8,128)(2,1)S(1)}, bf16[32,2688]{1,0:T(8,128)(2,1)S(1)}, u32[]{:S(2)}, u32[]{:S(2)}) collective-permute-start(bf16[32,2688]{1,0:T(8,128)(2,1)S(1)} %shard_map.68), channel_id=1, source_target_pairs={{0,8},{1,17},{2,10},{3,19},{4,12},{5,21},{6,14},{7,23},{8,0},{9,25... | collective-permute-start | bytes 516104 | tf_op jit(solution)/shard_map/ppermute | solution.py:105
  21.6 8.9 %collective-permute-start.7 = (bf16[32,2688]{1,0:T(8,128)(2,1)S(1)}, bf16[32,2688]{1,0:T(8,128)(2,1)S(1)}, u32[]{:S(2)}, u32[]{:S(2)}) collective-permute-start(bf16[32,2688]{1,0:T(8,128)(2,1)S(1)} %shard_map.69), channel_id=1, source_target_pairs={{0,16},{1,9},{2,18},{3,11},{4,20},{5,13},{6,22},{7,15},{8,24},{9,1... | collective-permute-start | bytes 516104 | tf_op jit(solution)/shard_map/ppermute | solution.py:105
  25.0 6.4 %collective-permute-start.9 = (bf16[32,2688]{1,0:T(8,128)(2,1)S(1)}, bf16[32,2688]{1,0:T(8,128)(2,1)S(1)}, u32[]{:S(2)}, u32[]{:S(2)}) collective-permute-start(bf16[32,2688]{1,0:T(8,128)(2,1)S(1)} %shard_map.70), channel_id=1, source_target_pairs={{0,24},{8,16},{16,8},{24,0},{1,25},{9,17},{17,9},{25,1},{2,26},{10... | collective-permute-start | bytes 516104 | tf_op jit(solution)/shard_map/ppermute | solution.py:90
  31.5 5.9 %collective-permute-start.10 = (bf16[8,2688]{1,0:T(8,128)(2,1)S(1)}, bf16[8,2688]{1,0:T(8,128)(2,1)S(1)}, u32[]{:S(2)}, u32[]{:S(2)}) collective-permute-start(bf16[8,2688]{1,0:T(8,128)(2,1)S(1)} %get-tuple-element.28), channel_id=1, source_target_pairs={{0,2},{1,3},{2,4},{3,5},{4,6},{5,7},{6,0},{7,1},{8,10},{9,11},{10,... | collective-permute-start | bytes 129032 | tf_op jit(solution)/shard_map/ppermute | solution.py:95
  32.0 5.5 %collective-permute-start.11 = (bf16[8,2688]{1,0:T(8,128)(2,1)S(1)}, bf16[8,2688]{1,0:T(8,128)(2,1)S(1)}, u32[]{:S(2)}, u32[]{:S(2)}) collective-permute-start(bf16[8,2688]{1,0:T(8,128)(2,1)S(1)} %get-tuple-element.29), channel_id=1, source_target_pairs={{0,4},{1,5},{2,6},{3,7},{4,0},{5,1},{6,2},{7,3},{8,12},{9,13},{10,... | collective-permute-start | bytes 129032 | tf_op jit(solution)/shard_map/ppermute | solution.py:95
  34.0 4.2 %collective-permute-start.12 = (bf16[8,2688]{1,0:T(8,128)(2,1)S(1)}, bf16[8,2688]{1,0:T(8,128)(2,1)S(1)}, u32[]{:S(2)}, u32[]{:S(2)}) collective-permute-start(bf16[8,2688]{1,0:T(8,128)(2,1)S(1)} %get-tuple-element.30), channel_id=1, source_target_pairs={{0,6},{1,7},{2,0},{3,1},{4,2},{5,3},{6,4},{7,5},{8,14},{9,15},{10,... | collective-permute-start | bytes 129032 | tf_op jit(solution)/shard_map/ppermute | solution.py:95
